TPU v7x, 32 devices: a whole 2x2x4 slice. The times are simulated.
32 devices in a mesh: seq: 8 (over y, x, core), sub: 4 (over z).
Axes of the slice: x: 2, y: 2, z: 4, core: 2. Of those that a mesh axis runs over, the one named last changes fastest.
Arguments:
- video: bfloat16 [4096, 1536], P(('seq', 'sub')), may hold values from -6 to 6
- conditioning: bfloat16 [5, 1024], replicated, may hold values from -6 to 6
- captions: bfloat16 [1280, 4096], P('sub'), may hold values from -6 to 6
- clip_lengths: int32 [5], replicated, may hold values from 1 to 2048, 4096 in all
- cap_lengths: int32 [5], replicated, may hold values from 64 to 256, as said below
- positions: int32 [4096, 3], P(('seq', 'sub')), may hold values from 0 to 63
- ada_weight: bfloat16 [1024, 6144], P(('seq', 'sub')), may hold values from -0.1875 to 0.1875
- ada_bias: bfloat16 [6144], P(('seq', 'sub')), may hold values from -3 to 3
- query_weight: bfloat16 [1536, 1536], P(('seq', 'sub')), may hold values from -0.15625 to 0.15625
- key_weight: bfloat16 [1536, 1536], P(('seq', 'sub')), may hold values from -0.15625 to 0.15625
- value_weight: bfloat16 [1536, 1536], P(('seq', 'sub')), may hold values from -0.15625 to 0.15625
- out_weight: bfloat16 [1536, 1536], P(('seq', 'sub')), may hold values from -0.15625 to 0.15625
- text_key_weight: bfloat16 [4096, 1536], P(('seq', 'sub')), may hold values from -0.09375 to 0.09375
- text_value_weight: bfloat16 [4096, 1536], P(('seq', 'sub')), may hold values from -0.09375 to 0.09375
- gate_weight: bfloat16 [1536, 4096], P(('seq', 'sub')), may hold values from -0.15625 to 0.15625
- up_weight: bfloat16 [1536, 4096], P(('seq', 'sub')), may hold values from -0.15625 to 0.15625
- down_weight: bfloat16 [4096, 1536], P(('seq', 'sub')), may hold values from -0.09375 to 0.09375
- attn_gain: bfloat16 [1536], P(('seq', 'sub')), may hold values from 0.5 to 1.5
- query_gain: bfloat16 [1536], P(('seq', 'sub')), may hold values from 0.5 to 1.5
- key_gain: bfloat16 [1536], P(('seq', 'sub')), may hold values from 0.5 to 1.5
- text_key_gain: bfloat16 [1536], P(('seq', 'sub')), may hold values from 0.5 to 1.5
- attn_out_gain: bfloat16 [1536], P(('seq', 'sub')), may hold values from 0.5 to 1.5
- ffn_gain: bfloat16 [1536], P(('seq', 'sub')), may hold values from 0.5 to 1.5
- ffn_out_gain: bfloat16 [1536], P(('seq', 'sub')), may hold values from 0.5 to 1.5
- cross_gate: bfloat16 [24], replicated, may hold values from -1.5 to 1.5
- cotangent: bfloat16 [4096, 1536], P(('seq', 'sub')), may hold values from -6 to 6
Outputs:
- block_out: bfloat16 [4096, 1536], P(('seq', 'sub'))
- video_grad: float32 [4096, 1536], P(('seq', 'sub'))
- caption_grad: float32 [1280, 4096], P('sub')
- cond_grad: float32 [5, 1024], replicated
- ada_weight_grad: float32 [1024, 6144], P(('seq', 'sub'))
- ada_bias_grad: float32 [6144], P(('seq', 'sub'))
- query_weight_grad: float32 [1536, 1536], P(('seq', 'sub'))
- key_weight_grad: float32 [1536, 1536], P(('seq', 'sub'))
- value_weight_grad: float32 [1536, 1536], P(('seq', 'sub'))
- out_weight_grad: float32 [1536, 1536], P(('seq', 'sub'))
- text_key_weight_grad: float32 [4096, 1536], P(('seq', 'sub'))
- text_value_weight_grad: float32 [4096, 1536], P(('seq', 'sub'))
- gate_weight_grad: float32 [1536, 4096], P(('seq', 'sub'))
- up_weight_grad: float32 [1536, 4096], P(('seq', 'sub'))
- down_weight_grad: float32 [4096, 1536], P(('seq', 'sub'))
- attn_gain_grad: float32 [1536], P(('seq', 'sub'))
- query_gain_grad: float32 [1536], P(('seq', 'sub'))
- key_gain_grad: float32 [1536], P(('seq', 'sub'))
- text_key_gain_grad: float32 [1536], P(('seq', 'sub'))
- attn_out_gain_grad: float32 [1536], P(('seq', 'sub'))
- ffn_gain_grad: float32 [1536], P(('seq', 'sub'))
- ffn_out_gain_grad: float32 [1536], P(('seq', 'sub'))
- cross_gate_grad: float32 [24], replicated
Inputs may be any that keep to these rules, and one draw needn't show every extreme that they name: `clip_lengths`: clip lengths sum to 4096; the longest clip has exactly 2048 tokens. `cap_lengths`: one clip's caption fills all 256 slots.
All inputs are finite; a program needn't handle non-finite values.
Results may differ from a plain program's by a relative error of at most 0.04.
Values may be sent and summed in bfloat16 or wider, within the bound.
No kernel may reach another device: no remote copies, remote signals or barrier semaphores. Data moves between devices by JAX's collectives and lax.ppermute only.
A program may use at most 384 MiB of HBM per device.

v0:
```python
import math

import jax
import jax.numpy as jnp
from jax import lax
from jax.sharding import PartitionSpec as P

CAP = 256


epsilon = 1e-06
rope_base = 10000.0
masked_score = -1e30
highest = lax.Precision.HIGHEST


def inv_rms(values):
    return lax.rsqrt(jnp.mean(values * values, -1, keepdims=True) + epsilon)


def norm_back(normed_hat, inverse, grad_hat):
    return inverse * (grad_hat - normed_hat * jnp.mean(normed_hat * grad_hat, -1, keepdims=True))


def round_keep(values):
    return lax.optimization_barrier(values.astype(jnp.bfloat16)).astype(jnp.float32)


def rope_tables(positions, head_dim):
    pair_total = head_dim // 2
    frame_pairs = pair_total // 4
    height_pairs = (pair_total - frame_pairs) // 2
    width_pairs = pair_total - frame_pairs - height_pairs
    pieces = []
    for axis_id, pair_count in enumerate((frame_pairs, height_pairs, width_pairs)):
        frequency = rope_base ** (-jnp.arange(pair_count, dtype=jnp.float32) / pair_count)
        pieces.append(positions[:, axis_id].astype(jnp.float32)[:, None] * frequency[None, :])
    angles = jnp.concatenate(pieces, 1)
    return (jnp.cos(angles), jnp.sin(angles))


def rotate(values, cosine, sine):
    shaped = values.reshape(values.shape[0], values.shape[1], -1, 2)
    even_part = shaped[..., 0]
    odd_part = shaped[..., 1]
    cos_part = cosine[:, None, :]
    sin_part = sine[:, None, :]
    turned = jnp.stack(
        [even_part * cos_part - odd_part * sin_part, even_part * sin_part + odd_part * cos_part], -1
    )
    return turned.reshape(values.shape)


def clip_index(token_index, clip_lengths):
    bounds = jnp.cumsum(clip_lengths)
    return jnp.sum((token_index[:, None] >= bounds[None, :]).astype(jnp.int32), 1)


def body(
    video,
    conditioning,
    captions,
    clip_lengths,
    cap_lengths,
    positions,
    ada_weight,
    ada_bias,
    query_weight,
    key_weight,
    value_weight,
    out_weight,
    text_key_weight,
    text_value_weight,
    gate_weight,
    up_weight,
    down_weight,
    attn_gain,
    query_gain,
    key_gain,
    text_key_gain,
    attn_out_gain,
    ffn_gain,
    ffn_out_gain,
    cross_gate,
    cotangent,
):
    num_sub = lax.axis_size("sub")
    num_seq = lax.axis_size("seq")
    tok_rows = video.shape[0]
    model_width = video.shape[1]
    heads_total = cross_gate.shape[0]
    head_dim = model_width // heads_total
    heads_local = heads_total // num_sub
    score_scale = 1.0 / math.sqrt(head_dim)
    device_index = lax.axis_index(("seq", "sub"))
    seq_index = lax.axis_index("seq")
    group_rows = tok_rows * num_sub
    total_tokens = group_rows * num_seq
    clip_count = clip_lengths.shape[0]
    clip_range = jnp.arange(clip_count, dtype=jnp.int32)
    barrier_set = lax.optimization_barrier(
        (
            ada_weight,
            ada_bias,
            query_weight,
            key_weight,
            value_weight,
            out_weight,
            text_key_weight,
            text_value_weight,
            attn_gain,
            query_gain,
            key_gain,
            text_key_gain,
            attn_out_gain,
            video,
        )
    )
    ada_full = lax.all_gather(barrier_set[0], ("seq", "sub"), axis=0, tiled=True)
    ada_bias_full = lax.all_gather(barrier_set[1], ("seq", "sub"), axis=0, tiled=True)
    query_full = lax.all_gather(barrier_set[2], ("seq", "sub"), axis=0, tiled=True)
    key_full = lax.all_gather(barrier_set[3], ("seq", "sub"), axis=0, tiled=True)
    value_full = lax.all_gather(barrier_set[4], ("seq", "sub"), axis=0, tiled=True)
    out_full = lax.all_gather(barrier_set[5], ("seq", "sub"), axis=0, tiled=True)
    text_key_full = lax.all_gather(barrier_set[6], ("seq", "sub"), axis=0, tiled=True)
    text_value_full = lax.all_gather(barrier_set[7], ("seq", "sub"), axis=0, tiled=True)
    attn_gain_full = lax.all_gather(barrier_set[8], ("seq", "sub"), axis=0, tiled=True)
    query_gain_full = lax.all_gather(barrier_set[9], ("seq", "sub"), axis=0, tiled=True)
    key_gain_full = lax.all_gather(barrier_set[10], ("seq", "sub"), axis=0, tiled=True)
    text_key_gain_full = lax.all_gather(barrier_set[11], ("seq", "sub"), axis=0, tiled=True)
    attn_out_gain_full = lax.all_gather(barrier_set[12], ("seq", "sub"), axis=0, tiled=True)
    barrier_set = lax.optimization_barrier(
        (gate_weight, up_weight, down_weight, ffn_gain, ffn_out_gain, video)
    )
    gate_full = lax.all_gather(barrier_set[0], ("seq", "sub"), axis=0, tiled=True)
    up_full = lax.all_gather(barrier_set[1], ("seq", "sub"), axis=0, tiled=True)
    down_full = lax.all_gather(barrier_set[2], ("seq", "sub"), axis=0, tiled=True)
    ffn_gain_full = lax.all_gather(barrier_set[3], ("seq", "sub"), axis=0, tiled=True)
    ffn_out_gain_full = lax.all_gather(barrier_set[4], ("seq", "sub"), axis=0, tiled=True)
    cond_float = conditioning.astype(jnp.float32)
    cond_act = jax.nn.silu(cond_float).astype(jnp.bfloat16)
    modulation = jnp.dot(
        cond_act, ada_full, preferred_element_type=jnp.float32
    ) + ada_bias_full.astype(jnp.float32)
    token_index = device_index * tok_rows + jnp.arange(tok_rows, dtype=jnp.int32)
    token_clip = clip_index(token_index, clip_lengths)
    clip_onehot = (token_clip[:, None] == clip_range[None, :]).astype(jnp.float32)
    per_token = jnp.dot(clip_onehot, modulation, precision=highest)
    attn_scale = per_token[:, :model_width]
    attn_gate = per_token[:, model_width : 2 * model_width]
    ffn_scale = per_token[:, 2 * model_width : 3 * model_width]
    ffn_gate = per_token[:, 3 * model_width :]
    video_float = video.astype(jnp.float32)
    video_inv = inv_rms(video_float)
    video_hat = video_float * video_inv
    attn_gain_f = attn_gain_full.astype(jnp.float32)
    attn_mult = attn_gain_f * (1.0 + attn_scale)
    normed = (video_hat * attn_mult).astype(jnp.bfloat16)
    query_pre = jnp.dot(normed, query_full, preferred_element_type=jnp.float32)
    key_pre = jnp.dot(normed, key_full, preferred_element_type=jnp.float32)
    values_tok = jnp.dot(normed, value_full, preferred_element_type=jnp.float32).astype(
        jnp.bfloat16
    )
    query_inv = inv_rms(query_pre)
    query_hat = query_pre * query_inv
    key_inv = inv_rms(key_pre)
    key_hat = key_pre * key_inv
    query_gain_f = query_gain_full.astype(jnp.float32)
    key_gain_f = key_gain_full.astype(jnp.float32)
    cosine, sine = rope_tables(positions, head_dim)
    query_tok = rotate(
        (query_hat * query_gain_f).reshape(tok_rows, heads_total, head_dim), cosine, sine
    ).astype(jnp.bfloat16)
    key_tok = rotate(
        (key_hat * key_gain_f).reshape(tok_rows, heads_total, head_dim), cosine, sine
    ).astype(jnp.bfloat16)
    query_heads, key_heads, value_heads = (
        lax.all_to_all(
            query_tok.reshape(tok_rows, model_width), "sub", split_axis=1, concat_axis=0, tiled=True
        ),
        lax.all_to_all(
            key_tok.reshape(tok_rows, model_width), "sub", split_axis=1, concat_axis=0, tiled=True
        ),
        lax.all_to_all(values_tok, "sub", split_axis=1, concat_axis=0, tiled=True),
    )
    key_all, value_all = (
        lax.all_gather(key_heads, "seq", axis=0, tiled=True),
        lax.all_gather(value_heads, "seq", axis=0, tiled=True),
    )
    group_clip = clip_index(
        seq_index * group_rows + jnp.arange(group_rows, dtype=jnp.int32), clip_lengths
    )
    query_blocks = query_heads.reshape(group_rows, heads_local, head_dim)
    key_block = min(1024, total_tokens)
    block_count = total_tokens // key_block
    key_stack = key_all.reshape(block_count, key_block, heads_local, head_dim)
    value_stack = value_all.reshape(block_count, key_block, heads_local, head_dim)
    block_starts = jnp.arange(block_count, dtype=jnp.int32) * key_block

    def block_scores(key_blk, block_start):
        key_clip = clip_index(block_start + jnp.arange(key_block, dtype=jnp.int32), clip_lengths)
        allowed = (group_clip[:, None] == key_clip[None, :])[:, None, :]
        scores = (
            jnp.einsum("qhd,khd->qhk", query_blocks, key_blk, preferred_element_type=jnp.float32)
            * score_scale
        )
        return (jnp.where(allowed, scores, masked_score), allowed)

    def forward_step(running, block_in):
        run_max, run_sum, run_acc = running
        key_blk, value_blk, block_start = block_in
        scores, allowed = block_scores(key_blk, block_start)
        new_max = jnp.maximum(run_max, jnp.max(scores, -1))
        prob_values = jnp.where(allowed, jnp.exp(scores - new_max[..., None]), 0.0)
        factor = jnp.exp(run_max - new_max)
        new_sum = run_sum * factor + jnp.sum(prob_values, -1)
        new_acc = run_acc * factor[..., None] + jnp.einsum(
            "qhk,khd->qhd",
            prob_values.astype(jnp.bfloat16),
            value_blk,
            preferred_element_type=jnp.float32,
        )
        return ((new_max, new_sum, new_acc), None)

    start_state = (
        jnp.full((group_rows, heads_local), masked_score, jnp.float32),
        jnp.zeros((group_rows, heads_local), jnp.float32),
        jnp.zeros((group_rows, heads_local, head_dim), jnp.float32),
    )
    (run_max, run_sum, run_acc), unused_out = lax.scan(
        forward_step, start_state, (key_stack, value_stack, block_starts)
    )
    self_out = run_acc / run_sum[..., None]
    log_sum = run_max + jnp.log(run_sum)
    self_tok = lax.all_to_all(
        self_out.astype(jnp.bfloat16).reshape(group_rows, heads_local * head_dim),
        "sub",
        split_axis=0,
        concat_axis=1,
        tiled=True,
    )
    cap_shard = captions.shape[0]
    cap_rows = cap_shard // num_seq
    cap_local = lax.dynamic_slice_in_dim(captions, seq_index * cap_rows, cap_rows, 0)
    text_key_pre = jnp.dot(cap_local, text_key_full, preferred_element_type=jnp.float32)
    text_inv = inv_rms(text_key_pre)
    text_hat = text_key_pre * text_inv
    text_key_gain_f = text_key_gain_full.astype(jnp.float32)
    text_keys = (text_hat * text_key_gain_f).astype(jnp.bfloat16)
    text_values = jnp.dot(cap_local, text_value_full, preferred_element_type=jnp.float32).astype(
        jnp.bfloat16
    )
    text_keys_all, text_values_all = (
        lax.all_gather(text_keys, ("seq", "sub"), axis=0, tiled=True),
        lax.all_gather(text_values, ("seq", "sub"), axis=0, tiled=True),
    )
    cap_total = text_keys_all.shape[0]
    slot_index = jnp.arange(cap_total, dtype=jnp.int32)
    owner_block = slot_index // cap_rows
    caption_row = (
        owner_block % num_sub * cap_shard
        + owner_block // num_sub * cap_rows
        + slot_index % cap_rows
    )
    caption_clip = caption_row // CAP
    clip_cap = jnp.sum(
        jnp.where(caption_clip[:, None] == clip_range[None, :], cap_lengths[None, :], 0), 1
    )
    caption_valid = caption_row % CAP < clip_cap
    text_key_heads = text_keys_all.reshape(cap_total, heads_total, head_dim)
    text_value_heads = text_values_all.reshape(cap_total, heads_total, head_dim)
    cross_allowed = ((token_clip[:, None] == caption_clip[None, :]) & caption_valid[None, :])[
        :, None, :
    ]
    cross_scores = (
        jnp.einsum("qhd,khd->qhk", query_tok, text_key_heads, preferred_element_type=jnp.float32)
        * score_scale
    )
    cross_probs = jax.nn.softmax(jnp.where(cross_allowed, cross_scores, masked_score), -1)
    cross_probs_low = cross_probs.astype(jnp.bfloat16)
    cross_out = jnp.einsum(
        "qhk,khd->qhd", cross_probs_low, text_value_heads, preferred_element_type=jnp.float32
    )
    gate_tanh = jnp.tanh(cross_gate.astype(jnp.float32))
    mixed = (
        (
            self_tok.astype(jnp.float32).reshape(tok_rows, heads_total, head_dim)
            + gate_tanh[None, :, None] * cross_out
        )
        .reshape(tok_rows, model_width)
        .astype(jnp.bfloat16)
    )
    projected = jnp.dot(mixed, out_full, preferred_element_type=jnp.float32)
    proj_inv = inv_rms(projected)
    proj_hat = projected * proj_inv
    attn_tanh = jnp.tanh(attn_gate)
    attn_out_f = attn_out_gain_full.astype(jnp.float32)
    hidden_state = video_float + attn_tanh * proj_hat * attn_out_f
    hidden_inv = inv_rms(hidden_state)
    hidden_hat = hidden_state * hidden_inv
    ffn_gain_f = ffn_gain_full.astype(jnp.float32)
    ffn_mult = ffn_gain_f * (1.0 + ffn_scale)
    ffn_in = (hidden_hat * ffn_mult).astype(jnp.bfloat16)
    gate_pre = jnp.dot(ffn_in, gate_full, preferred_element_type=jnp.float32)
    up_pre = jnp.dot(ffn_in, up_full, preferred_element_type=jnp.float32)
    activated = (jax.nn.silu(gate_pre) * up_pre).astype(jnp.bfloat16)
    down_out = jnp.dot(activated, down_full, preferred_element_type=jnp.float32)
    down_inv = inv_rms(down_out)
    down_hat = down_out * down_inv
    ffn_tanh = jnp.tanh(ffn_gate)
    ffn_out_f = ffn_out_gain_full.astype(jnp.float32)
    block_out = (hidden_state + ffn_tanh * down_hat * ffn_out_f).astype(jnp.bfloat16)
    grad_out = cotangent.astype(jnp.float32)
    ffn_gate_grad = grad_out * down_hat * ffn_out_f * (1.0 - ffn_tanh * ffn_tanh)
    ffn_out_gain_part = jnp.sum(grad_out * ffn_tanh * down_hat, 0)
    down_grad = norm_back(down_hat, down_inv, grad_out * ffn_tanh * ffn_out_f).astype(jnp.bfloat16)
    down_weight_term = jnp.einsum(
        "tf,td->fd", activated, down_grad, preferred_element_type=jnp.float32
    )
    act_grad = jnp.einsum("td,fd->tf", down_grad, down_full, preferred_element_type=jnp.float32)
    gate_sig = jax.nn.sigmoid(gate_pre)
    gate_grad = (act_grad * up_pre * gate_sig * (1.0 + gate_pre * (1.0 - gate_sig))).astype(
        jnp.bfloat16
    )
    up_grad = (act_grad * jax.nn.silu(gate_pre)).astype(jnp.bfloat16)
    gate_weight_term = jnp.einsum(
        "td,tf->df", ffn_in, gate_grad, preferred_element_type=jnp.float32
    )
    up_weight_term = jnp.einsum("td,tf->df", ffn_in, up_grad, preferred_element_type=jnp.float32)
    ffn_in_grad = jnp.einsum(
        "tf,df->td", gate_grad, gate_full, preferred_element_type=jnp.float32
    ) + jnp.einsum("tf,df->td", up_grad, up_full, preferred_element_type=jnp.float32)
    ffn_gain_part = jnp.sum(ffn_in_grad * hidden_hat * (1.0 + ffn_scale), 0)
    ffn_scale_grad = ffn_in_grad * hidden_hat * ffn_gain_f
    hidden_grad = grad_out + norm_back(hidden_hat, hidden_inv, ffn_in_grad * ffn_mult)
    attn_gate_grad = hidden_grad * proj_hat * attn_out_f * (1.0 - attn_tanh * attn_tanh)
    attn_out_gain_part = jnp.sum(hidden_grad * attn_tanh * proj_hat, 0)
    proj_grad = norm_back(proj_hat, proj_inv, hidden_grad * attn_tanh * attn_out_f).astype(
        jnp.bfloat16
    )
    out_weight_term = jnp.einsum("td,te->de", mixed, proj_grad, preferred_element_type=jnp.float32)
    mixed_grad = jnp.einsum(
        "te,de->td", proj_grad, out_full, preferred_element_type=jnp.float32
    ).astype(jnp.bfloat16)
    mixed_heads_grad = mixed_grad.astype(jnp.float32).reshape(tok_rows, heads_total, head_dim)
    cross_gate_part = jnp.sum(mixed_heads_grad * cross_out, (0, 2)) * (1.0 - gate_tanh * gate_tanh)
    cross_out_grad = (mixed_heads_grad * gate_tanh[None, :, None]).astype(jnp.bfloat16)
    cross_prob_grad = jnp.einsum(
        "qhd,khd->qhk", cross_out_grad, text_value_heads, preferred_element_type=jnp.float32
    )
    text_value_term = jnp.einsum(
        "qhk,qhd->khd", cross_probs_low, cross_out_grad, preferred_element_type=jnp.float32
    )
    cross_delta = jnp.sum(cross_probs * cross_prob_grad, -1, keepdims=True)
    cross_score_grad = (cross_probs * (cross_prob_grad - cross_delta)).astype(jnp.bfloat16)
    query_cross_grad = (
        jnp.einsum(
            "qhk,khd->qhd", cross_score_grad, text_key_heads, preferred_element_type=jnp.float32
        )
        * score_scale
    )
    text_key_term = (
        jnp.einsum("qhk,qhd->khd", cross_score_grad, query_tok, preferred_element_type=jnp.float32)
        * score_scale
    )
    dout_flat = lax.all_to_all(mixed_grad, "sub", split_axis=1, concat_axis=0, tiled=True)
    dout_heads = dout_flat.reshape(group_rows, heads_local, head_dim)
    self_delta = jnp.sum(dout_heads.astype(jnp.float32) * self_out, -1)

    def backward_step(query_acc, block_in):
        key_blk, value_blk, block_start = block_in
        scores, allowed = block_scores(key_blk, block_start)
        prob_values = jnp.where(allowed, jnp.exp(scores - log_sum[..., None]), 0.0)
        prob_grad = jnp.einsum(
            "qhd,khd->qhk", dout_heads, value_blk, preferred_element_type=jnp.float32
        )
        value_term = jnp.einsum(
            "qhk,qhd->khd",
            prob_values.astype(jnp.bfloat16),
            dout_heads,
            preferred_element_type=jnp.float32,
        )
        score_grad = (prob_values * (prob_grad - self_delta[..., None])).astype(jnp.bfloat16)
        query_acc = (
            query_acc
            + jnp.einsum("qhk,khd->qhd", score_grad, key_blk, preferred_element_type=jnp.float32)
            * score_scale
        )
        key_term = (
            jnp.einsum("qhk,qhd->khd", score_grad, query_blocks, preferred_element_type=jnp.float32)
            * score_scale
        )
        return (query_acc, (key_term, value_term))

    query_zero = jnp.zeros((group_rows, heads_local, head_dim), jnp.float32)
    query_self_grad, (key_terms, value_terms) = lax.scan(
        backward_step, query_zero, (key_stack, value_stack, block_starts)
    )
    key_grad_heads, value_grad_heads = (
        lax.psum_scatter(
            key_terms.reshape(total_tokens, heads_local * head_dim).astype(jnp.bfloat16),
            "seq",
            scatter_dimension=0,
            tiled=True,
        ).astype(jnp.float32),
        lax.psum_scatter(
            value_terms.reshape(total_tokens, heads_local * head_dim).astype(jnp.bfloat16),
            "seq",
            scatter_dimension=0,
            tiled=True,
        ).astype(jnp.float32),
    )
    query_back, key_back, value_back = (
        lax.all_to_all(
            query_self_grad.reshape(group_rows, heads_local * head_dim).astype(jnp.bfloat16),
            "sub",
            split_axis=0,
            concat_axis=1,
            tiled=True,
        ).astype(jnp.float32),
        lax.all_to_all(
            round_keep(key_grad_heads).astype(jnp.bfloat16),
            "sub",
            split_axis=0,
            concat_axis=1,
            tiled=True,
        ).astype(jnp.float32),
        lax.all_to_all(
            round_keep(value_grad_heads).astype(jnp.bfloat16),
            "sub",
            split_axis=0,
            concat_axis=1,
            tiled=True,
        ).astype(jnp.float32),
    )
    query_rot_grad = round_keep(
        query_back.reshape(tok_rows, heads_total, head_dim) + query_cross_grad
    )
    query_norm_grad = rotate(query_rot_grad, cosine, -sine).reshape(tok_rows, model_width)
    query_gain_part = jnp.sum(query_norm_grad * query_hat, 0)
    query_pre_grad = norm_back(query_hat, query_inv, query_norm_grad * query_gain_f).astype(
        jnp.bfloat16
    )
    key_norm_grad = rotate(
        key_back.reshape(tok_rows, heads_total, head_dim), cosine, -sine
    ).reshape(tok_rows, model_width)
    key_gain_part = jnp.sum(key_norm_grad * key_hat, 0)
    key_pre_grad = norm_back(key_hat, key_inv, key_norm_grad * key_gain_f).astype(jnp.bfloat16)
    value_grad = value_back.astype(jnp.bfloat16)
    query_weight_term = jnp.einsum(
        "td,te->de", normed, query_pre_grad, preferred_element_type=jnp.float32
    )
    key_weight_term = jnp.einsum(
        "td,te->de", normed, key_pre_grad, preferred_element_type=jnp.float32
    )
    value_weight_term = jnp.einsum(
        "td,te->de", normed, value_grad, preferred_element_type=jnp.float32
    )
    normed_grad = (
        jnp.einsum("te,de->td", query_pre_grad, query_full, preferred_element_type=jnp.float32)
        + jnp.einsum("te,de->td", key_pre_grad, key_full, preferred_element_type=jnp.float32)
        + jnp.einsum("te,de->td", value_grad, value_full, preferred_element_type=jnp.float32)
    )
    attn_gain_part = jnp.sum(normed_grad * video_hat * (1.0 + attn_scale), 0)
    attn_scale_grad = normed_grad * video_hat * attn_gain_f
    video_grad = hidden_grad + norm_back(video_hat, video_inv, normed_grad * attn_mult)
    text_key_sum, text_value_sum = (
        lax.psum_scatter(
            text_key_term.reshape(cap_total, model_width),
            ("seq", "sub"),
            scatter_dimension=0,
            tiled=True,
        ),
        lax.psum_scatter(
            text_value_term.reshape(cap_total, model_width),
            ("seq", "sub"),
            scatter_dimension=0,
            tiled=True,
        ),
    )
    text_key_low = round_keep(text_key_sum)
    text_value_low = text_value_sum.astype(jnp.bfloat16)
    text_key_gain_part = jnp.sum(text_key_low * text_hat, 0)
    text_key_pre_grad = norm_back(text_hat, text_inv, text_key_low * text_key_gain_f).astype(
        jnp.bfloat16
    )
    text_key_weight_term = jnp.einsum(
        "tc,td->cd", cap_local, text_key_pre_grad, preferred_element_type=jnp.float32
    )
    text_value_weight_term = jnp.einsum(
        "tc,td->cd", cap_local, text_value_low, preferred_element_type=jnp.float32
    )
    caption_rows_grad = jnp.einsum(
        "td,cd->tc", text_key_pre_grad, text_key_full, preferred_element_type=jnp.float32
    ) + jnp.einsum("td,cd->tc", text_value_low, text_value_full, preferred_element_type=jnp.float32)
    caption_grad = lax.all_gather(
        caption_rows_grad.astype(jnp.bfloat16), "seq", axis=0, tiled=True
    ).astype(caption_rows_grad.dtype)
    token_mod_grad = jnp.concatenate(
        [attn_scale_grad, attn_gate_grad, ffn_scale_grad, ffn_gate_grad], 1
    )
    mod_part = jnp.einsum("tc,tm->cm", clip_onehot, token_mod_grad, precision=highest)
    mod_sum, gate_sum = lax.psum((mod_part, cross_gate_part), ("seq", "sub"))
    mod_low = mod_sum.astype(jnp.bfloat16)
    bias_rows = ada_bias.shape[0]
    ada_bias_grad = jnp.sum(
        lax.dynamic_slice_in_dim(
            mod_low.astype(jnp.float32), device_index * bias_rows, bias_rows, 1
        ),
        0,
    )
    cond_rows = ada_weight.shape[0]
    cond_slice = lax.dynamic_slice_in_dim(cond_act, device_index * cond_rows, cond_rows, 1)
    ada_weight_grad = jnp.einsum(
        "cr,cm->rm", cond_slice, mod_low, preferred_element_type=jnp.float32
    )
    cond_sig = jax.nn.sigmoid(cond_float)
    cond_grad = (
        jnp.einsum("cm,rm->cr", mod_low, ada_full, preferred_element_type=jnp.float32)
        * cond_sig
        * (1.0 + cond_float * (1.0 - cond_sig))
    )
    (
        query_weight_grad,
        key_weight_grad,
        value_weight_grad,
        out_weight_grad,
        text_key_weight_grad,
        text_value_weight_grad,
        attn_gain_grad,
        query_gain_grad,
        key_gain_grad,
        text_key_gain_grad,
        attn_out_gain_grad,
    ) = (
        lax.psum_scatter(query_weight_term, ("seq", "sub"), scatter_dimension=0, tiled=True),
        lax.psum_scatter(key_weight_term, ("seq", "sub"), scatter_dimension=0, tiled=True),
        lax.psum_scatter(value_weight_term, ("seq", "sub"), scatter_dimension=0, tiled=True),
        lax.psum_scatter(out_weight_term, ("seq", "sub"), scatter_dimension=0, tiled=True),
        lax.psum_scatter(text_key_weight_term, ("seq", "sub"), scatter_dimension=0, tiled=True),
        lax.psum_scatter(text_value_weight_term, ("seq", "sub"), scatter_dimension=0, tiled=True),
        lax.psum_scatter(attn_gain_part, ("seq", "sub"), scatter_dimension=0, tiled=True),
        lax.psum_scatter(query_gain_part, ("seq", "sub"), scatter_dimension=0, tiled=True),
        lax.psum_scatter(key_gain_part, ("seq", "sub"), scatter_dimension=0, tiled=True),
        lax.psum_scatter(text_key_gain_part, ("seq", "sub"), scatter_dimension=0, tiled=True),
        lax.psum_scatter(attn_out_gain_part, ("seq", "sub"), scatter_dimension=0, tiled=True),
    )
    gate_weight_grad, up_weight_grad, down_weight_grad, ffn_gain_grad, ffn_out_gain_grad = (
        lax.psum_scatter(gate_weight_term, ("seq", "sub"), scatter_dimension=0, tiled=True),
        lax.psum_scatter(up_weight_term, ("seq", "sub"), scatter_dimension=0, tiled=True),
        lax.psum_scatter(down_weight_term, ("seq", "sub"), scatter_dimension=0, tiled=True),
        lax.psum_scatter(ffn_gain_part, ("seq", "sub"), scatter_dimension=0, tiled=True),
        lax.psum_scatter(ffn_out_gain_part, ("seq", "sub"), scatter_dimension=0, tiled=True),
    )
    return (
        block_out,
        video_grad,
        caption_grad,
        cond_grad,
        ada_weight_grad,
        ada_bias_grad,
        query_weight_grad,
        key_weight_grad,
        value_weight_grad,
        out_weight_grad,
        text_key_weight_grad,
        text_value_weight_grad,
        gate_weight_grad,
        up_weight_grad,
        down_weight_grad,
        attn_gain_grad,
        query_gain_grad,
        key_gain_grad,
        text_key_gain_grad,
        attn_out_gain_grad,
        ffn_gain_grad,
        ffn_out_gain_grad,
        gate_sum,
    )


def solution(mesh):
    placed = (
        P(("seq", "sub"), None),
        P(),
        P("sub", None),
        P(),
        P(),
        P(("seq", "sub"), None),
        P(("seq", "sub"), None),
        P(("seq", "sub")),
        P(("seq", "sub"), None),
        P(("seq", "sub"), None),
        P(("seq", "sub"), None),
        P(("seq", "sub"), None),
        P(("seq", "sub"), None),
        P(("seq", "sub"), None),
        P(("seq", "sub"), None),
        P(("seq", "sub"), None),
        P(("seq", "sub"), None),
        P(("seq", "sub")),
        P(("seq", "sub")),
        P(("seq", "sub")),
        P(("seq", "sub")),
        P(("seq", "sub")),
        P(("seq", "sub")),
        P(("seq", "sub")),
        P(),
        P(("seq", "sub"), None),
    )
    return jax.shard_map(
        body,
        mesh=mesh,
        in_specs=placed,
        out_specs=(
            P(("seq", "sub"), None),
            P(("seq", "sub"), None),
            P("sub", None),
            P(),
            P(("seq", "sub"), None),
            P(("seq", "sub")),
            P(("seq", "sub"), None),
            P(("seq", "sub"), None),
            P(("seq", "sub"), None),
            P(("seq", "sub"), None),
            P(("seq", "sub"), None),
            P(("seq", "sub"), None),
            P(("seq", "sub"), None),
            P(("seq", "sub"), None),
            P(("seq", "sub"), None),
            P(("seq", "sub")),
            P(("seq", "sub")),
            P(("seq", "sub")),
            P(("seq", "sub")),
            P(("seq", "sub")),
            P(("seq", "sub")),
            P(("seq", "sub")),
            P(),
        ),
        check_vma=False,
    )
```

profile of v0, /device:TPU:0, one launch (start us, length us, event | category | flops | bytes accessed | tf_op | source)
XLA Modules:
  0.0 3359.7 jit_solution(13927837446089272986)
XLA Ops:
  18.0 43.6 %all-reduce.16 = (bf16[6144]{0:T(1024)(128)(2,1)S(1)}, bf16[1536]{0:T(1024)(128)(2,1)S(1)}, bf16[1536]{0:T(1024)(128)(2,1)S(1)}, bf16[1536]{0:T(1024)(128)(2,1)S...) all-reduce(bf16[6144]{0:T(1024)(128)(2,1)S(1)} %dynamic-update-slic, ...), channel_id=1, replica_groups=mesh['seq'=8,'sub'=4] {'seq','sub'}, use_global_device_ids=true, to_apply=%add | all-reduce | flops 16896 | bytes 67584
  66.6 43.6 %all-gather.16.cloned.1.call-done = bf16[1024,6144]{1,0:T(8,128)(2,1)} async-done(((bf16[32,6144]{1,0:T(8,128)(2,1)}), bf16[1024,6144]{1,0:T(8,128)(2,1)}) %all-gather.16.cloned.1.call-update) | async-done | bytes 12582928 | tf_op jit(solution)/shard_map/all_gather | solution.py:119
  119.8 55.0 %all-gather.18.cloned.1.call-done = bf16[1536,1536]{1,0:T(8,128)(2,1)} async-done(((bf16[48,1536]{1,0:T(8,128)(2,1)}), bf16[1536,1536]{1,0:T(8,128)(2,1)}) %all-gather.18.cloned.1.call-update) | async-done | bytes 4718608 | tf_op jit(solution)/shard_map/all_gather | solution.py:122
  185.5 17.2 all_to_all.119
  203.7 37.7 %all-gather.24.cloned.1.call-done = bf16[1536,1536]{1,0:T(8,128)(2,1)} async-done(((bf16[48,1536]{1,0:T(8,128)(2,1)}), bf16[1536,1536]{1,0:T(8,128)(2,1)}) %all-gather.24.cloned.1.call-update) | async-done | bytes 4718608 | tf_op jit(solution)/shard_map/all_gather | solution.py:123
  244.6 21.8 all_to_all.120
  266.8 75.5 %all-gather.32.cloned.1.call-done = bf16[4096,1536]{1,0:T(8,128)(2,1)} async-done(((bf16[128,1536]{1,0:T(8,128)(2,1)}), bf16[4096,1536]{1,0:T(8,128)(2,1)}) %all-gather.32.cloned.1.call-update) | async-done | bytes 12582928 | tf_op jit(solution)/shard_map/all_gather | solution.py:125
  350.6 88.7 %all-gather.28.cloned.1.call-done = bf16[4096,1536]{1,0:T(8,128)(2,1)} async-done(((bf16[128,1536]{1,0:T(8,128)(2,1)}), bf16[4096,1536]{1,0:T(8,128)(2,1)}) %all-gather.28.cloned.1.call-update) | async-done | bytes 12582928 | tf_op jit(solution)/shard_map/all_gather | solution.py:126
  449.4 54.4 %all-gather.22.cloned.1.call-done = bf16[1536,1536]{1,0:T(8,128)(2,1)} async-done(((bf16[48,1536]{1,0:T(8,128)(2,1)}), bf16[1536,1536]{1,0:T(8,128)(2,1)}) %all-gather.22.cloned.1.call-update) | async-done | bytes 4718608 | tf_op jit(solution)/shard_map/all_gather | solution.py:121
  552.9 18.8 all-gather.26.cloned.1.call-done
  587.1 106.7 %while.34 = (s32[]{:T(128)}, f32[512,6]{0,1:T(8,128)S(1)}, f32[512,6]{0,1:T(8,128)}, f32[512,6,64]{0,2,1:T(8,128)}, s32[512]{0:T(512)}, /*index=5*/s32[4]{0:T(12...) while((s32[]{:T(128)}, f32[512,6]{0,1:T(8,128)S(1)}, ...), condition=%wide.region_10.11_spmd.clone, body=%wide.region_6.10_spmd.clone.sunk | while | flops 847345664 | bytes 94031096 | solution.py:230
  705.4 10.3 all-to-all-done.3
  729.3 19.0 fusion.152
  748.3 9.3 add_convert_fusion.1
  770.8 91.8 %all-gather.38.cloned.1.call-done = bf16[1536,4096]{1,0:T(8,128)(2,1)} async-done(((bf16[48,4096]{1,0:T(8,128)(2,1)}), bf16[1536,4096]{1,0:T(8,128)(2,1)}) %all-gather.38.cloned.1.call-update) | async-done | bytes 12582928 | tf_op jit(solution)/shard_map/all_gather | solution.py:135
  870.4 89.5 %all-gather.40.cloned.1.call-done = bf16[1536,4096]{1,0:T(8,128)(2,1)} async-done(((bf16[48,4096]{1,0:T(8,128)(2,1)}), bf16[1536,4096]{1,0:T(8,128)(2,1)}) %all-gather.40.cloned.1.call-update) | async-done | bytes 12582928 | tf_op jit(solution)/shard_map/all_gather | solution.py:136
  959.9 9.0 multiply_convert_fusion.2
  968.8 88.1 %all-gather.42.cloned.1.call-done = bf16[4096,1536]{1,0:T(8,128)(2,1)} async-done(((bf16[128,1536]{1,0:T(8,128)(2,1)}), bf16[4096,1536]{1,0:T(8,128)(2,1)}) %all-gather.42.cloned.1.call-update) | async-done | bytes 12582928 | tf_op jit(solution)/shard_map/all_gather | solution.py:137
  1066.4 10.2 multiply_convert_fusion
  1076.6 10.0 fusion.154
  1086.6 9.8 multiply_reduce_fusion.2
  1102.6 12.2 fusion.50
  1114.8 10.8 fusion.52
  1132.9 9.2 copy.244
  1147.8 12.5 fusion.58
  1160.2 9.3 copy.256
  1174.6 131.5 %while.35 = (s32[]{:T(128)}, f32[512,6,64]{0,2,1:T(8,128)}, bf16[4,1024,6,64]{1,3,2,0:T(8,128)(2,1)}, bf16[4,1024,6,64]{1,3,2,0:T(8,128)(2,1)}, bf16[4,1024,6,64...) while((s32[]{:T(128)}, f32[512,6,64]{0,2,1:T(8,128)}, ...), condition=%wide.region_24.25_spmd.clone, body=%wide.region_22.24_spmd.clone.sunk | while | flops 2052537344 | bytes 142549840 | solution.py:396
  1230.9 9.0 bitcast_dynamic-update-slice_fusion.5
  1296.3 9.4 bitcast_dynamic-update-slice_fusion.5
  1322.6 68.4 %reduce-scatter.40.cloned.1.call-done = f32[40,1536]{1,0:T(8,128)} async-done(((f32[1280,1536]{1,0:T(8,128)}), f32[40,1536]{1,0:T(8,128)}) %reduce-scatter.40.cloned.1.call-update) | async-done | bytes 245776
  1400.9 10.2 fusion.57
  1420.3 13.4 all_to_all.121
  1493.0 14.5 all_to_all.122
  1513.4 11.6 fusion.163
  1526.0 11.7 fusion.161
  1537.8 12.3 fusion.162
  1551.1 11.0 fusion.101
  1562.3 10.7 fusion.103
  1591.3 42.9 %all-reduce.18 = (bf16[5,6144]{1,0:T(8,128)(2,1)S(1)}, f32[1536]{0:T(1024)S(1)}, f32[1536]{0:T(1024)S(1)}, f32[1536]{0:T(1024)S(1)}, f32[1536]{0:T(1024)S(1)}, /...) all-reduce(f32[5,6144]{1,0:T(8,128)S(1)} %fusion.62, ...), channel_id=1, replica_groups=mesh['seq'=8,'sub'=4] {'seq','sub'}, use_global_device_ids=true, to_apply=%region_34.35 | all-reduce | flops 41496 | bytes 270528 | tf_op jit(solution)/shard_map/psum | solution.py:503
  1653.7 11.9 reduce-scatter.28.cloned.1.call-done
  1665.5 141.9 %reduce-scatter.24.cloned.1.call-done = f32[48,1536]{1,0:T(8,128)} async-done(((f32[1536,1536]{1,0:T(8,128)}), f32[48,1536]{1,0:T(8,128)}) %reduce-scatter.24.cloned.1.call-update) | async-done | bytes 294928 | tf_op jit(solution)/shard_map/reduce_scatter | solution.py:537
  1807.4 141.1 %reduce-scatter.22.cloned.1.call-done = f32[48,1536]{1,0:T(8,128)} async-done(((f32[1536,1536]{1,0:T(8,128)}), f32[48,1536]{1,0:T(8,128)}) %reduce-scatter.22.cloned.1.call-update) | async-done | bytes 294928 | tf_op jit(solution)/shard_map/reduce_scatter | solution.py:536
  1948.5 142.4 %reduce-scatter.26.cloned.1.call-done = f32[48,1536]{1,0:T(8,128)} async-done(((f32[1536,1536]{1,0:T(8,128)}), f32[48,1536]{1,0:T(8,128)}) %reduce-scatter.26.cloned.1.call-update) | async-done | bytes 294928 | tf_op jit(solution)/shard_map/reduce_scatter | solution.py:538
  2090.9 251.3 %reduce-scatter.38.cloned.1.call-done = f32[128,1536]{1,0:T(8,128)} async-done(((f32[4096,1536]{1,0:T(8,128)}), f32[128,1536]{1,0:T(8,128)}) %reduce-scatter.38.cloned.1.call-update) | async-done | bytes 786448 | tf_op jit(solution)/shard_map/reduce_scatter | solution.py:551
  2342.2 253.2 %reduce-scatter.34.cloned.1.call-done = f32[48,4096]{1,0:T(8,128)} async-done(((f32[1536,4096]{1,0:T(8,128)}), f32[48,4096]{1,0:T(8,128)}) %reduce-scatter.34.cloned.1.call-update) | async-done | bytes 786448 | tf_op jit(solution)/shard_map/reduce_scatter | solution.py:549
  2595.4 251.9 %reduce-scatter.36.cloned.1.call-done = f32[48,4096]{1,0:T(8,128)} async-done(((f32[1536,4096]{1,0:T(8,128)}), f32[48,4096]{1,0:T(8,128)}) %reduce-scatter.36.cloned.1.call-update) | async-done | bytes 786448 | tf_op jit(solution)/shard_map/reduce_scatter | solution.py:550
  2847.3 253.1 %reduce-scatter.32.cloned.1.call-done = f32[128,1536]{1,0:T(8,128)} async-done(((f32[4096,1536]{1,0:T(8,128)}), f32[128,1536]{1,0:T(8,128)}) %reduce-scatter.32.cloned.1.call-update) | async-done | bytes 786448 | tf_op jit(solution)/shard_map/reduce_scatter | solution.py:541
  3100.4 252.1 %reduce-scatter.30.cloned.1.call-done = f32[128,1536]{1,0:T(8,128)} async-done(((f32[4096,1536]{1,0:T(8,128)}), f32[128,1536]{1,0:T(8,128)}) %reduce-scatter.30.cloned.1.call-update) | async-done | bytes 786448 | tf_op jit(solution)/shard_map/reduce_scatter | solution.py:540
  (525 shorter events, 561.7 us)
Async XLA Ops:
  7.2 335.1 %copy-start = (bf16[320,4096]{1,0:T(8,128)(2,1)S(1)}, bf16[320,4096]{1,0:T(8,128)(2,1)}, u32[]{:S(2)}) copy-start(bf16[320,4096]{1,0:T(8,128)(2,1)} %param.32) | copy-start | bytes 7864324
  7.2 103.0 %all-gather.16.cloned.1.call-start = ((), (), s32[]{:S(2)}) async-start(), calls=%async_computation.21 | async-start | bytes 12976128 | tf_op jit(solution)/shard_map/all_gather | solution.py:119
  7.9 166.9 %all-gather.18.cloned.1.call-start = ((), (), s32[]{:S(2)}) async-start(), calls=%async_computation.22 | async-start | bytes 4866048 | tf_op jit(solution)/shard_map/all_gather | solution.py:122
  8.7 232.8 %all-gather.24.cloned.1.call-start = ((), (), s32[]{:S(2)}) async-start(), calls=%async_computation.25 | async-start | bytes 4866048 | tf_op jit(solution)/shard_map/all_gather | solution.py:123
  9.4 332.9 %all-gather.32.cloned.1.call-start = ((), (), s32[]{:S(2)}) async-start(), calls=%async_computation.29 | async-start | bytes 12976128 | tf_op jit(solution)/shard_map/all_gather | solution.py:125
  10.0 429.3 %all-gather.28.cloned.1.call-start = ((), (), s32[]{:S(2)}) async-start(), calls=%async_computation.27 | async-start | bytes 12976128 | tf_op jit(solution)/shard_map/all_gather | solution.py:126
  10.6 493.2 %all-gather.22.cloned.1.call-start = ((), (), s32[]{:S(2)}) async-start(), calls=%async_computation.24 | async-start | bytes 4866048 | tf_op jit(solution)/shard_map/all_gather | solution.py:121
  11.2 526.3 %all-gather.20.cloned.1.call-start = ((), (), s32[]{:S(2)}) async-start(), calls=%async_computation.23 | async-start | bytes 3538944 | tf_op jit(solution)/shard_map/all_gather | solution.py:187
  61.6 56.3 %copy-start.52 = (f32[1536]{0:T(1024)}, f32[1536]{0:T(1024)S(1)}, u32[]{:S(2)}) copy-start(f32[1536]{0:T(1024)S(1)} %convert_element_type.257) | copy-start | bytes 18436
  61.6 116.4 %copy-start.54 = (f32[1536]{0:T(1024)}, f32[1536]{0:T(1024)S(1)}, u32[]{:S(2)}) copy-start(f32[1536]{0:T(1024)S(1)} %convert_element_type.259) | copy-start | bytes 18436
  64.7 445.7 %copy-start.45 = (f32[128,32]{0,1:T(8,128)}, f32[128,32]{0,1:T(8,128)S(1)}, u32[]{:S(2)}) copy-start(f32[128,32]{0,1:T(8,128)S(1)} %get-tuple-element.628) | copy-start | bytes 49156
  66.6 51.4 %copy-start.68 = (f32[128]{0:T(128)}, f32[128]{0:T(128)S(1)}, u32[]{:S(2)}) copy-start(f32[128]{0:T(128)S(1)} %add_rsqrt_fusion.6) | copy-start | bytes 1540
  66.6 53.0 %copy-start.20 = (bf16[128,1536]{1,0:T(8,128)(2,1)S(1)}, bf16[128,1536]{1,0:T(8,128)(2,1)}, u32[]{:S(2)}) copy-start(bf16[128,1536]{1,0:T(8,128)(2,1)} %param.30) | copy-start | bytes 1179652
  119.8 384.0 %copy-start.10 = (bf16[128,1536]{1,0:T(8,128)(2,1)}, bf16[128,1536]{1,0:T(8,128)(2,1)S(1)}, u32[]{:S(2)}) copy-start(bf16[128,1536]{1,0:T(8,128)(2,1)S(1)} %fusion.84) | copy-start | bytes 1179652
  178.0 66.6 %copy-start.70 = (f32[128]{0:T(128)}, f32[128]{0:T(128)S(1)}, u32[]{:S(2)}) copy-start(f32[128]{0:T(128)S(1)} %add_rsqrt_fusion.5) | copy-start | bytes 1540
  203.7 368.0 %all-gather.26.cloned.1.call-start = ((), (), s32[]{:S(2)}) async-start(), calls=%async_computation.26 | async-start | bytes 3538944 | tf_op jit(solution)/shard_map/all_gather | solution.py:188
  266.4 450.2 %all-gather.34.cloned.1.call-start = ((), (), s32[]{:S(2)}) async-start(), calls=%async_computation.30 | async-start | bytes 4055040 | tf_op jit(solution)/shard_map/all_gather | solution.py:254
  266.7 82.4 %copy-start.58 = (f32[1536]{0:T(1024)}, f32[1536]{0:T(1024)S(1)}, u32[]{:S(2)}) copy-start(f32[1536]{0:T(1024)S(1)} %convert_element_type.274) | copy-start | bytes 18436
  349.1 97.6 %copy-start.74 = (f32[40]{0:T(128)}, f32[40]{0:T(128)S(1)}, u32[]{:S(2)}) copy-start(f32[40]{0:T(128)S(1)} %add_rsqrt_fusion.3) | copy-start | bytes 484
  350.6 372.4 %all-gather.30.cloned.1.call-start = ((), (), s32[]{:S(2)}) async-start(), calls=%async_computation.28 | async-start | bytes 4055040 | tf_op jit(solution)/shard_map/all_gather | solution.py:255
  446.7 318.3 %all-gather.36.cloned.1.call-start = ((), (), s32[]{:S(2)}) async-start(), calls=%async_computation.31 | async-start | bytes 4866048 | tf_op jit(solution)/shard_map/all_gather | solution.py:124
  447.5 415.2 %all-gather.38.cloned.1.call-start = ((), (), s32[]{:S(2)}) async-start(), calls=%async_computation.32 | async-start | bytes 12976128 | tf_op jit(solution)/shard_map/all_gather | solution.py:135
  448.0 511.8 %all-gather.40.cloned.1.call-start = ((), (), s32[]{:S(2)}) async-start(), calls=%async_computation.33 | async-start | bytes 12976128 | tf_op jit(solution)/shard_map/all_gather | solution.py:136
  448.8 608.1 %all-gather.42.cloned.1.call-start = ((), (), s32[]{:S(2)}) async-start(), calls=%async_computation.34 | async-start | bytes 12976128 | tf_op jit(solution)/shard_map/all_gather | solution.py:137
  449.4 57.7 %copy-start.56 = (f32[1536]{0:T(1024)}, f32[1536]{0:T(1024)S(1)}, u32[]{:S(2)}) copy-start(f32[1536]{0:T(1024)S(1)} %convert_element_type.264) | copy-start | bytes 18436
  449.4 70.7 %copy-start.78 = (s32[5]{0:T(128)S(1)}, s32[5]{0:T(128)}, u32[]{:S(2)}) copy-start(s32[5]{0:T(128)} %param.34) | copy-start | bytes 64
  513.0 15.8 all-to-all-start.1
  697.7 18.0 all-to-all-start.3
  702.5 619.1 %reduce-scatter.20.cloned.1.call-start = ((), (), s32[]{:S(2)}) async-start(), calls=%async_computation.37 | async-start | bytes 8110080 | tf_op jit(solution)/shard_map/reduce_scatter | solution.py:468
  770.8 189.1 %copy-start.23 = (bf16[128,1536]{1,0:T(8,128)(2,1)}, bf16[128,1536]{1,0:T(8,128)(2,1)S(1)}, u32[]{:S(2)}) copy-start(bf16[128,1536]{1,0:T(8,128)(2,1)S(1)} %multiply_convert_fusion.8) | copy-start | bytes 1179652
  1144.2 25.4 all-to-all-start.4
  1147.7 243.3 %reduce-scatter.40.cloned.1.call-start = ((), (), s32[]{:S(2)}) async-start(), calls=%async_computation.48 | async-start | bytes 8110080
  1169.6 270.9 %reduce-scatter.16.cloned.1.call-start = ((), (), s32[]{:S(2)}) async-start(), calls=%async_computation.35 | async-start | bytes 3538944 | tf_op jit(solution)/shard_map/reduce_scatter | solution.py:400
  1313.6 178.3 %reduce-scatter.18.cloned.1.call-start = ((), (), s32[]{:S(2)}) async-start(), calls=%async_computation.36 | async-start | bytes 3538944 | tf_op jit(solution)/shard_map/reduce_scatter | solution.py:406
  1318.0 74.2 %copy-start.28 = (f32[40,1536]{1,0:T(8,128)S(1)}, f32[40,1536]{1,0:T(8,128)}, u32[]{:S(2)}) copy-start(f32[40,1536]{1,0:T(8,128)} %copy-done.27) | copy-start | bytes 737284
  1318.0 74.2 %copy-start.59 = (f32[1536]{0:T(1024)S(1)}, f32[1536]{0:T(1024)}, u32[]{:S(2)}) copy-start(f32[1536]{0:T(1024)} %copy-done.58) | copy-start | bytes 18436
  1318.0 74.2 %copy-start.75 = (f32[40]{0:T(128)S(1)}, f32[40]{0:T(128)}, u32[]{:S(2)}) copy-start(f32[40]{0:T(128)} %copy-done.74) | copy-start | bytes 484
  1321.5 327.4 %all-gather.44.cloned.1.call-start = ((), (), s32[]{:S(2)}) async-start(), calls=%async_computation.38 | async-start | bytes 2949120 | tf_op jit(solution)/shard_map/all_gather | solution.py:496
  1411.1 254.4 %reduce-scatter.28.cloned.1.call-start = ((), (), s32[]{:S(2)}) async-start(), calls=%async_computation.42 | async-start | bytes 9732096 | tf_op jit(solution)/shard_map/reduce_scatter | solution.py:539
  1442.3 16.4 all-to-all-start.6
  1446.9 360.5 %reduce-scatter.24.cloned.1.call-start = ((), (), s32[]{:S(2)}) async-start(), calls=%async_computation.40 | async-start | bytes 9732096 | tf_op jit(solution)/shard_map/reduce_scatter | solution.py:537
  1480.5 468.0 %reduce-scatter.22.cloned.1.call-start = ((), (), s32[]{:S(2)}) async-start(), calls=%async_computation.39 | async-start | bytes 9732096 | tf_op jit(solution)/shard_map/reduce_scatter | solution.py:536
  1491.8 599.1 %reduce-scatter.26.cloned.1.call-start = ((), (), s32[]{:S(2)}) async-start(), calls=%async_computation.41 | async-start | bytes 9732096 | tf_op jit(solution)/shard_map/reduce_scatter | solution.py:538
  1512.4 829.8 %reduce-scatter.38.cloned.1.call-start = ((), (), s32[]{:S(2)}) async-start(), calls=%async_computation.47 | async-start | bytes 25952256 | tf_op jit(solution)/shard_map/reduce_scatter | solution.py:551
  1525.1 1070.3 %reduce-scatter.34.cloned.1.call-start = ((), (), s32[]{:S(2)}) async-start(), calls=%async_computation.45 | async-start | bytes 25952256 | tf_op jit(solution)/shard_map/reduce_scatter | solution.py:549
  1537.8 1309.5 %reduce-scatter.36.cloned.1.call-start = ((), (), s32[]{:S(2)}) async-start(), calls=%async_computation.46 | async-start | bytes 25952256 | tf_op jit(solution)/shard_map/reduce_scatter | solution.py:550
  1550.2 1550.2 %reduce-scatter.32.cloned.1.call-start = ((), (), s32[]{:S(2)}) async-start(), calls=%async_computation.44 | async-start | bytes 25952256 | tf_op jit(solution)/shard_map/reduce_scatter | solution.py:541
  1562.2 1790.2 %reduce-scatter.30.cloned.1.call-start = ((), (), s32[]{:S(2)}) async-start(), calls=%async_computation.43 | async-start | bytes 25952256 | tf_op jit(solution)/shard_map/reduce_scatter | solution.py:540
  (92 other events, 680.2 us)
Sparse Core Ops, SparseCore 0:
  10.9 99.2 all-gather.15
  113.0 61.7 all-gather.17
  177.6 63.7 all-gather.23
  244.2 98.0 all-gather.31
  345.0 94.2 all-gather.27
  442.0 61.7 all-gather.21
  506.3 31.1 all-gather.19
  539.3 32.3 all-gather.25
  575.1 61.1 all-gather.33
  639.5 59.9 all-gather.29
  702.3 62.6 all-gather.35
  767.8 94.8 all-gather.37
  865.5 94.2 all-gather.39
  962.6 94.2 all-gather.41
  1142.3 120.7 reduce-scatter.19
  1269.5 121.4 reduce-scatter.39
  1394.8 45.5 reduce-scatter.15
  1444.0 46.2 reduce-scatter.17
  1492.2 30.0 all-gather.43
  1528.6 136.8 reduce-scatter.27
  1673.0 134.3 reduce-scatter.23
  1813.9 134.5 reduce-scatter.21
  1956.0 134.8 reduce-scatter.25
  2097.7 244.4 reduce-scatter.37
  2350.3 245.0 reduce-scatter.33
  2602.2 245.0 reduce-scatter.35
  2855.3 245.0 reduce-scatter.31
  3107.4 245.0 reduce-scatter.29
where the time goes:
time: 3370 us; the launch traced here: 3360 us
  waiting for transfers between devices  2460 us (73%)
  matrix products  440 us (13%)
  local copies, waits for them, and re-layouts  155 us (5%)
  blocking collectives  153 us (5%)
  other arithmetic  117 us (3%)
    reduce_scatter x1, waiting for transfers between devices, body(): lax.psum_scatter(gate_weight_term, ('seq', 'sub'), scatter_dimension=0, t...  253 us
    reduce_scatter x1, waiting for transfers between devices, body(): lax.psum_scatter(text_value_weight_term, ('seq', 'sub'), scatter_dimensio...  253 us
    reduce_scatter x1, waiting for transfers between devices, body(): lax.psum_scatter(text_key_weight_term, ('seq', 'sub'), scatter_dimension=...  252 us
    reduce_scatter x1, waiting for transfers between devices, body(): lax.psum_scatter(up_weight_term, ('seq', 'sub'), scatter_dimension=0, til...  252 us
    reduce_scatter x1, waiting for transfers between devices, body(): lax.psum_scatter(down_weight_term, ('seq', 'sub'), scatter_dimension=0, t...  251 us
    all_gather x2, waiting for transfers between devices, body(): lax.all_gather(barrier_set[2], ('seq', 'sub'), axis=0, tiled=True)  142 us
    reduce_scatter x1, waiting for transfers between devices, body(): lax.psum_scatter(value_weight_term, ('seq', 'sub'), scatter_dimension=0,...  142 us
    reduce_scatter x1, waiting for transfers between devices, body(): lax.psum_scatter(key_weight_term, ('seq', 'sub'), scatter_dimension=0, ti...  142 us
  transfers between devices with their start and end apart: 32, of which 26 were waited for; matrix products, arithmetic and copies ran while one was open for 18% of the time, Pallas kernels for 0%

commit v1 on v0

v1 whole, which is shorter than its diff:
```python
import functools
import math

import jax
import jax.numpy as jnp
import numpy as np
from jax import lax
from jax.experimental import pallas as pl
from jax.experimental.pallas import tpu as pltpu
from jax.sharding import PartitionSpec as P

CAP = 256
KEY_BLOCK = 256
epsilon = 1e-06
rope_base = 10000.0
masked_score = -1e30
BF = jnp.bfloat16
F32 = jnp.float32
BOTH = ("seq", "sub")
VMEM_BYTES = 56 * 1024 * 1024


def xor_permute(values, axis, mask):
    count = lax.axis_size(axis)
    return lax.ppermute(values, axis, [(i, i ^ mask) for i in range(count)])


def axis_bits(axis):
    masks, mask = [], 1
    while mask < lax.axis_size(axis):
        masks.append(mask)
        mask *= 2
    return masks


def gather_cube(values, axis, order):
    index = lax.axis_index(axis)
    buffer = values[None]
    for mask in order:
        other = xor_permute(buffer, axis, mask)
        high = (index // mask) % 2 == 1
        buffer = jnp.stack([jnp.where(high, other, buffer), jnp.where(high, buffer, other)], 0)
    now = list(reversed(order))
    wanted = sorted(order, reverse=True)
    buffer = buffer.reshape((2,) * len(order) + values.shape)
    buffer = buffer.transpose(
        [now.index(mask) for mask in wanted] + list(range(len(order), buffer.ndim))
    )
    return buffer.reshape((-1,) + values.shape[1:])


def gather_seq(values):
    masks = axis_bits("seq")
    half = values.shape[-1] // 2
    first = masks[1:] + masks[:1]
    second = masks[1:][::-1] + masks[:1]
    return jnp.concatenate(
        [
            gather_cube(values[..., :half], "seq", first),
            gather_cube(values[..., half:], "seq", second),
        ],
        -1,
    )


def scatter_cube(values, axis, order):
    index = lax.axis_index(axis)
    count = lax.axis_size(axis)
    buffer = values.reshape((2,) * len(order) + (values.shape[0] // count,) + values.shape[1:])
    axes = sorted(order, reverse=True)
    for mask in order:
        place = axes.index(mask)
        bit = (index // mask) % 2
        mine = lax.dynamic_index_in_dim(buffer, bit, place, keepdims=False)
        send = lax.dynamic_index_in_dim(buffer, 1 - bit, place, keepdims=False)
        other = xor_permute(send, axis, mask)
        buffer = (mine.astype(F32) + other.astype(F32)).astype(values.dtype)
        axes.pop(place)
    return buffer


def scatter_seq(values):
    masks = axis_bits("seq")
    half = values.shape[-1] // 2
    first = masks[:1] + masks[1:]
    second = masks[:1] + masks[1:][::-1]
    return jnp.concatenate(
        [
            scatter_cube(values[..., :half], "seq", first),
            scatter_cube(values[..., half:], "seq", second),
        ],
        -1,
    )


def gather_line(values, axis):
    count = lax.axis_size(axis)
    index = lax.axis_index(axis)
    up = [(i, i + 1) for i in range(count - 1)]
    down = [(i + 1, i) for i in range(count - 1)]
    below, above = [], []
    from_below = from_above = values
    for _ in range(count - 1):
        from_below = lax.ppermute(from_below, axis, up)
        from_above = lax.ppermute(from_above, axis, down)
        below.append(from_below)
        above.append(from_above)
    line = jnp.concatenate(below[::-1] + [values] + above, 0)
    rows = values.shape[0]
    return lax.dynamic_slice_in_dim(line, (count - 1 - index) * rows, count * rows, 0)


def total(values, axes):
    for axis in axes:
        for mask in axis_bits(axis):
            values = values + xor_permute(values, axis, mask)
    return values


def swap_blocks(values, axis):
    return lax.all_to_all(values, axis, split_axis=0, concat_axis=0, tiled=True)


def gather_rows(values, axis):
    return lax.all_gather(values, axis, axis=0, tiled=True)


def scatter_rows(values, axis):
    return lax.psum_scatter(values, axis, scatter_dimension=0, tiled=True)


def inv_rms(values):
    return lax.rsqrt(jnp.mean(values * values, -1, keepdims=True) + epsilon)


def norm_back(normed_hat, inverse, grad_hat):
    return inverse * (grad_hat - normed_hat * jnp.mean(normed_hat * grad_hat, -1, keepdims=True))


def dot(left, right):
    return jnp.dot(left, right, preferred_element_type=F32)


def dot_nt(left, right):
    return lax.dot_general(left, right, (((1,), (1,)), ((), ())), preferred_element_type=F32)


def dot_tn(left, right):
    return lax.dot_general(left, right, (((0,), (0,)), ((), ())), preferred_element_type=F32)


def rope_tables(positions, head_dim, heads):
    pair_total = head_dim // 2
    frame_pairs = pair_total // 4
    height_pairs = (pair_total - frame_pairs) // 2
    width_pairs = pair_total - frame_pairs - height_pairs
    frequency = np.zeros((3, pair_total), np.float32)
    start = 0
    for axis_id, pair_count in enumerate((frame_pairs, height_pairs, width_pairs)):
        exponent = -np.arange(pair_count, dtype=np.float32) / np.float32(pair_count)
        frequency[axis_id, start : start + pair_count] = np.float32(rope_base) ** exponent
        start += pair_count
    frequency = jnp.asarray(np.repeat(frequency, 2, axis=1))
    angles = (
        positions[:, 0:1] * frequency[0:1]
        + positions[:, 1:2] * frequency[1:2]
        + positions[:, 2:3] * frequency[2:3]
    )
    sign = jnp.asarray(np.where(np.arange(head_dim) % 2 == 0, -1.0, 1.0).astype(np.float32))
    cosine = jnp.cos(angles)
    sine = jnp.sin(angles) * sign[None, :]
    return (jnp.tile(cosine, (1, heads)), jnp.tile(sine, (1, heads)))


def rotate(values, cosine, sine):
    even = lax.broadcasted_iota(jnp.int32, values.shape, 1) % 2 == 0
    swapped = jnp.where(even, jnp.roll(values, -1, 1), jnp.roll(values, 1, 1))
    return values * cosine + swapped * sine


def clip_index(token_index, clip_lengths):
    bounds = jnp.cumsum(clip_lengths)
    return jnp.sum((token_index[:, None] >= bounds[None, :]).astype(jnp.int32), 1)


def pick_rows(onehot, rows):
    picked = onehot[:, 0:1] * rows[0:1]
    for clip in range(1, rows.shape[0]):
        picked = picked + onehot[:, clip : clip + 1] * rows[clip : clip + 1]
    return picked


def forward_kernel(
    heads,
    head_dim,
    ranges,
    gates,
    q_ref,
    kv_ref,
    tkv_ref,
    meta_ref,
    mixed_ref,
    self_ref,
    cross_ref,
    lse_ref,
    max_ref,
    sum_ref,
    acc_ref,
):
    width = heads * head_dim
    rows = q_ref.shape[0]
    max_ref[...] = jnp.full(max_ref.shape, masked_score, F32)
    sum_ref[...] = jnp.zeros(sum_ref.shape, F32)
    acc_ref[...] = jnp.zeros(acc_ref.shape, F32)
    first = meta_ref[0:1, :]
    last = meta_ref[1:2, :]
    clip = meta_ref[2:3, :]

    def self_step(block, carry):
        start = pl.multiple_of(block * KEY_BLOCK, KEY_BLOCK)
        key_index = start + lax.broadcasted_iota(jnp.int32, (KEY_BLOCK, rows), 0)
        allowed = (key_index >= first) & (key_index < last)
        for h in range(heads):
            lanes = slice(h * head_dim, (h + 1) * head_dim)
            v_lanes = slice(width + h * head_dim, width + (h + 1) * head_dim)
            keys = kv_ref[pl.ds(start, KEY_BLOCK), lanes]
            values = kv_ref[pl.ds(start, KEY_BLOCK), v_lanes]
            scores = jnp.where(allowed, dot_nt(keys, q_ref[:, lanes]), masked_score)
            old_max = max_ref[h : h + 1, :]
            new_max = jnp.maximum(old_max, jnp.max(scores, 0, keepdims=True))
            probs = jnp.exp(scores - new_max)
            factor = jnp.exp(old_max - new_max)
            max_ref[h : h + 1, :] = new_max
            sum_ref[h : h + 1, :] = sum_ref[h : h + 1, :] * factor + jnp.sum(
                probs, 0, keepdims=True
            )
            acc_ref[lanes, :] = acc_ref[lanes, :] * factor + dot_tn(values, probs.astype(BF))
        return carry

    lax.fori_loop(ranges[0], ranges[1], self_step, 0)
    for h in range(heads):
        lanes = slice(h * head_dim, (h + 1) * head_dim)
        sums = sum_ref[h : h + 1, :]
        self_ref[:, lanes] = (acc_ref[lanes, :] / sums).T
        lse_ref[h : h + 1, :] = max_ref[h : h + 1, :] + jnp.log(sums)

    acc_ref[...] = jnp.zeros(acc_ref.shape, F32)

    def cross_step(which, carry):
        start = pl.multiple_of(which * CAP, CAP)
        slot = lax.broadcasted_iota(jnp.int32, (CAP, rows), 0)
        valid = slot < ranges[4 + which]
        here = clip == which
        for h in range(heads):
            lanes = slice(h * head_dim, (h + 1) * head_dim)
            v_lanes = slice(width + h * head_dim, width + (h + 1) * head_dim)
            keys = tkv_ref[pl.ds(start, CAP), lanes]
            values = tkv_ref[pl.ds(start, CAP), v_lanes]
            scores = jnp.where(valid, dot_nt(keys, q_ref[:, lanes]), masked_score)
            top = jnp.max(scores, 0, keepdims=True)
            probs = jnp.exp(scores - top)
            sums = jnp.sum(probs, 0, keepdims=True)
            probs = probs / sums
            acc_ref[lanes, :] = jnp.where(here, dot_tn(values, probs.astype(BF)), acc_ref[lanes, :])
            row = slice(heads + h, heads + h + 1)
            lse_ref[row, :] = jnp.where(here, top + jnp.log(sums), lse_ref[row, :])
        return carry

    lse_ref[heads : 2 * heads, :] = jnp.zeros((heads, rows), F32)
    lax.fori_loop(ranges[2], ranges[3], cross_step, 0)
    for h in range(heads):
        lanes = slice(h * head_dim, (h + 1) * head_dim)
        cross = acc_ref[lanes, :].T
        cross_ref[:, lanes] = cross
        mixed_ref[:, lanes] = (
            self_ref[:, lanes].astype(BF).astype(F32) + gates[h] * cross
        ).astype(BF)


def backward_kernel(
    heads,
    head_dim,
    ranges,
    gates,
    q_ref,
    kv_ref,
    tkv_ref,
    meta_ref,
    dout_ref,
    self_ref,
    lse_ref,
    dq_ref,
    dkv_ref,
    dtkv_ref,
    delta_ref,
    gated_ref,
    acc_ref,
):
    width = heads * head_dim
    rows = q_ref.shape[0]
    dkv_ref[...] = jnp.zeros(dkv_ref.shape, dkv_ref.dtype)
    dtkv_ref[...] = jnp.zeros(dtkv_ref.shape, dtkv_ref.dtype)
    acc_ref[...] = jnp.zeros(acc_ref.shape, F32)
    for h in range(heads):
        lanes = slice(h * head_dim, (h + 1) * head_dim)
        grad = dout_ref[:, lanes].astype(F32)
        delta_ref[h : h + 1, :] = jnp.sum((grad * self_ref[:, lanes]).T, 0, keepdims=True)
        gated_ref[:, lanes] = (grad * gates[h]).astype(BF)
    first = meta_ref[0:1, :]
    last = meta_ref[1:2, :]
    clip = meta_ref[2:3, :]

    def self_step(block, carry):
        start = pl.multiple_of(block * KEY_BLOCK, KEY_BLOCK)
        key_index = start + lax.broadcasted_iota(jnp.int32, (KEY_BLOCK, rows), 0)
        allowed = (key_index >= first) & (key_index < last)
        for h in range(heads):
            lanes = slice(h * head_dim, (h + 1) * head_dim)
            v_lanes = slice(width + h * head_dim, width + (h + 1) * head_dim)
            keys = kv_ref[pl.ds(start, KEY_BLOCK), lanes]
            values = kv_ref[pl.ds(start, KEY_BLOCK), v_lanes]
            queries = q_ref[:, lanes]
            grads = dout_ref[:, lanes]
            scores = dot_nt(keys, queries)
            probs = jnp.where(allowed, jnp.exp(scores - lse_ref[h : h + 1, :]), 0.0)
            prob_grad = dot_nt(values, grads)
            dkv_ref[pl.ds(start, KEY_BLOCK), v_lanes] = dot(probs.astype(BF), grads).astype(
                dkv_ref.dtype
            )
            score_grad = (probs * (prob_grad - delta_ref[h : h + 1, :])).astype(BF)
            dkv_ref[pl.ds(start, KEY_BLOCK), lanes] = dot(score_grad, queries).astype(
                dkv_ref.dtype
            )
            acc_ref[lanes, :] = acc_ref[lanes, :] + dot_tn(keys, score_grad)
        return carry

    lax.fori_loop(ranges[0], ranges[1], self_step, 0)

    def cross_step(which, carry):
        start = pl.multiple_of(which * CAP, CAP)
        slot = lax.broadcasted_iota(jnp.int32, (CAP, rows), 0)
        allowed = (slot < ranges[4 + which]) & (clip == which)
        for h in range(heads):
            lanes = slice(h * head_dim, (h + 1) * head_dim)
            v_lanes = slice(width + h * head_dim, width + (h + 1) * head_dim)
            keys = tkv_ref[pl.ds(start, CAP), lanes]
            values = tkv_ref[pl.ds(start, CAP), v_lanes]
            queries = q_ref[:, lanes]
            grads = gated_ref[:, lanes]
            scores = dot_nt(keys, queries)
            probs = jnp.where(
                allowed, jnp.exp(scores - lse_ref[heads + h : heads + h + 1, :]), 0.0
            )
            prob_grad = dot_nt(values, grads)
            dtkv_ref[pl.ds(start, CAP), v_lanes] = dot(probs.astype(BF), grads).astype(
                dtkv_ref.dtype
            )
            inner = jnp.sum(probs * prob_grad, 0, keepdims=True)
            score_grad = (probs * (prob_grad - inner)).astype(BF)
            dtkv_ref[pl.ds(start, CAP), lanes] = dot(score_grad, queries).astype(dtkv_ref.dtype)
            acc_ref[lanes, :] = acc_ref[lanes, :] + dot_tn(keys, score_grad)
        return carry

    lax.fori_loop(ranges[2], ranges[3], cross_step, 0)
    for h in range(heads):
        lanes = slice(h * head_dim, (h + 1) * head_dim)
        dq_ref[:, lanes] = acc_ref[lanes, :].T * (1.0 / math.sqrt(head_dim))


SMEM = pl.BlockSpec(memory_space=pltpu.SMEM)
WHOLE = pl.BlockSpec(memory_space=pltpu.VMEM)


def attend_forward(ranges, gates, queries, kv, tkv, meta, heads, head_dim):
    rows, width = queries.shape
    lse_rows = -(-2 * heads // 8) * 8
    work = 4 * rows * kv.shape[0] * width // 2
    return pl.pallas_call(
        functools.partial(forward_kernel, heads, head_dim),
        out_shape=(
            jax.ShapeDtypeStruct((rows, width), BF),
            jax.ShapeDtypeStruct((rows, width), F32),
            jax.ShapeDtypeStruct((rows, width), F32),
            jax.ShapeDtypeStruct((lse_rows, rows), F32),
        ),
        in_specs=[SMEM, SMEM] + [WHOLE] * 4,
        out_specs=(WHOLE,) * 4,
        scratch_shapes=[
            pltpu.VMEM((8, rows), F32),
            pltpu.VMEM((8, rows), F32),
            pltpu.VMEM((width, rows), F32),
        ],
        compiler_params=pltpu.CompilerParams(vmem_limit_bytes=VMEM_BYTES),
        cost_estimate=pl.CostEstimate(
            flops=work * 4, bytes_accessed=kv.size * 2, transcendentals=work // (4 * head_dim)
        ),
    )(ranges, gates, queries, kv, tkv, meta)


def attend_backward(ranges, gates, queries, kv, tkv, meta, dout, self_out, lse, heads, head_dim):
    rows, width = queries.shape
    work = 10 * rows * kv.shape[0] * width // 2
    return pl.pallas_call(
        functools.partial(backward_kernel, heads, head_dim),
        out_shape=(
            jax.ShapeDtypeStruct((rows, width), F32),
            jax.ShapeDtypeStruct(kv.shape, BF),
            jax.ShapeDtypeStruct(tkv.shape, BF),
        ),
        in_specs=[SMEM, SMEM] + [WHOLE] * 7,
        out_specs=(WHOLE,) * 3,
        scratch_shapes=[
            pltpu.VMEM((8, rows), F32),
            pltpu.VMEM((rows, width), BF),
            pltpu.VMEM((width, rows), F32),
        ],
        compiler_params=pltpu.CompilerParams(vmem_limit_bytes=VMEM_BYTES),
        cost_estimate=pl.CostEstimate(
            flops=work * 4, bytes_accessed=kv.size * 4, transcendentals=work // (10 * head_dim)
        ),
    )(ranges, gates, queries, kv, tkv, meta, dout, self_out, lse)


def body(
    video,
    conditioning,
    captions,
    clip_lengths,
    cap_lengths,
    positions,
    ada_weight,
    ada_bias,
    query_weight,
    key_weight,
    value_weight,
    out_weight,
    text_key_weight,
    text_value_weight,
    gate_weight,
    up_weight,
    down_weight,
    attn_gain,
    query_gain,
    key_gain,
    text_key_gain,
    attn_out_gain,
    ffn_gain,
    ffn_out_gain,
    cross_gate,
    cotangent,
):
    num_sub = lax.axis_size("sub")
    num_seq = lax.axis_size("seq")
    rows, width = video.shape
    heads_total = cross_gate.shape[0]
    head_dim = width // heads_total
    heads = heads_total // num_sub
    cols = width // num_sub
    device = lax.axis_index(BOTH)
    seq = lax.axis_index("seq")
    sub = lax.axis_index("sub")
    group = rows * num_sub
    tokens = group * num_seq
    clips = clip_lengths.shape[0]
    clip_range = jnp.arange(clips, dtype=jnp.int32)
    score_scale = 1.0 / math.sqrt(head_dim)

    ends = jnp.cumsum(clip_lengths)
    starts = ends - clip_lengths
    group_clip = clip_index(seq * group + jnp.arange(group, dtype=jnp.int32), clip_lengths)
    group_hot_bool = group_clip[:, None] == clip_range[None, :]
    group_hot = group_hot_bool.astype(F32)
    own_hot = lax.dynamic_slice_in_dim(group_hot, sub * rows, rows, 0)
    first = jnp.sum(jnp.where(group_hot_bool, starts[None, :], 0), 1)
    last = jnp.sum(jnp.where(group_hot_bool, ends[None, :], 0), 1)
    meta = jnp.concatenate(
        [first[None], last[None], group_clip[None], jnp.zeros((5, group), jnp.int32)], 0
    )
    ranges = jnp.concatenate(
        [
            jnp.stack(
                [
                    first[0] // KEY_BLOCK,
                    (last[-1] + KEY_BLOCK - 1) // KEY_BLOCK,
                    group_clip[0],
                    group_clip[-1] + 1,
                ]
            ),
            cap_lengths,
        ]
    ).astype(jnp.int32)
    gate_tanh = jnp.tanh(cross_gate.astype(F32))
    gates = lax.dynamic_slice_in_dim(gate_tanh, sub * heads, heads, 0)

    cond_float = conditioning.astype(F32)
    cond_act = jax.nn.silu(cond_float).astype(BF)
    cond_rows = ada_weight.shape[0]
    cond_slice = lax.dynamic_slice_in_dim(cond_act, device * cond_rows, cond_rows, 1)
    mod_part = dot(cond_slice, ada_weight)
    mod_part = mod_part + lax.dynamic_update_slice_in_dim(
        jnp.zeros((1, 4 * width), F32), ada_bias.astype(F32)[None], device * ada_bias.shape[0], 1
    )
    mod_part = mod_part.reshape(clips, 4, width)
    gain_rows = attn_gain.shape[0]

    def spread(gains):
        stacked = jnp.stack(gains).astype(F32)
        return lax.dynamic_update_slice_in_dim(
            jnp.zeros((len(gains), width), F32), stacked, device * gain_rows, 1
        )

    early = total(
        jnp.concatenate([mod_part[:, 0], spread([attn_gain, query_gain, key_gain])], 0),
        ("sub", "seq"),
    )
    late = total(
        jnp.concatenate(
            [
                mod_part[:, 1],
                mod_part[:, 2],
                mod_part[:, 3],
                spread([text_key_gain, attn_out_gain, ffn_gain, ffn_out_gain]),
            ],
            0,
        ),
        ("sub", "seq"),
    )
    scale_rows = early[:clips]
    attn_gain_f = early[clips : clips + 1]
    query_gain_f = lax.dynamic_slice_in_dim(early[clips + 1 : clips + 2], sub * cols, cols, 1)
    key_gain_f = lax.dynamic_slice_in_dim(early[clips + 2 : clips + 3], sub * cols, cols, 1)
    attn_gate = pick_rows(own_hot, late[:clips])
    ffn_scale = pick_rows(own_hot, late[clips : 2 * clips])
    ffn_gate = pick_rows(own_hot, late[2 * clips : 3 * clips])
    text_key_gain_f = lax.dynamic_slice_in_dim(
        late[3 * clips : 3 * clips + 1], sub * cols, cols, 1
    )
    attn_out_f = late[3 * clips + 1 : 3 * clips + 2]
    ffn_gain_f = late[3 * clips + 2 : 3 * clips + 3]
    ffn_out_f = late[3 * clips + 3 : 3 * clips + 4]

    packed = jnp.concatenate(
        [video, jnp.pad(positions.astype(BF), ((0, 0), (0, 128 - positions.shape[1])))], 1
    )
    packed = gather_line(packed, "sub")
    video_group = packed[:, :width].astype(F32)
    group_pos = packed[:, width : width + 3].astype(F32)
    w_rows = query_weight.shape[0]
    qkv_weight = jnp.concatenate(
        [w.reshape(w_rows, num_sub, cols) for w in (query_weight, key_weight, value_weight)], 2
    ).transpose(1, 0, 2)
    qkv_weight = swap_blocks(qkv_weight, "sub").reshape(num_sub * w_rows, 3 * cols)
    qkv_weight = gather_rows(qkv_weight, "seq")

    cap_shard = captions.shape[0]
    cap_total = cap_shard * num_sub
    t_rows = text_key_weight.shape[0]
    cap_cols = lax.dynamic_slice_in_dim(
        captions, seq * num_sub * t_rows, num_sub * t_rows, 1
    ).reshape(cap_shard, num_sub, t_rows)
    cap_cols = swap_blocks(cap_cols.transpose(1, 0, 2), "sub").reshape(cap_total, t_rows)
    text_weight = jnp.concatenate(
        [
            text_key_weight.reshape(t_rows, num_sub, 1, cols),
            text_value_weight.reshape(t_rows, num_sub, 1, cols),
        ],
        2,
    ).reshape(t_rows, 2 * width)
    text_part = dot(cap_cols, text_weight).astype(BF)
    text_part = scatter_rows(text_part, "seq")
    slots = cap_total // num_seq
    text_part = text_part.reshape(slots, num_sub, 2 * cols).transpose(1, 0, 2)
    text_pre = jnp.sum(swap_blocks(text_part, "sub").astype(F32), 0)
    text_key_pre = text_pre[:, :cols]
    text_square = total(jnp.sum(text_key_pre * text_key_pre, 1)[None], ("sub",))
    text_inv = lax.rsqrt(text_square / width + epsilon).reshape(slots, 1)
    text_hat = text_key_pre * text_inv
    tkv = jnp.concatenate(
        [(text_hat * text_key_gain_f).astype(BF), text_pre[:, cols:].astype(BF)], 1
    )
    tkv = gather_rows(tkv, "seq")

    out_full = gather_rows(out_weight, BOTH)
    units = gate_weight.shape[1] // num_seq
    gate_up = jnp.concatenate(
        [w.reshape(w_rows, num_seq, units) for w in (gate_weight, up_weight)], 2
    ).transpose(1, 0, 2)
    gate_up = swap_blocks(gate_up, "seq").reshape(num_seq * w_rows, 2 * units)
    gate_up = gather_rows(gate_up, "sub")
    gate_up = (
        gate_up.reshape(num_sub, num_seq, w_rows, 2 * units)
        .transpose(1, 0, 2, 3)
        .reshape(width, 2 * units)
    )
    down_block = gather_rows(down_weight, "sub")

    video_inv = inv_rms(video_group)
    video_hat = video_group * video_inv
    attn_scale1 = 1.0 + pick_rows(group_hot, scale_rows)
    normed = (video_hat * (attn_gain_f * attn_scale1)).astype(BF)
    qkv_pre = dot(normed, qkv_weight)
    query_pre = qkv_pre[:, :cols]
    key_pre = qkv_pre[:, cols : 2 * cols]
    squares = total(
        jnp.stack([jnp.sum(query_pre * query_pre, 1), jnp.sum(key_pre * key_pre, 1)]), ("sub",)
    )
    inverse = lax.rsqrt(squares / width + epsilon)
    query_inv = inverse[0].reshape(group, 1)
    key_inv = inverse[1].reshape(group, 1)
    query_hat = query_pre * query_inv
    key_hat = key_pre * key_inv
    cosine, sine = rope_tables(group_pos, head_dim, heads)
    queries = (rotate(query_hat * query_gain_f, cosine, sine).astype(BF) * score_scale).astype(BF)
    keys = rotate(key_hat * key_gain_f, cosine, sine).astype(BF)
    kv = gather_rows(jnp.concatenate([keys, qkv_pre[:, 2 * cols :].astype(BF)], 1), "seq")

    mixed_heads, self_out, cross_out, lse = attend_forward(
        ranges, gates, queries, kv, tkv, meta, heads, head_dim
    )
    mixed = (
        swap_blocks(mixed_heads.reshape(num_sub, rows, cols), "sub")
        .transpose(1, 0, 2)
        .reshape(rows, width)
    )

    video_own = video.astype(F32)
    projected = dot(mixed, out_full)
    proj_inv = inv_rms(projected)
    proj_hat = projected * proj_inv
    attn_tanh = jnp.tanh(attn_gate)
    hidden_state = video_own + attn_tanh * proj_hat * attn_out_f
    hidden_inv = inv_rms(hidden_state)
    hidden_hat = hidden_state * hidden_inv
    ffn_mult = ffn_gain_f * (1.0 + ffn_scale)
    ffn_in = gather_seq((hidden_hat * ffn_mult).astype(BF))
    gate_up_pre = dot(ffn_in, gate_up)
    gate_pre = gate_up_pre[:, :units]
    up_pre = gate_up_pre[:, units:]
    gate_sig = jax.nn.sigmoid(gate_pre)
    gate_act = gate_pre * gate_sig
    activated = (gate_act * up_pre).astype(BF)
    down_out = scatter_seq(dot(activated, down_block).astype(BF)).astype(F32)
    down_inv = inv_rms(down_out)
    down_hat = down_out * down_inv
    ffn_tanh = jnp.tanh(ffn_gate)
    block_out = (hidden_state + ffn_tanh * down_hat * ffn_out_f).astype(BF)

    grad_out = cotangent.astype(F32)
    ffn_gate_grad = grad_out * down_hat * ffn_out_f * (1.0 - ffn_tanh * ffn_tanh)
    ffn_out_gain_part = jnp.sum(grad_out * ffn_tanh * down_hat, 0)
    down_grad = gather_seq(
        norm_back(down_hat, down_inv, grad_out * ffn_tanh * ffn_out_f).astype(BF)
    )
    down_weight_term = dot_tn(activated, down_grad).astype(BF)
    act_grad = dot_nt(down_grad, down_block)
    gate_grad = (act_grad * up_pre * gate_sig * (1.0 + gate_pre * (1.0 - gate_sig))).astype(BF)
    up_grad = (act_grad * gate_act).astype(BF)
    gate_up_grad = jnp.concatenate([gate_grad, up_grad], 1)
    ffn_in_grad = scatter_seq(dot_nt(gate_up_grad, gate_up).astype(BF)).astype(F32)
    gate_up_term = dot_tn(ffn_in, gate_up_grad).astype(BF)
    down_weight_grad = scatter_rows(down_weight_term, "sub").astype(F32)
    gate_up_term = (
        gate_up_term.reshape(num_seq, num_sub, w_rows, 2 * units)
        .transpose(1, 0, 2, 3)
        .reshape(width, 2 * units)
    )
    gate_up_term = scatter_rows(gate_up_term, "sub").reshape(num_seq, w_rows, 2 * units)
    gate_up_term = swap_blocks(gate_up_term, "seq").transpose(1, 0, 2).astype(F32)
    gate_weight_grad = gate_up_term[:, :, :units].reshape(w_rows, num_seq * units)
    up_weight_grad = gate_up_term[:, :, units:].reshape(w_rows, num_seq * units)

    ffn_gain_part = jnp.sum(ffn_in_grad * hidden_hat * (1.0 + ffn_scale), 0)
    ffn_scale_grad = ffn_in_grad * hidden_hat * ffn_gain_f
    hidden_grad = grad_out + norm_back(hidden_hat, hidden_inv, ffn_in_grad * ffn_mult)
    attn_gate_grad = hidden_grad * proj_hat * attn_out_f * (1.0 - attn_tanh * attn_tanh)
    attn_out_gain_part = jnp.sum(hidden_grad * attn_tanh * proj_hat, 0)
    proj_grad = norm_back(proj_hat, proj_inv, hidden_grad * attn_tanh * attn_out_f).astype(BF)
    mixed_grad = dot_nt(proj_grad, out_full).astype(BF)
    out_weight_term = dot_tn(mixed, proj_grad).astype(BF)
    out_weight_grad = scatter_rows(scatter_rows(out_weight_term, "seq"), "sub").astype(F32)

    dout = swap_blocks(
        mixed_grad.reshape(rows, num_sub, cols).transpose(1, 0, 2), "sub"
    ).reshape(group, cols)
    cross_gate_part = jnp.sum(
        (dout.astype(F32) * cross_out).reshape(group, heads, head_dim), (0, 2)
    ) * (1.0 - gates * gates)
    query_rot_grad, dkv, dtkv = attend_backward(
        ranges, gates, queries, kv, tkv, meta, dout, self_out, lse, heads, head_dim
    )
    query_rot_grad = query_rot_grad.astype(BF).astype(F32)
    dkv = scatter_seq(dkv)
    key_rot_grad = dkv[:, :cols].astype(F32)
    value_grad = dkv[:, cols:]
    query_norm_grad = rotate(query_rot_grad, cosine, -sine)
    query_gain_part = jnp.sum(query_norm_grad * query_hat, 0)
    query_hat_grad = query_norm_grad * query_gain_f
    key_norm_grad = rotate(key_rot_grad, cosine, -sine)
    key_gain_part = jnp.sum(key_norm_grad * key_hat, 0)
    key_hat_grad = key_norm_grad * key_gain_f
    inner = total(
        jnp.stack([jnp.sum(query_hat * query_hat_grad, 1), jnp.sum(key_hat * key_hat_grad, 1)]),
        ("sub",),
    ) / width
    query_pre_grad = query_inv * (query_hat_grad - query_hat * inner[0].reshape(group, 1))
    key_pre_grad = key_inv * (key_hat_grad - key_hat * inner[1].reshape(group, 1))
    qkv_grad = jnp.concatenate([query_pre_grad.astype(BF), key_pre_grad.astype(BF), value_grad], 1)
    qkv_term = dot_tn(normed, qkv_grad).astype(BF)
    normed_part = dot_nt(qkv_grad, qkv_weight)
    normed_grad = scatter_rows(normed_part.astype(BF), "sub").astype(F32)
    qkv_term = scatter_seq(qkv_term).reshape(num_sub, w_rows, 3 * cols)
    qkv_term = swap_blocks(qkv_term, "sub").transpose(1, 0, 2).astype(F32)
    query_weight_grad, key_weight_grad, value_weight_grad = (
        qkv_term[:, :, i * cols : (i + 1) * cols].reshape(w_rows, width) for i in range(3)
    )

    own_hat = lax.dynamic_slice_in_dim(video_hat, sub * rows, rows, 0)
    own_inv = lax.dynamic_slice_in_dim(video_inv, sub * rows, rows, 0)
    own_scale1 = lax.dynamic_slice_in_dim(attn_scale1, sub * rows, rows, 0)
    video_grad = hidden_grad + norm_back(own_hat, own_inv, normed_grad * (attn_gain_f * own_scale1))
    hat_grad = normed_part * video_hat
    attn_gain_part = jnp.sum(hat_grad * attn_scale1, 0)
    scale_part = dot_tn(group_hot.astype(BF), (hat_grad * attn_gain_f).astype(BF))

    dtkv = scatter_rows(dtkv, "seq")
    text_key_low = dtkv[:, :cols].astype(F32)
    text_key_gain_part = jnp.sum(text_key_low * text_hat, 0)
    text_hat_grad = text_key_low * text_key_gain_f
    text_inner = total(jnp.sum(text_hat * text_hat_grad, 1)[None], ("sub",)) / width
    text_pre_grad = text_inv * (text_hat_grad - text_hat * text_inner.reshape(slots, 1))
    text_grad = jnp.concatenate([text_pre_grad.astype(BF), dtkv[:, cols:]], 1)
    text_grad = gather_rows(text_grad, BOTH)
    text_grad = (
        text_grad.reshape(num_seq, num_sub, slots, 2 * cols)
        .transpose(0, 2, 1, 3)
        .reshape(cap_total, 2 * width)
    )
    text_term = dot_tn(cap_cols, text_grad).reshape(t_rows, num_sub, 2, cols)
    text_key_weight_grad = text_term[:, :, 0].reshape(t_rows, width)
    text_value_weight_grad = text_term[:, :, 1].reshape(t_rows, width)
    caption_cols = dot_nt(text_grad, text_weight).astype(BF).reshape(num_sub, cap_shard, t_rows)
    caption_cols = (
        swap_blocks(caption_cols, "sub").transpose(1, 0, 2).reshape(cap_shard, num_sub * t_rows)
    )
    caption_grad = (
        gather_rows(caption_cols[None], "seq")
        .transpose(1, 0, 2)
        .reshape(cap_shard, captions.shape[1])
        .astype(F32)
    )

    def clip_sums(values):
        return dot_tn(own_hot.astype(BF), values.astype(BF))

    def place(part):
        return lax.dynamic_update_slice_in_dim(
            jnp.zeros((1, width), F32), part.reshape(1, -1), sub * cols, 1
        )

    gate_row = lax.dynamic_update_slice_in_dim(
        jnp.zeros((1, width), F32), cross_gate_part.reshape(1, -1), sub * heads, 1
    )
    late_sum = total(
        jnp.concatenate(
            [
                clip_sums(attn_gate_grad),
                clip_sums(ffn_scale_grad),
                clip_sums(ffn_gate_grad),
                attn_out_gain_part[None],
                ffn_gain_part[None],
                ffn_out_gain_part[None],
                gate_row,
            ],
            0,
        ),
        ("sub", "seq"),
    )
    early_sum = total(
        jnp.concatenate(
            [
                scale_part,
                attn_gain_part[None],
                place(query_gain_part),
                place(key_gain_part),
                place(text_key_gain_part),
            ],
            0,
        ),
        ("sub", "seq"),
    )

    def own_gain(row):
        return lax.dynamic_slice_in_dim(row, device * gain_rows, gain_rows, 0)

    mod_low = jnp.concatenate(
        [
            early_sum[:clips],
            late_sum[:clips],
            late_sum[clips : 2 * clips],
            late_sum[2 * clips : 3 * clips],
        ],
        1,
    ).astype(BF)
    bias_rows = ada_bias.shape[0]
    ada_bias_grad = jnp.sum(
        lax.dynamic_slice_in_dim(mod_low.astype(F32), device * bias_rows, bias_rows, 1), 0
    )
    ada_weight_grad = dot_tn(cond_slice, mod_low)
    cond_part = lax.dynamic_update_slice_in_dim(
        jnp.zeros(conditioning.shape, F32), dot_nt(mod_low, ada_weight), device * cond_rows, 1
    )
    cond_sig = jax.nn.sigmoid(cond_float)
    cond_grad = (
        total(cond_part, ("sub", "seq")) * cond_sig * (1.0 + cond_float * (1.0 - cond_sig))
    )
    return (
        block_out,
        video_grad,
        caption_grad,
        cond_grad,
        ada_weight_grad,
        ada_bias_grad,
        query_weight_grad,
        key_weight_grad,
        value_weight_grad,
        out_weight_grad,
        text_key_weight_grad,
        text_value_weight_grad,
        gate_weight_grad,
        up_weight_grad,
        down_weight_grad,
        own_gain(early_sum[clips]),
        own_gain(early_sum[clips + 1]),
        own_gain(early_sum[clips + 2]),
        own_gain(early_sum[clips + 3]),
        own_gain(late_sum[3 * clips]),
        own_gain(late_sum[3 * clips + 1]),
        own_gain(late_sum[3 * clips + 2]),
        late_sum[3 * clips + 3, :heads_total],
    )


def solution(mesh):
    matrix = P(BOTH, None)
    vector = P(BOTH)
    return jax.shard_map(
        body,
        mesh=mesh,
        in_specs=(matrix, P(), P("sub", None), P(), P(), matrix, matrix, vector)
        + (matrix,) * 9
        + (vector,) * 7
        + (P(), matrix),
        out_specs=(matrix, matrix, P("sub", None), P(), matrix, vector)
        + (matrix,) * 9
        + (vector,) * 7
        + (P(),),
        check_vma=False,
    )
```

time: 3370 us -> 949 us (0.28)
  waiting for transfers between devices: 2460 us -> 500 us
  matrix products: 440 us -> 73.2 us
  blocking collectives: 153 us -> 13.3 us
  starting transfers between devices: 18 us -> 108 us
  other arithmetic: 117 us -> 61.2 us
  Pallas kernels: 0 us -> 52.3 us
  local copies, waits for them, and re-layouts: 155 us -> 116 us
    reduce_scatter x12 -> x7, waiting for transfers between devices: 1710 us -> 81.1 us  [scatter_rows(): return lax.psum_scatter(values, axis, scatter_dimension=0, tiled=True)]
    all_gather x15 -> x8, waiting for transfers between devices: 657 us -> 175 us  [gather_rows(): return lax.all_gather(values, axis, axis=0, tiled=True)]
    dot_general x65 -> x22, matrix products: 421 us -> 73.2 us  [the longest x10 30.7 us: dot_tn(): lax.dot_general(left, right, (((0,), (0,)), ((), ())), preferred_element_...]
    ppermute x0 -> x75, waiting for transfers between devices: none -> 169 us  [the longest x69 168 us: xor_permute(): return lax.ppermute(values, axis, [(i, i ^ mask) for i in range(count)])]
    unnamed x29 -> x15, waiting for transfers between devices: 74.8 us -> 0.76 us
    ppermute x0 -> x75, starting transfers between devices: none -> 70.8 us  [the longest x69 58.5 us: xor_permute(): return lax.ppermute(values, axis, [(i, i ^ mask) for i in range(count)])]
    all_to_all x4 -> x1, blocking collectives: 66.8 us -> 13.3 us  [swap_blocks(): return lax.all_to_all(values, axis, split_axis=0, concat_axis=0, tiled=True)]
    pallas_call x0 -> x2, Pallas kernels: none -> 52.3 us  [the longest x1 30.2 us: attend_forward(): pl.pallas_call(functools.partial(forward_kernel, heads, head_dim), out_sh...]
  transfers between devices with their start and end apart: 32 -> 98, of which waited for: 26 -> 66; matrix products, arithmetic and copies ran while one was open for 18% -> 22% of each run, Pallas kernels for 0% -> 3%
where the time goes in v1:
time: 949 us; the launch traced here: 945 us
  waiting for transfers between devices  500 us (53%)
  local copies, waits for them, and re-layouts  116 us (12%)
  starting transfers between devices  108 us (11%)
  matrix products  73.2 us (8%)
  other arithmetic  61.2 us (6%)
  Pallas kernels  52.3 us (6%)
  between operations  21.4 us (2%)
  blocking collectives  13.3 us (1%)
    all_gather x8, waiting for transfers between devices, gather_rows(): return lax.all_gather(values, axis, axis=0, tiled=True)  175 us
    ppermute x69, waiting for transfers between devices, xor_permute(): return lax.ppermute(values, axis, [(i, i ^ mask) for i in range(count)])  168 us
    reduce_scatter x7, waiting for transfers between devices, scatter_rows(): return lax.psum_scatter(values, axis, scatter_dimension=0, tiled=True)  81.1 us
    all_to_all x8, waiting for transfers between devices, swap_blocks(): return lax.all_to_all(values, axis, split_axis=0, concat_axis=0, tiled=True)  73.3 us
    ppermute x69, starting transfers between devices, xor_permute(): return lax.ppermute(values, axis, [(i, i ^ mask) for i in range(count)])  58.5 us
    all_to_all x8, starting transfers between devices, swap_blocks(): return lax.all_to_all(values, axis, split_axis=0, concat_axis=0, tiled=True)  35.7 us
    dot_general x10, matrix products, dot_tn(): lax.dot_general(left, right, (((0,), (0,)), ((), ())), preferred_element_...  30.7 us
    pallas_call x1, Pallas kernels, attend_forward(): pl.pallas_call(functools.partial(forward_kernel, heads, head_dim), out_sh...  30.2 us
  transfers between devices with their start and end apart: 98, of which 66 were waited for; matrix products, arithmetic and copies ran while one was open for 22% of the time, Pallas kernels for 3%

profile of v1, /device:TPU:0, one launch (start us, length us, event | category | flops | bytes accessed | tf_op | source)
XLA Modules:
  0.0 944.7 jit_solution(12116583448873401877)
XLA Ops:
  9.8 6.3 all-to-all-start.1
  17.7 8.8 all-to-all-done.1
  26.5 5.4 convolution_convert_fusion
  38.1 5.5 all-to-all-start
  44.2 13.7 %all-to-all-done = bf16[4,48,1152]{2,1,0:T(8,128)(2,1)S(1)} async-done(((bf16[4,48,1152]{2,1,0:T(8,128)(2,1)}), bf16[4,48,1152]{2,1,0:T(8,128)(2,1)S(1)}, u32[]{:S(2)}, u32[]{:S(2)}) %all-to-all-start) | async-done | bytes 442400 | tf_op jit(solution)/shard_map/all_to_all | solution.py:121
  67.7 5.1 collective-permute-done.1
  87.6 5.3 collective-permute-start.7
  98.0 5.7 reduce-scatter.8.cloned.1.call-done
  105.9 5.0 all-to-all-start.2
  118.7 16.8 %all-to-all-done.2 = bf16[4,160,768]{2,1,0:T(8,128)(2,1)S(1)} async-done(((bf16[4,160,768]{2,1,0:T(8,128)(2,1)}), bf16[4,160,768]{2,1,0:T(8,128)(2,1)S(1)}, u32[]{:S(2)}, u32[]{:S(2)}) %all-to-all-start.2) | async-done | bytes 983072 | tf_op jit(solution)/shard_map/all_to_all | solution.py:121
  145.4 5.9 fusion.122
  184.8 34.2 %all-gather.11.cloned.1.call-done.kv_ref = bf16[4096,768]{1,0:T(8,128)(2,1)} async-done(((bf16[512,768]{1,0:T(8,128)(2,1)}), bf16[4096,768]{1,0:T(8,128)(2,1)}) %all-gather.11.cloned.1.call-update) | async-done | bytes 6291472 | tf_op jit(solution)/shard_map/all_gather | solution.py:125
  219.0 30.2 %shard_map.443 = (bf16[512,384]{1,0:T(8,128)(2,1)}, f32[512,384]{1,0:T(8,128)}, f32[512,384]{1,0:T(8,128)}, f32[16,512]{1,0:T(8,128)}) custom-call(s32[9]{0:T(128)} %concatenate.94.ranges, f32[6]{0:T(128)} %dynamic_slice.227.gates, bf16[512,384]{1,0:T(8,128)(2,1)} %fusion.72.q_ref, bf16[4096,768]{1,0:T(8,128)(2,1)} %all-gather.11.cloned.1.call-done.kv_ref, ...), custom_call_target="tpu_custom_call" | custom-call | flops 6442450944 | bytes 6291456 | tf_op jit(solution)/shard_map/pallas_call | solution.py:378
  251.1 4.6 all-to-all-start.3
  256.5 32.7 %all-gather.15.cloned.1.call-done = bf16[1536,1536]{1,0:T(8,128)(2,1)} async-done(((bf16[48,1536]{1,0:T(8,128)(2,1)}), bf16[1536,1536]{1,0:T(8,128)(2,1)}) %all-gather.15.cloned.1.call-update) | async-done | bytes 4718608 | tf_op jit(solution)/shard_map/all_gather | solution.py:125
  294.2 5.5 collective-permute-start.20
  299.7 5.3 collective-permute-done.20
  308.6 8.3 collective-permute-done.21
  319.6 37.4 %all-gather.17.cloned.1.call-done = bf16[1536,1024]{1,0:T(8,128)(2,1)} async-done(((bf16[384,1024]{1,0:T(8,128)(2,1)}), bf16[1536,1024]{1,0:T(8,128)(2,1)}) %all-gather.17.cloned.1.call-update) | async-done | bytes 3145744 | tf_op jit(solution)/shard_map/all_gather | solution.py:125
  369.9 24.6 %all-gather.19.cloned.1.call-done = bf16[512,1536]{1,0:T(8,128)(2,1)} async-done(((bf16[128,1536]{1,0:T(8,128)(2,1)}), bf16[512,1536]{1,0:T(8,128)(2,1)}) %all-gather.19.cloned.1.call-update) | async-done | bytes 1572880 | tf_op jit(solution)/shard_map/all_gather | solution.py:125
  409.0 6.3 collective-permute-done.27
  439.0 4.8 collective-permute-done.33
  463.6 8.1 collective-permute-done.39
  484.2 13.3 %all_to_all.45 = bf16[4,128,384]{2,1,0:T(8,128)(2,1)} all-to-all(bf16[4,128,384]{2,1,0:T(8,128)(2,1)S(1)} %bitcast.525), channel_id=1, replica_groups=mesh['seq'=8,'sub'=4] {'sub'}, dimensions={0} | all-to-all | bytes 786432 | tf_op jit(solution)/shard_map/all_to_all | solution.py:121
  497.5 22.1 %shard_map.444 = (f32[512,384]{1,0:T(8,128)}, bf16[4096,768]{1,0:T(8,128)(2,1)}, bf16[1280,768]{1,0:T(8,128)(2,1)}) custom-call(s32[9]{0:T(128)} %concatenate.94.ranges, f32[6]{0:T(128)} %dynamic_slice.227.gates, bf16[512,384]{1,0:T(8,128)(2,1)} %fusion.72.q_ref, bf16[4096,768]{1,0:T(8,128)(2,1)} %all-gather.11.cloned.1.call-done.kv_ref, ...), custom_call_target="tpu_custom_call" | custom-call | flops 16106127360 | bytes 12582912 | tf_op jit(solution)/shard_map/pallas_call | solution.py:403
  519.6 5.2 convolution_convert_fusion.6
  528.6 46.7 %reduce-scatter.12.cloned.1.call-done = bf16[160,768]{1,0:T(8,128)(2,1)} async-done(((bf16[1280,768]{1,0:T(8,128)(2,1)}), bf16[160,768]{1,0:T(8,128)(2,1)}) %reduce-scatter.12.cloned.1.call-update) | async-done | bytes 245776 | tf_op jit(solution)/shard_map/reduce_scatter | solution.py:129
  588.9 5.4 convolution_convert_fusion.4
  604.6 6.7 collective-permute-done.59
  611.8 8.2 collective-permute-done.60
  623.3 4.2 collective-permute-done.62
  637.4 23.0 %collective-permute-done.45 = bf16[2,512,384]{2,1,0:T(8,128)(2,1)S(1)} collective-permute-done((bf16[2,512,384]{2,1,0:T(8,128)(2,1)S(1)}, bf16[2,512,384]{2,1,0:T(8,128)(2,1)S(1)}, u32[]{:S(2)}, u32[]{:S(2)}) %collective-permute-start.45) | collective-permute-done | bytes 786464 | tf_op jit(solution)/shard_map/ppermute | solution.py:25
  666.5 7.3 collective-permute-done.46
  679.9 4.4 collective-permute-done.48
  684.8 6.3 multiply_reduce_fusion
  698.3 4.4 convolution_convert_fusion.2
  736.5 36.7 %all-gather.21.cloned.1.call-done = bf16[5120,768]{1,0:T(8,128)(2,1)} async-done(((bf16[160,768]{1,0:T(8,128)(2,1)}), bf16[5120,768]{1,0:T(8,128)(2,1)}) %all-gather.21.cloned.1.call-update) | async-done | bytes 7864336 | tf_op jit(solution)/shard_map/all_gather | solution.py:125
  773.2 12.5 %copy.414 = bf16[8,4,160,768]{3,1,2,0:T(4,128)(2,1)} copy(bf16[8,4,160,768]{3,2,1,0:T(8,128)(2,1)} %bitcast.492) | data formatting | bytes 15728640 | tf_op jit(solution)/shard_map/reshape | solution.py:734
  785.6 8.4 copy.452
  794.0 6.3 convolution_convert_fusion.7
  807.3 17.8 %all-to-all-done.6 = bf16[4,320,128]{2,1,0:T(8,128)(2,1)S(1)} async-done(((bf16[4,320,128]{2,1,0:T(8,128)(2,1)}), bf16[4,320,128]{2,1,0:T(8,128)(2,1)S(1)}, u32[]{:S(2)}, u32[]{:S(2)}) %all-to-all-start.6) | async-done | bytes 327712 | tf_op jit(solution)/shard_map/all_to_all | solution.py:121
  828.5 5.2 collective-permute-done.74
  855.7 10.3 %all-to-all-done.8 = bf16[8,48,1024]{2,1,0:T(8,128)(2,1)S(1)} async-done(((bf16[8,48,1024]{2,1,0:T(8,128)(2,1)}), bf16[8,48,1024]{2,1,0:T(8,128)(2,1)S(1)}, u32[]{:S(2)}, u32[]{:S(2)}) %all-to-all-start.8) | async-done | bytes 786464 | tf_op jit(solution)/shard_map/all_to_all | solution.py:121
  868.2 9.9 %reduce-scatter.10.cloned.1.call-done = bf16[128,1536]{1,0:T(8,128)(2,1)} async-done(((bf16[512,1536]{1,0:T(8,128)(2,1)}), bf16[128,1536]{1,0:T(8,128)(2,1)}) %reduce-scatter.10.cloned.1.call-update) | async-done | bytes 393232 | tf_op jit(solution)/shard_map/reduce_scatter | solution.py:129
  882.4 18.8 %reduce-scatter.16.cloned.1.call-done = bf16[48,1536]{1,0:T(8,128)(2,1)} async-done(((bf16[192,1536]{1,0:T(8,128)(2,1)}), bf16[48,1536]{1,0:T(8,128)(2,1)}) %reduce-scatter.16.cloned.1.call-update) | async-done | bytes 147472 | tf_op jit(solution)/shard_map/reduce_scatter | solution.py:129
  902.9 10.8 %copy.422 = bf16[3072,1280]{1,0:T(8,128)(2,1)} copy(bf16[3072,1280]{0,1:T(8,128)(2,1)} %bitcast.479) | data formatting | bytes 15728640 | tf_op jit(solution)/shard_map/dot_general | solution.py:149
  913.7 5.9 fusion.149
  922.6 9.8 %all-gather.23.cloned.1.call-done = bf16[8,320,512]{2,1,0:T(8,128)(2,1)} async-done(((bf16[1,320,512]{2,1,0:T(8,128)(2,1)}), bf16[8,320,512]{2,1,0:T(8,128)(2,1)}) %all-gather.23.cloned.1.call-update) | async-done | bytes 2621456 | tf_op jit(solution)/shard_map/all_gather | solution.py:125
  (822 shorter events, 328.2 us)
Async XLA Ops:
  9.8 16.6 %all-to-all-start.1 = ((bf16[4,320,128]{2,1,0:T(8,128)(2,1)}), bf16[4,320,128]{2,1,0:T(8,128)(2,1)S(1)}, u32[]{:S(2)}, u32[]{:S(2)}) async-start(bf16[4,320,128]{2,1,0:T(8,128)(2,1)} %copy.367), calls=%async_computation.1 | async-start | bytes 655360 | tf_op jit(solution)/shard_map/all_to_all | solution.py:121
  16.1 87.6 %reduce-scatter.8.cloned.1.call-start = ((), (), s32[]{:S(2)}) async-start(), calls=%async_computation.18 | async-start | bytes 8847360 | tf_op jit(solution)/shard_map/reduce_scatter | solution.py:129
  33.7 39.3 %collective-permute-start.5 = (bf16[128,1664]{1,0:T(8,128)(2,1)}, bf16[128,1664]{1,0:T(8,128)(2,1)S(1)}, u32[]{:S(2)}, u32[]{:S(2)}) collective-permute-start(bf16[128,1664]{1,0:T(8,128)(2,1)} %fusion.64), channel_id=1, source_target_pairs={{0,1},{1,2},{2,3},{4,5},{5,6},{6,7},{8,9},{9,10},{10,11},{12,13},{... | collective-permute-start | bytes 1277960 | tf_op jit(solution)/shard_map/ppermute | solution.py:104
  35.6 49.0 %collective-permute-start.8 = (bf16[128,1664]{1,0:T(8,128)(2,1)}, bf16[128,1664]{1,0:T(8,128)(2,1)S(1)}, u32[]{:S(2)}, u32[]{:S(2)}) collective-permute-start(bf16[128,1664]{1,0:T(8,128)(2,1)} %fusion.64), channel_id=1, source_target_pairs={{1,0},{2,1},{3,2},{5,4},{6,5},{7,6},{9,8},{10,9},{11,10},{13,12},{... | collective-permute-start | bytes 1277960 | tf_op jit(solution)/shard_map/ppermute | solution.py:105
  38.1 19.9 %all-to-all-start = ((bf16[4,48,1152]{2,1,0:T(8,128)(2,1)}), bf16[4,48,1152]{2,1,0:T(8,128)(2,1)S(1)}, u32[]{:S(2)}, u32[]{:S(2)}) async-start(bf16[4,48,1152]{2,1,0:T(8,128)(2,1)} %copy.362), calls=%async_computation | async-start | bytes 884736 | tf_op jit(solution)/shard_map/all_to_all | solution.py:121
  43.6 101.6 %all-gather.9.cloned.1.call-start = ((), (), s32[]{:S(2)}) async-start(), calls=%async_computation.16 | async-start | bytes 3981312 | tf_op jit(solution)/shard_map/all_gather | solution.py:125
  73.0 14.6 %collective-permute-start.6 = (bf16[128,1664]{1,0:T(8,128)(2,1)S(1)}, bf16[128,1664]{1,0:T(8,128)(2,1)S(1)}, u32[]{:S(2)}, u32[]{:S(2)}) collective-permute-start(bf16[128,1664]{1,0:T(8,128)(2,1)S(1)} %collective-permute-done.5), channel_id=1, source_target_pairs={{0,1},{1,2},{2,3},{4,5},{5,6},{6,7},{8,9},{9,10},{10,11},{12,13},{... | collective-permute-start | bytes 1277960 | tf_op jit(solution)/shard_map/ppermute | solution.py:104
  84.6 12.1 %collective-permute-start.9 = (bf16[128,1664]{1,0:T(8,128)(2,1)S(1)}, bf16[128,1664]{1,0:T(8,128)(2,1)S(1)}, u32[]{:S(2)}, u32[]{:S(2)}) collective-permute-start(bf16[128,1664]{1,0:T(8,128)(2,1)S(1)} %collective-permute-done.8), channel_id=1, source_target_pairs={{1,0},{2,1},{3,2},{5,4},{6,5},{7,6},{9,8},{10,9},{11,10},{13,12},{... | collective-permute-start | bytes 1277960 | tf_op jit(solution)/shard_map/ppermute | solution.py:105
  87.6 23.4 %collective-permute-start.7 = (bf16[128,1664]{1,0:T(8,128)(2,1)S(1)}, bf16[128,1664]{1,0:T(8,128)(2,1)}, u32[]{:S(2)}, u32[]{:S(2)}) collective-permute-start(bf16[128,1664]{1,0:T(8,128)(2,1)S(1)} %collective-permute-done.6), channel_id=1, source_target_pairs={{0,1},{1,2},{2,3},{4,5},{5,6},{6,7},{8,9},{9,10},{10,11},{12,13},{... | collective-permute-start | bytes 1277960 | tf_op jit(solution)/shard_map/ppermute | solution.py:104
  96.7 20.1 %collective-permute-start.10 = (bf16[128,1664]{1,0:T(8,128)(2,1)S(1)}, bf16[128,1664]{1,0:T(8,128)(2,1)}, u32[]{:S(2)}, u32[]{:S(2)}) collective-permute-start(bf16[128,1664]{1,0:T(8,128)(2,1)S(1)} %collective-permute-done.9), channel_id=1, source_target_pairs={{1,0},{2,1},{3,2},{5,4},{6,5},{7,6},{9,8},{10,9},{11,10},{13,12},{... | collective-permute-start | bytes 1277960 | tf_op jit(solution)/shard_map/ppermute | solution.py:105
  105.9 29.5 %all-to-all-start.2 = ((bf16[4,160,768]{2,1,0:T(8,128)(2,1)}), bf16[4,160,768]{2,1,0:T(8,128)(2,1)S(1)}, u32[]{:S(2)}, u32[]{:S(2)}) async-start(bf16[4,160,768]{2,1,0:T(8,128)(2,1)} %bitcast.471), calls=%async_computation.3 | async-start | bytes 1966080 | tf_op jit(solution)/shard_map/all_to_all | solution.py:121
  110.9 73.9 %all-gather.13.cloned.1.call-start = ((), (), s32[]{:S(2)}) async-start(), calls=%async_computation.19 | async-start | bytes 2211840 | tf_op jit(solution)/shard_map/all_gather | solution.py:125
  144.7 74.3 %all-gather.11.cloned.1.call-start = ((), (), s32[]{:S(2)}) async-start(), calls=%async_computation.17 | async-start | bytes 7077888 | tf_op jit(solution)/shard_map/all_gather | solution.py:125
  162.7 126.6 %all-gather.15.cloned.1.call-start = ((), (), s32[]{:S(2)}) async-start(), calls=%async_computation.20 | async-start | bytes 4866048 | tf_op jit(solution)/shard_map/all_gather | solution.py:125
  166.0 16.2 %all-to-all-start.4 = ((bf16[8,48,1024]{2,1,0:T(8,128)(2,1)}), bf16[8,48,1024]{2,1,0:T(8,128)(2,1)S(1)}, u32[]{:S(2)}, u32[]{:S(2)}) async-start(bf16[8,48,1024]{2,1,0:T(8,128)(2,1)} %copy.387), calls=%async_computation.5 | async-start | bytes 1572864 | tf_op jit(solution)/shard_map/all_to_all | solution.py:121
  169.7 187.3 %all-gather.17.cloned.1.call-start = ((), (), s32[]{:S(2)}) async-start(), calls=%async_computation.21 | async-start | bytes 3932160 | tf_op jit(solution)/shard_map/all_gather | solution.py:125
  251.1 38.1 %all-to-all-start.3 = ((bf16[4,128,384]{1,2,0:T(8,128)(2,1)}), bf16[4,128,384]{1,2,0:T(8,128)(2,1)S(1)}, u32[]{:S(2)}, u32[]{:S(2)}) async-start(bf16[4,128,384]{1,2,0:T(8,128)(2,1)} %copy.371), calls=%async_computation.4 | async-start | bytes 786432 | tf_op jit(solution)/shard_map/all_to_all | solution.py:121
  255.7 138.8 %all-gather.19.cloned.1.call-start = ((), (), s32[]{:S(2)}) async-start(), calls=%async_computation.22 | async-start | bytes 1966080 | tf_op jit(solution)/shard_map/all_gather | solution.py:125
  307.0 11.0 %collective-permute-start.24 = (bf16[2,1,128,768]{3,2,0,1:T(8,128)(2,1)S(1)}, bf16[2,1,128,768]{3,2,0,1:T(8,128)(2,1)S(1)}, u32[]{:S(2)}, u32[]{:S(2)}) collective-permute-start(bf16[2,1,128,768]{3,2,0,1:T(8,128)(2,1)S(1)} %fusion.80), channel_id=1, source_target_pairs={{0,8},{4,12},{8,0},{12,4},{16,24},{20,28},{24,16},{28,20},{1,9},{5... | collective-permute-start | bytes 1179656 | tf_op jit(solution)/shard_map/ppermute | solution.py:25
  318.0 41.3 %collective-permute-start.22 = (bf16[2,2,1,128,768]{4,3,1,0,2:T(8,128)(2,1)}, bf16[2,2,1,128,768]{4,3,1,0,2:T(8,128)(2,1)}, u32[]{:S(2)}, u32[]{:S(2)}) collective-permute-start(bf16[2,2,1,128,768]{4,3,1,0,2:T(8,128)(2,1)} %fusion.60), channel_id=1, source_target_pairs={{0,4},{4,0},{8,12},{12,8},{16,20},{20,16},{24,28},{28,24},{1,5},{5... | collective-permute-start | bytes 2359304 | tf_op jit(solution)/shard_map/ppermute | solution.py:25
  319.0 42.4 %collective-permute-start.25 = (bf16[2,2,1,128,768]{4,3,1,0,2:T(8,128)(2,1)}, bf16[2,2,1,128,768]{4,3,1,0,2:T(8,128)(2,1)}, u32[]{:S(2)}, u32[]{:S(2)}) collective-permute-start(bf16[2,2,1,128,768]{4,3,1,0,2:T(8,128)(2,1)} %fusion.59), channel_id=1, source_target_pairs={{0,4},{4,0},{8,12},{12,8},{16,20},{20,16},{24,28},{28,24},{1,5},{5... | collective-permute-start | bytes 2359304 | tf_op jit(solution)/shard_map/ppermute | solution.py:25
  319.6 255.7 %reduce-scatter.12.cloned.1.call-start = ((), (), s32[]{:S(2)}) async-start(), calls=%async_computation.24 | async-start | bytes 2211840 | tf_op jit(solution)/shard_map/reduce_scatter | solution.py:129
  403.9 11.5 %collective-permute-start.27 = (bf16[2,128,768]{2,1,0:T(8,128)(2,1)}, bf16[2,128,768]{2,1,0:T(8,128)(2,1)}, u32[]{:S(2)}, u32[]{:S(2)}) collective-permute-start(bf16[2,128,768]{2,1,0:T(8,128)(2,1)} %dynamic-slice_bitcast_fusion.14), channel_id=1, source_target_pairs={{0,8},{4,12},{8,0},{12,4},{16,24},{20,28},{24,16},{28,20},{1,9},{5... | collective-permute-start | bytes 1179656 | tf_op jit(solution)/shard_map/ppermute | solution.py:25
  407.6 11.3 %collective-permute-start.30 = (bf16[2,128,768]{2,1,0:T(8,128)(2,1)}, bf16[2,128,768]{2,1,0:T(8,128)(2,1)}, u32[]{:S(2)}, u32[]{:S(2)}) collective-permute-start(bf16[2,128,768]{2,1,0:T(8,128)(2,1)} %dynamic-slice_bitcast_fusion.13), channel_id=1, source_target_pairs={{0,16},{4,20},{8,24},{12,28},{16,0},{20,4},{24,8},{28,12},{1,17},{... | collective-permute-start | bytes 1179656 | tf_op jit(solution)/shard_map/ppermute | solution.py:25
  460.5 11.2 %collective-permute-start.39 = (bf16[2,128,768]{2,1,0:T(8,128)(2,1)S(1)}, bf16[2,128,768]{2,1,0:T(8,128)(2,1)S(1)}, u32[]{:S(2)}, u32[]{:S(2)}) collective-permute-start(bf16[2,128,768]{2,1,0:T(8,128)(2,1)S(1)} %dynamic-slice_bitcast_fusion.12), channel_id=1, source_target_pairs={{0,8},{4,12},{8,0},{12,4},{16,24},{20,28},{24,16},{28,20},{1,9},{5... | collective-permute-start | bytes 1179656 | tf_op jit(solution)/shard_map/ppermute | solution.py:25
  519.6 174.5 %reduce-scatter.20.cloned.1.call-start = ((), (), s32[]{:S(2)}) async-start(), calls=%async_computation.30 | async-start | bytes 1966080 | tf_op jit(solution)/shard_map/reduce_scatter | solution.py:129
  524.8 211.6 %reduce-scatter.14.cloned.1.call-start = ((), (), s32[]{:S(2)}) async-start(), calls=%async_computation.27 | async-start | bytes 5308416 | tf_op jit(solution)/shard_map/reduce_scatter | solution.py:129
  528.5 244.6 %all-gather.21.cloned.1.call-start = ((), (), s32[]{:S(2)}) async-start(), calls=%async_computation.25 | async-start | bytes 8110080 | tf_op jit(solution)/shard_map/all_gather | solution.py:125
  586.3 261.6 %reduce-scatter.18.cloned.1.call-start = ((), (), s32[]{:S(2)}) async-start(), calls=%async_computation.29 | async-start | bytes 3932160 | tf_op jit(solution)/shard_map/reduce_scatter | solution.py:129
  596.4 281.7 %reduce-scatter.10.cloned.1.call-start = ((), (), s32[]{:S(2)}) async-start(), calls=%async_computation.23 | async-start | bytes 1966080 | tf_op jit(solution)/shard_map/reduce_scatter | solution.py:129
  598.9 12.5 %collective-permute-start.59 = (f32[19,1536]{1,0:T(8,128)S(1)}, f32[19,1536]{1,0:T(8,128)S(1)}, u32[]{:S(2)}, u32[]{:S(2)}) collective-permute-start(f32[19,1536]{1,0:T(8,128)S(1)} %concatenate.120), channel_id=1, source_target_pairs={{0,1},{1,0},{2,3},{3,2},{4,5},{5,4},{6,7},{7,6},{8,9},{9,8},{10,11... | collective-permute-start | bytes 350216 | tf_op jit(solution)/shard_map/ppermute | solution.py:25
  604.6 28.2 %collective-permute-start.44 = (bf16[2,2,512,384]{3,2,0,1:T(8,128)(2,1)S(1)}, bf16[2,2,512,384]{3,2,0,1:T(8,128)(2,1)S(1)}, u32[]{:S(2)}, u32[]{:S(2)}) collective-permute-start(bf16[2,2,512,384]{3,2,0,1:T(8,128)(2,1)S(1)} %bitcast.524), channel_id=1, source_target_pairs={{0,4},{4,0},{8,12},{12,8},{16,20},{20,16},{24,28},{28,24},{1,5},{5... | collective-permute-start | bytes 4718600 | tf_op jit(solution)/shard_map/ppermute | solution.py:25
  623.2 11.6 %collective-permute-start.49 = (bf16[2,2,512,384]{3,2,1,0:T(8,128)(2,1)S(1)}, bf16[2,2,512,384]{3,2,1,0:T(8,128)(2,1)S(1)}, u32[]{:S(2)}, u32[]{:S(2)}) collective-permute-start(bf16[2,2,512,384]{3,2,1,0:T(8,128)(2,1)S(1)} %dynamic-slice_bitcast_fusion), channel_id=1, source_target_pairs={{0,4},{4,0},{8,12},{12,8},{16,20},{20,16},{24,28},{28,24},{1,5},{5... | collective-permute-start | bytes 4718600 | tf_op jit(solution)/shard_map/ppermute | solution.py:25
  633.3 27.1 %collective-permute-start.45 = (bf16[2,512,384]{2,1,0:T(8,128)(2,1)S(1)}, bf16[2,512,384]{2,1,0:T(8,128)(2,1)S(1)}, u32[]{:S(2)}, u32[]{:S(2)}) collective-permute-start(bf16[2,512,384]{2,1,0:T(8,128)(2,1)S(1)} %dynamic-slice_bitcast_fusion.4), channel_id=1, source_target_pairs={{0,8},{4,12},{8,0},{12,4},{16,24},{20,28},{24,16},{28,20},{1,9},{5... | collective-permute-start | bytes 2359304 | tf_op jit(solution)/shard_map/ppermute | solution.py:25
  635.3 30.8 %collective-permute-start.50 = (bf16[2,512,384]{2,1,0:T(8,128)(2,1)S(1)}, bf16[2,512,384]{2,1,0:T(8,128)(2,1)S(1)}, u32[]{:S(2)}, u32[]{:S(2)}) collective-permute-start(bf16[2,512,384]{2,1,0:T(8,128)(2,1)S(1)} %dynamic-slice_bitcast_fusion.3), channel_id=1, source_target_pairs={{0,16},{4,20},{8,24},{12,28},{16,0},{20,4},{24,8},{28,12},{1,17},{... | collective-permute-start | bytes 2359304 | tf_op jit(solution)/shard_map/ppermute | solution.py:25
  660.6 13.2 %collective-permute-start.46 = (bf16[512,384]{1,0:T(8,128)(2,1)S(1)}, bf16[512,384]{1,0:T(8,128)(2,1)S(1)}, u32[]{:S(2)}, u32[]{:S(2)}) collective-permute-start(bf16[512,384]{1,0:T(8,128)(2,1)S(1)} %dynamic-slice_bitcast_fusion.10), channel_id=1, source_target_pairs={{0,16},{4,20},{8,24},{12,28},{16,0},{20,4},{24,8},{28,12},{1,17},{... | collective-permute-start | bytes 1179656 | tf_op jit(solution)/shard_map/ppermute | solution.py:25
  696.0 205.2 %reduce-scatter.16.cloned.1.call-start = ((), (), s32[]{:S(2)}) async-start(), calls=%async_computation.28 | async-start | bytes 737280 | tf_op jit(solution)/shard_map/reduce_scatter | solution.py:129
  712.6 17.5 %collective-permute-start.69 = (bf16[2,2,192,576]{3,2,1,0:T(8,128)(2,1)}, bf16[2,2,192,576]{3,2,1,0:T(8,128)(2,1)}, u32[]{:S(2)}, u32[]{:S(2)}) collective-permute-start(bf16[2,2,192,576]{3,2,1,0:T(8,128)(2,1)} %dynamic-slice_bitcast_fusion.2), channel_id=1, source_target_pairs={{0,4},{4,0},{8,12},{12,8},{16,20},{20,16},{24,28},{28,24},{1,5},{5... | collective-permute-start | bytes 2654216 | tf_op jit(solution)/shard_map/ppermute | solution.py:25
  720.6 13.5 %collective-permute-start.72 = (bf16[2,2,192,576]{3,2,1,0:T(8,128)(2,1)}, bf16[2,2,192,576]{3,2,1,0:T(8,128)(2,1)}, u32[]{:S(2)}, u32[]{:S(2)}) collective-permute-start(bf16[2,2,192,576]{3,2,1,0:T(8,128)(2,1)} %dynamic-slice_bitcast_fusion.1), channel_id=1, source_target_pairs={{0,4},{4,0},{8,12},{12,8},{16,20},{20,16},{24,28},{28,24},{1,5},{5... | collective-permute-start | bytes 2654216 | tf_op jit(solution)/shard_map/ppermute | solution.py:25
  729.4 75.6 %collective-permute-start.65 = (f32[5,1024]{1,0:T(8,128)S(1)}, f32[5,1024]{1,0:T(8,128)S(1)}, u32[]{:S(2)}, u32[]{:S(2)}) collective-permute-start(f32[5,1024]{1,0:T(8,128)S(1)} %add.688), channel_id=1, source_target_pairs={{0,2},{1,3},{2,0},{3,1},{4,6},{5,7},{6,4},{7,5},{8,10},{9,11},{10,... | collective-permute-start | bytes 61448 | tf_op jit(solution)/shard_map/ppermute | solution.py:25
  731.7 73.7 %collective-permute-start.70 = (bf16[2,192,576]{2,1,0:T(8,128)(2,1)S(1)}, bf16[2,192,576]{2,1,0:T(8,128)(2,1)}, u32[]{:S(2)}, u32[]{:S(2)}) collective-permute-start(bf16[2,192,576]{2,1,0:T(8,128)(2,1)S(1)} %dynamic-slice_bitcast_fusion.8), channel_id=1, source_target_pairs={{0,8},{4,12},{8,0},{12,4},{16,24},{20,28},{24,16},{28,20},{1,9},{5... | collective-permute-start | bytes 1327112 | tf_op jit(solution)/shard_map/ppermute | solution.py:25
  735.7 90.6 %collective-permute-start.73 = (bf16[2,192,576]{2,1,0:T(8,128)(2,1)S(1)}, bf16[2,192,576]{2,1,0:T(8,128)(2,1)}, u32[]{:S(2)}, u32[]{:S(2)}) collective-permute-start(bf16[2,192,576]{2,1,0:T(8,128)(2,1)S(1)} %dynamic-slice_bitcast_fusion.7), channel_id=1, source_target_pairs={{0,16},{4,20},{8,24},{12,28},{16,0},{20,4},{24,8},{28,12},{1,17},{... | collective-permute-start | bytes 1327112 | tf_op jit(solution)/shard_map/ppermute | solution.py:25
  800.4 24.7 %all-to-all-start.6 = ((bf16[4,320,128]{2,1,0:T(8,128)(2,1)}), bf16[4,320,128]{2,1,0:T(8,128)(2,1)S(1)}, u32[]{:S(2)}, u32[]{:S(2)}) async-start(bf16[4,320,128]{2,1,0:T(8,128)(2,1)} %bitcast.548), calls=%async_computation.9 | async-start | bytes 655360 | tf_op jit(solution)/shard_map/all_to_all | solution.py:121
  803.8 128.5 %all-gather.23.cloned.1.call-start = ((), (), s32[]{:S(2)}) async-start(), calls=%async_computation.26 | async-start | bytes 2949120 | tf_op jit(solution)/shard_map/all_gather | solution.py:125
  805.0 34.3 %collective-permute-start.66 = (f32[5,1024]{1,0:T(8,128)S(1)}, f32[5,1024]{1,0:T(8,128)S(1)}, u32[]{:S(2)}, u32[]{:S(2)}) collective-permute-start(f32[5,1024]{1,0:T(8,128)S(1)} %add.689), channel_id=1, source_target_pairs={{0,4},{4,0},{8,12},{12,8},{16,20},{20,16},{24,28},{28,24},{1,5},{5... | collective-permute-start | bytes 61448 | tf_op jit(solution)/shard_map/ppermute | solution.py:25
  806.5 21.0 %collective-permute-start.71 = (bf16[192,576]{1,0:T(8,128)(2,1)S(1)}, bf16[192,576]{1,0:T(8,128)(2,1)}, u32[]{:S(2)}, u32[]{:S(2)}) collective-permute-start(bf16[192,576]{1,0:T(8,128)(2,1)S(1)} %dynamic-slice_bitcast_fusion.16), channel_id=1, source_target_pairs={{0,16},{4,20},{8,24},{12,28},{16,0},{20,4},{24,8},{28,12},{1,17},{... | collective-permute-start | bytes 663560 | tf_op jit(solution)/shard_map/ppermute | solution.py:25
  834.7 15.0 %all-to-all-start.7 = ((bf16[4,48,1152]{2,1,0:T(8,128)(2,1)}), bf16[4,48,1152]{2,1,0:T(8,128)(2,1)S(1)}, u32[]{:S(2)}, u32[]{:S(2)}) async-start(bf16[4,48,1152]{2,1,0:T(8,128)(2,1)} %bitcast.188), calls=%async_computation.10 | async-start | bytes 884736 | tf_op jit(solution)/shard_map/all_to_all | solution.py:121
  849.7 16.3 %all-to-all-start.8 = ((bf16[8,48,1024]{2,1,0:T(8,128)(2,1)}), bf16[8,48,1024]{2,1,0:T(8,128)(2,1)S(1)}, u32[]{:S(2)}, u32[]{:S(2)}) async-start(bf16[8,48,1024]{2,1,0:T(8,128)(2,1)} %bitcast.536), calls=%async_computation.14 | async-start | bytes 1572864 | tf_op jit(solution)/shard_map/all_to_all | solution.py:121
  (211 other events, 2797.1 us)
Sparse Core Ops, SparseCore 0:
  32.1 71.5 reduce-scatter.7
  106.3 34.5 all-gather.8
  144.8 26.1 all-gather.12
  173.5 45.4 all-gather.10
  222.0 67.1 all-gather.14
  291.3 65.6 all-gather.16
  358.7 35.7 all-gather.18
  519.7 55.5 reduce-scatter.11
  577.6 39.8 reduce-scatter.19
  621.4 64.7 reduce-scatter.13
  690.0 83.1 all-gather.20
  775.4 63.7 reduce-scatter.17
  841.6 36.4 reduce-scatter.9
  880.3 20.8 reduce-scatter.15
  903.7 28.5 all-gather.22

commit v2 on v1

v2 whole, which is shorter than its diff:
```python
import functools
import math

import jax
import jax.numpy as jnp
import numpy as np
from jax import lax
from jax.experimental import pallas as pl
from jax.experimental.pallas import tpu as pltpu
from jax.sharding import PartitionSpec as P

CAP = 256
KEY_BLOCK = 512
epsilon = 1e-06
rope_base = 10000.0
masked_score = -1e30
BF = jnp.bfloat16
F32 = jnp.float32
BOTH = ("seq", "sub")
VMEM_BYTES = 56 * 1024 * 1024
KERNEL_WORK = 16


def axis_bits(axis):
    masks, mask = [], 1
    while mask < lax.axis_size(axis):
        masks.append(mask)
        mask *= 2
    return masks


def send(values, axis, mask):
    count = lax.axis_size(axis)
    return lax.ppermute(values, axis, [(i, i ^ mask) for i in range(count)])


class Flow:
    def __init__(self, stages):
        self.stages = stages
        self.result = None
        self.done = False
        self.wanted = next(stages)

    def feed(self, arrived):
        try:
            self.wanted = self.stages.send(arrived)
        except StopIteration as stop:
            self.wanted, self.done, self.result = [], True, stop.value


class Schedule:
    def __init__(self):
        self.frontier = ()

    def tie(self, *arrays):
        tied = lax.optimization_barrier(tuple(arrays) + self.frontier)
        return tied[: len(arrays)]

    def step(self, *flows, work=None, args=()):
        flows = [flow for flow in flows if not flow.done]
        sends = [item for flow in flows for item in flow.wanted]
        tied = self.tie(*[item[0] for item in sends], *args)
        arrived = [send(value, item[1], item[2]) for value, item in zip(tied, sends)]
        outputs = work(*tied[len(sends) :]) if work is not None else ()
        self.frontier = tuple(arrived) + tuple(jax.tree.leaves(outputs))
        for flow in flows:
            count = len(flow.wanted)
            flow.feed(arrived[:count])
            arrived = arrived[count:]
        return outputs

    def start(self, flow, *others):
        tied = lax.optimization_barrier(
            tuple(item[0] for item in flow.wanted) + self.frontier + tuple(others)
        )
        flow.feed([send(v, item[1], item[2]) for v, item in zip(tied, flow.wanted)])
        return flow.result

    def held(self, values):
        return list(self.tie(*values))


def in_order(pieces, index):
    mask = 1
    while mask < len(pieces):
        flip = (index // mask) % 2 == 1
        pieces = [jnp.where(flip, pieces[i ^ mask], pieces[i]) for i in range(len(pieces))]
        mask *= 2
    return pieces


def rows_in_order(pieces, index):
    shape = pieces[0][1].shape
    result = jnp.zeros((len(pieces),) + shape, pieces[0][1].dtype)
    for mask, piece in pieces:
        result = lax.dynamic_update_index_in_dim(result, piece, index ^ mask, 0)
    return result.reshape((len(pieces) * shape[0],) + shape[1:])


def gather_even_odd(values, axis="seq"):
    arrived = yield [(values, axis, mask) for mask in range(2, lax.axis_size(axis), 2)]
    even = jnp.concatenate([values] + arrived, 0)
    (odd,) = yield [(even, axis, 1)]
    return even, odd


def scatter_even_odd(even, odd, axis="seq"):
    count = lax.axis_size(axis) // 2
    rows = even.shape[0] // count
    (other,) = yield [(odd, axis, 1)]
    held = (even.astype(F32) + other.astype(F32)).astype(even.dtype)
    arrived = yield [
        (held[i * rows : (i + 1) * rows], axis, 2 * i) for i in range(1, count)
    ]
    result = held[:rows].astype(F32)
    for piece in arrived:
        result = result + piece.astype(F32)
    return result


def gather_seq(values, dim=0, dtype=None):
    even, odd = yield from gather_even_odd(values)
    return place(even, odd, lax.axis_index("seq"), dim, dtype or values.dtype)


def scatter_seq(values):
    index = lax.axis_index("seq")
    count = lax.axis_size("seq")
    blocks = values.reshape((count, values.shape[0] // count) + values.shape[1:])
    halves = [
        jnp.concatenate(
            [
                lax.dynamic_index_in_dim(blocks, index ^ mask, 0, keepdims=False)
                for mask in range(core, count, 2)
            ],
            0,
        )
        for core in range(2)
    ]
    result = yield from scatter_even_odd(*halves)
    return result


def pair_sum(pieces):
    while len(pieces) > 1:
        pieces = [pieces[i] + pieces[i + 1] for i in range(0, len(pieces), 2)]
    return pieces[0]


def total(values, axes):
    for axis in axes:
        groups = [range(1, lax.axis_size(axis))]
        if axis == "seq":
            groups = [range(2, lax.axis_size(axis), 2), [1]]
        for masks in groups:
            arrived = yield [(values, axis, mask) for mask in masks]
            values = pair_sum([values] + arrived)
    return values


def total_cube(values, axes):
    for axis in axes:
        for mask in axis_bits(axis):
            (other,) = yield [(values, axis, mask)]
            values = values + other
    return values


def total_rows(values, axis="sub"):
    count = lax.axis_size(axis)
    rows = values.shape[1] // count
    arrived = yield [(values, axis, mask) for mask in range(1, count)]
    for mask, other in enumerate(arrived, 1):
        values = values + jnp.concatenate(
            [other[:, (i ^ mask) * rows : ((i ^ mask) + 1) * rows] for i in range(count)], 1
        )
    return values


def gather_direct(values, axis="sub"):
    arrived = yield [(values, axis, mask) for mask in range(1, lax.axis_size(axis))]
    return [values] + arrived


def swap_direct(blocks, axis="sub"):
    arrived = yield [(blocks[mask], axis, mask) for mask in range(1, len(blocks))]
    return [blocks[0]] + arrived


def scatter_direct(blocks, axis="sub"):
    arrived = yield [(blocks[mask], axis, mask) for mask in range(1, len(blocks))]
    result = blocks[0].astype(F32)
    for other in arrived:
        result = result + other.astype(F32)
    return result


def blocks_for(values, dim, axis="sub"):
    index = lax.axis_index(axis)
    count = lax.axis_size(axis)
    size = values.shape[dim] // count
    if dim == 0:
        blocks = values.reshape((count, size) + values.shape[1:])
        return [
            lax.dynamic_index_in_dim(blocks, index ^ mask, 0, keepdims=False)
            for mask in range(count)
        ]
    return in_order([values[:, i * size : (i + 1) * size] for i in range(count)], index)


def swap_blocks(values, axis):
    return lax.all_to_all(values, axis, split_axis=0, concat_axis=0, tiled=True)


def swap_copies(values, axis="sub"):
    return swap_blocks(jnp.broadcast_to(values[None], (lax.axis_size(axis),) + values.shape), axis)


def gather_rows(values, axis):
    return lax.all_gather(values, axis, axis=0, tiled=True)


def scatter_rows(values, axis):
    return lax.psum_scatter(values, axis, scatter_dimension=0, tiled=True)


def inv_rms(values):
    return lax.rsqrt(jnp.mean(values * values, -1, keepdims=True) + epsilon)


def norm_back(normed_hat, inverse, grad_hat):
    return inverse * (grad_hat - normed_hat * jnp.mean(normed_hat * grad_hat, -1, keepdims=True))


def dot(left, right):
    return jnp.dot(left, right, preferred_element_type=F32)


def dot_nt(left, right):
    return lax.dot_general(left, right, (((1,), (1,)), ((), ())), preferred_element_type=F32)


def dot_tn(left, right):
    return lax.dot_general(left, right, (((0,), (0,)), ((), ())), preferred_element_type=F32)


def rope_tables(positions, head_dim, heads):
    pair_total = head_dim // 2
    frame_pairs = pair_total // 4
    height_pairs = (pair_total - frame_pairs) // 2
    width_pairs = pair_total - frame_pairs - height_pairs
    frequency = np.zeros((3, pair_total), np.float32)
    start = 0
    for axis_id, pair_count in enumerate((frame_pairs, height_pairs, width_pairs)):
        exponent = -np.arange(pair_count, dtype=np.float32) / np.float32(pair_count)
        frequency[axis_id, start : start + pair_count] = np.float32(rope_base) ** exponent
        start += pair_count
    frequency = jnp.asarray(np.repeat(frequency, 2, axis=1))
    angles = (
        positions[:, 0:1] * frequency[0:1]
        + positions[:, 1:2] * frequency[1:2]
        + positions[:, 2:3] * frequency[2:3]
    )
    sign = jnp.asarray(np.where(np.arange(head_dim) % 2 == 0, -1.0, 1.0).astype(np.float32))
    cosine = jnp.cos(angles)
    sine = jnp.sin(angles) * sign[None, :]
    return (jnp.tile(cosine, (1, heads)), jnp.tile(sine, (1, heads)))


def rotate(values, cosine, sine):
    even = lax.broadcasted_iota(jnp.int32, values.shape, 1) % 2 == 0
    swapped = jnp.where(even, jnp.roll(values, -1, 1), jnp.roll(values, 1, 1))
    return values * cosine + swapped * sine


def clip_index(token_index, clip_lengths):
    bounds = jnp.cumsum(clip_lengths)
    return jnp.sum((token_index[:, None] >= bounds[None, :]).astype(jnp.int32), 1)


def pick_rows(onehot, rows):
    picked = onehot[:, 0:1] * rows[0:1]
    for clip in range(1, rows.shape[0]):
        picked = picked + onehot[:, clip : clip + 1] * rows[clip : clip + 1]
    return picked


def own_lanes(block, head, head_dim):
    if block.shape[1] == head_dim:
        return block
    lane = lax.broadcasted_iota(jnp.int32, block.shape, 1)
    return jnp.where(lane // head_dim == head, block, jnp.zeros_like(block))


def key_blocks(ranges, own_rows, rows, visit):
    per_group = rows // KEY_BLOCK
    per_block = KEY_BLOCK // own_rows

    def step(place, carry):
        block = (place // per_group) * per_group
        block = block + ((place % per_group) ^ (ranges[5] // per_block))
        row = lax.broadcasted_iota(jnp.int32, (KEY_BLOCK, rows), 0)
        index = place * KEY_BLOCK + (row ^ ((ranges[5] % per_block) * own_rows))
        visit(pl.multiple_of(block * KEY_BLOCK, KEY_BLOCK), index)
        return carry

    lax.fori_loop(ranges[0], ranges[1], step, 0)


def self_forward_kernel(
    head_dim,
    lanes,
    own_rows,
    ranges,
    q_ref,
    kv_ref,
    meta_ref,
    self_ref,
    lse_ref,
    max_ref,
    sum_ref,
    acc_ref,
):
    rows, width = q_ref.shape
    per = lanes // head_dim
    max_ref[...] = jnp.full(max_ref.shape, masked_score, F32)
    sum_ref[...] = jnp.zeros(sum_ref.shape, F32)
    acc_ref[...] = jnp.zeros(acc_ref.shape, F32)
    first = meta_ref[0:1, :]
    last = meta_ref[1:2, :]

    def visit(start, key_index):
        allowed = (key_index >= first) & (key_index < last)
        for part in range(width // lanes):
            k_lanes = slice(part * lanes, (part + 1) * lanes)
            keys = kv_ref[pl.ds(start, KEY_BLOCK), k_lanes]
            values = kv_ref[pl.ds(start, KEY_BLOCK), width + part * lanes : width + (part + 1) * lanes]
            for j in range(per):
                h = part * per + j
                own = slice(h * head_dim, (h + 1) * head_dim)
                queries = own_lanes(q_ref[:, k_lanes], j, head_dim)
                scores = jnp.where(allowed, dot_nt(keys, queries), masked_score)
                old_max = max_ref[h : h + 1, :]
                new_max = jnp.maximum(old_max, jnp.max(scores, 0, keepdims=True))
                probs = jnp.exp(scores - new_max)
                factor = jnp.exp(old_max - new_max)
                max_ref[h : h + 1, :] = new_max
                sum_ref[h : h + 1, :] = sum_ref[h : h + 1, :] * factor + jnp.sum(
                    probs, 0, keepdims=True
                )
                product = dot_tn(values, probs.astype(BF))[j * head_dim : (j + 1) * head_dim, :]
                acc_ref[own, :] = acc_ref[own, :] * factor + product

    key_blocks(ranges, own_rows, rows, visit)
    lse_ref[...] = jnp.zeros(lse_ref.shape, F32)
    for h in range(width // head_dim):
        own = slice(h * head_dim, (h + 1) * head_dim)
        sums = sum_ref[h : h + 1, :]
        acc_ref[own, :] = acc_ref[own, :] / sums
        lse_ref[h : h + 1, :] = max_ref[h : h + 1, :] + jnp.log(sums)
    for part in range(width // lanes):
        own = slice(part * lanes, (part + 1) * lanes)
        self_ref[:, own] = acc_ref[own, :].T


def cross_forward_kernel(
    head_dim, lanes, ranges, gates, q_ref, tkv_ref, meta_ref, self_ref, mixed_ref, cross_ref, lse_ref, acc_ref
):
    rows, width = q_ref.shape
    acc_ref[...] = jnp.zeros(acc_ref.shape, F32)
    lse_ref[...] = jnp.zeros(lse_ref.shape, F32)
    clip = meta_ref[2:3, :]
    per = lanes // head_dim

    def step(which, carry):
        start = pl.multiple_of(which * CAP, CAP)
        slot = lax.broadcasted_iota(jnp.int32, (CAP, rows), 0)
        valid = slot < ranges[6 + which]
        here = clip == which
        for part in range(width // lanes):
            keys = tkv_ref[pl.ds(start, CAP), part * lanes : (part + 1) * lanes]
            values = tkv_ref[pl.ds(start, CAP), width + part * lanes : width + (part + 1) * lanes]
            queries = q_ref[:, part * lanes : (part + 1) * lanes]
            for j in range(per):
                h = part * per + j
                own = slice(h * head_dim, (h + 1) * head_dim)
                scores = dot_nt(keys, own_lanes(queries, j, head_dim))
                scores = jnp.where(valid, scores, masked_score)
                top = jnp.max(scores, 0, keepdims=True)
                probs = jnp.exp(scores - top)
                sums = jnp.sum(probs, 0, keepdims=True)
                probs = (probs / sums).astype(BF)
                product = dot_tn(values, probs)[j * head_dim : (j + 1) * head_dim, :]
                acc_ref[own, :] = jnp.where(here, product, acc_ref[own, :])
                lse_ref[h : h + 1, :] = jnp.where(here, top + jnp.log(sums), lse_ref[h : h + 1, :])
        return carry

    lax.fori_loop(ranges[2], ranges[3], step, 0)
    lane = lax.broadcasted_iota(jnp.int32, (1, lanes), 1)
    for part in range(width // lanes):
        own = slice(part * lanes, (part + 1) * lanes)
        cross = acc_ref[own, :].T
        gate = jnp.full((1, lanes), gates[part * per], F32)
        for j in range(1, per):
            gate = jnp.where(lane // head_dim == j, gates[part * per + j], gate)
        cross_ref[:, own] = cross
        mixed_ref[:, own] = (self_ref[:, own].astype(BF).astype(F32) + gate * cross).astype(BF)


def cross_backward_kernel(
    head_dim, lanes, ranges, gates, q_ref, tkv_ref, meta_ref, dout_ref, lse_ref, acc_ref, dtkv_ref, gated_ref
):
    rows, width = q_ref.shape
    per = lanes // head_dim
    dtkv_ref[...] = jnp.zeros(dtkv_ref.shape, dtkv_ref.dtype)
    acc_ref[...] = jnp.zeros(acc_ref.shape, F32)
    lane = lax.broadcasted_iota(jnp.int32, (1, lanes), 1)
    for part in range(width // lanes):
        own = slice(part * lanes, (part + 1) * lanes)
        gate = jnp.full((1, lanes), gates[part * per], F32)
        for j in range(1, per):
            gate = jnp.where(lane // head_dim == j, gates[part * per + j], gate)
        gated_ref[:, own] = (dout_ref[:, own].astype(F32) * gate).astype(BF)
    clip = meta_ref[2:3, :]

    def step(which, carry):
        start = pl.multiple_of(which * CAP, CAP)
        slot = lax.broadcasted_iota(jnp.int32, (CAP, rows), 0)
        allowed = (slot < ranges[6 + which]) & (clip == which)
        for part in range(width // lanes):
            k_lanes = slice(part * lanes, (part + 1) * lanes)
            v_lanes = slice(width + part * lanes, width + (part + 1) * lanes)
            keys = tkv_ref[pl.ds(start, CAP), k_lanes]
            values = tkv_ref[pl.ds(start, CAP), v_lanes]
            key_grad = value_grad = 0.0
            for j in range(per):
                h = part * per + j
                own = slice(h * head_dim, (h + 1) * head_dim)
                queries = own_lanes(q_ref[:, k_lanes], j, head_dim)
                grads = own_lanes(gated_ref[:, k_lanes], j, head_dim)
                scores = dot_nt(keys, queries)
                probs = jnp.where(allowed, jnp.exp(scores - lse_ref[h : h + 1, :]), 0.0)
                prob_grad = dot_nt(values, grads)
                value_grad = value_grad + dot(probs.astype(BF), grads)
                inner = jnp.sum(probs * prob_grad, 0, keepdims=True)
                score_grad = (probs * (prob_grad - inner)).astype(BF)
                key_grad = key_grad + dot(score_grad, queries)
                product = dot_tn(keys, score_grad)[j * head_dim : (j + 1) * head_dim, :]
                acc_ref[own, :] = acc_ref[own, :] + product
            dtkv_ref[pl.ds(start, CAP), k_lanes] = key_grad.astype(dtkv_ref.dtype)
            dtkv_ref[pl.ds(start, CAP), v_lanes] = value_grad.astype(dtkv_ref.dtype)
        return carry

    lax.fori_loop(ranges[2], ranges[3], step, 0)


def self_backward_kernel(
    head_dim,
    lanes,
    own_rows,
    ranges,
    q_ref,
    kv_ref,
    meta_ref,
    dout_ref,
    self_ref,
    lse_ref,
    start_ref,
    dq_ref,
    dkv_ref,
    delta_ref,
    acc_ref,
):
    rows, width = q_ref.shape
    per = lanes // head_dim
    dkv_ref[...] = jnp.zeros(dkv_ref.shape, dkv_ref.dtype)
    acc_ref[...] = start_ref[...]
    for part in range(width // lanes):
        own = slice(part * lanes, (part + 1) * lanes)
        product = (dout_ref[:, own].astype(F32) * self_ref[:, own]).T
        for j in range(per):
            h = part * per + j
            delta_ref[h : h + 1, :] = jnp.sum(
                product[j * head_dim : (j + 1) * head_dim, :], 0, keepdims=True
            )
    first = meta_ref[0:1, :]
    last = meta_ref[1:2, :]

    def visit(start, key_index):
        allowed = (key_index >= first) & (key_index < last)
        for part in range(width // lanes):
            k_lanes = slice(part * lanes, (part + 1) * lanes)
            v_lanes = slice(width + part * lanes, width + (part + 1) * lanes)
            keys = kv_ref[pl.ds(start, KEY_BLOCK), k_lanes]
            values = kv_ref[pl.ds(start, KEY_BLOCK), v_lanes]
            key_grad = value_grad = 0.0
            for j in range(per):
                h = part * per + j
                own = slice(h * head_dim, (h + 1) * head_dim)
                queries = own_lanes(q_ref[:, k_lanes], j, head_dim)
                grads = own_lanes(dout_ref[:, k_lanes], j, head_dim)
                scores = dot_nt(keys, queries)
                probs = jnp.where(allowed, jnp.exp(scores - lse_ref[h : h + 1, :]), 0.0)
                prob_grad = dot_nt(values, grads)
                value_grad = value_grad + dot(probs.astype(BF), grads)
                score_grad = (probs * (prob_grad - delta_ref[h : h + 1, :])).astype(BF)
                key_grad = key_grad + dot(score_grad, queries)
                product = dot_tn(keys, score_grad)[j * head_dim : (j + 1) * head_dim, :]
                acc_ref[own, :] = acc_ref[own, :] + product
            dkv_ref[pl.ds(start, KEY_BLOCK), k_lanes] = key_grad.astype(BF)
            dkv_ref[pl.ds(start, KEY_BLOCK), v_lanes] = value_grad.astype(BF)

    key_blocks(ranges, own_rows, rows, visit)
    for part in range(width // lanes):
        own = slice(part * lanes, (part + 1) * lanes)
        dq_ref[:, own] = acc_ref[own, :].T * (1.0 / math.sqrt(head_dim))


SMEM = pl.BlockSpec(memory_space=pltpu.SMEM)
WHOLE = pl.BlockSpec(memory_space=pltpu.VMEM)


def join_kernel(rows, seq_ref, even_ref, odd_ref, out_ref):
    for core, source in enumerate((even_ref, odd_ref)):
        for i in range(source.shape[0] // rows):
            start = pl.multiple_of((seq_ref[0] ^ (2 * i + core)) * rows, rows)
            out_ref[pl.ds(start, rows), :] = source[i * rows : (i + 1) * rows, :]


def join_columns_kernel(rows, seq_ref, even_ref, odd_ref, out_ref):
    lanes = even_ref.shape[1]
    for core, source in enumerate((even_ref, odd_ref)):
        for i in range(source.shape[0] // rows):
            start = pl.multiple_of((seq_ref[0] ^ (2 * i + core)) * lanes, lanes)
            piece = source[i * rows : (i + 1) * rows, :]
            out_ref[:, pl.ds(start, lanes)] = piece.astype(out_ref.dtype)


def place(even, odd, seq, dim, dtype):
    chips = lax.axis_size("seq") // 2
    rows = even.shape[0] // chips
    kernel = join_kernel if dim == 0 else join_columns_kernel
    shape = (2 * even.shape[0], even.shape[1])
    if dim == 1:
        shape = (rows, 2 * chips * even.shape[1])
    return pl.pallas_call(
        functools.partial(kernel, rows),
        out_shape=jax.ShapeDtypeStruct(shape, dtype),
        in_specs=[SMEM] + [WHOLE] * 2,
        out_specs=WHOLE,
        compiler_params=pltpu.CompilerParams(vmem_limit_bytes=VMEM_BYTES),
    )(jnp.reshape(seq, (1,)).astype(jnp.int32), even, odd)


def kernel_call(kernel, outputs, scratch, smem, arrays, work):
    return pl.pallas_call(
        kernel,
        out_shape=tuple(jax.ShapeDtypeStruct(shape, dtype) for shape, dtype in outputs),
        in_specs=[SMEM] * len(smem) + [WHOLE] * len(arrays),
        out_specs=(WHOLE,) * len(outputs),
        scratch_shapes=[pltpu.VMEM(shape, dtype) for shape, dtype in scratch],
        compiler_params=pltpu.CompilerParams(vmem_limit_bytes=VMEM_BYTES),
        cost_estimate=pl.CostEstimate(
            flops=work, bytes_accessed=sum(a.size * 2 for a in arrays), transcendentals=0
        ),
    )(*smem, *arrays)


def self_forward(ranges, queries, kv, meta, head_dim, lanes, own_rows):
    rows, width = queries.shape
    return kernel_call(
        functools.partial(self_forward_kernel, head_dim, lanes, own_rows),
        [((rows, width), F32), ((8, rows), F32)],
        [((8, rows), F32), ((8, rows), F32), ((width, rows), F32)],
        [ranges],
        [queries, kv, meta],
        KERNEL_WORK * rows * kv.shape[0] * width,
    )


def cross_forward(ranges, gates, queries, tkv, meta, self_out, head_dim, lanes):
    rows, width = queries.shape
    return kernel_call(
        functools.partial(cross_forward_kernel, head_dim, lanes),
        [((rows, width), BF), ((rows, width), F32), ((8, rows), F32)],
        [((width, rows), F32)],
        [ranges, gates],
        [queries, tkv, meta, self_out],
        KERNEL_WORK * rows * CAP * width,
    )


def cross_backward(ranges, gates, queries, tkv, meta, dout, lse, head_dim, lanes):
    rows, width = queries.shape
    return kernel_call(
        functools.partial(cross_backward_kernel, head_dim, lanes),
        [((width, rows), F32), (tkv.shape, BF)],
        [((rows, width), BF)],
        [ranges, gates],
        [queries, tkv, meta, dout, lse],
        2 * KERNEL_WORK * rows * CAP * width,
    )


def self_backward(ranges, queries, kv, meta, dout, self_out, lse, start, head_dim, lanes, own_rows):
    rows, width = queries.shape
    return kernel_call(
        functools.partial(self_backward_kernel, head_dim, lanes, own_rows),
        [((rows, width), F32), (kv.shape, BF)],
        [((8, rows), F32), ((width, rows), F32)],
        [ranges],
        [queries, kv, meta, dout, self_out, lse, start],
        2 * KERNEL_WORK * rows * kv.shape[0] * width,
    )


def body(
    video,
    conditioning,
    captions,
    clip_lengths,
    cap_lengths,
    positions,
    ada_weight,
    ada_bias,
    query_weight,
    key_weight,
    value_weight,
    out_weight,
    text_key_weight,
    text_value_weight,
    gate_weight,
    up_weight,
    down_weight,
    attn_gain,
    query_gain,
    key_gain,
    text_key_gain,
    attn_out_gain,
    ffn_gain,
    ffn_out_gain,
    cross_gate,
    cotangent,
):
    num_sub = lax.axis_size("sub")
    num_seq = lax.axis_size("seq")
    rows, width = video.shape
    heads_total = cross_gate.shape[0]
    head_dim = width // heads_total
    heads = heads_total // num_sub
    cols = width // num_sub
    device = lax.axis_index(BOTH)
    seq = lax.axis_index("seq")
    sub = lax.axis_index("sub")
    group = rows * num_sub
    tokens = group * num_seq
    clips = clip_lengths.shape[0]
    clip_range = jnp.arange(clips, dtype=jnp.int32)
    score_scale = 1.0 / math.sqrt(head_dim)

    ends = jnp.cumsum(clip_lengths)
    starts = ends - clip_lengths
    member = jnp.arange(group, dtype=jnp.int32)
    group_token = (seq * num_sub + (sub ^ (member // rows))) * rows + member % rows
    group_clip = clip_index(group_token, clip_lengths)
    group_hot_bool = group_clip[:, None] == clip_range[None, :]
    group_hot = group_hot_bool.astype(F32)
    own_hot = group_hot[:rows]
    first = jnp.sum(jnp.where(group_hot_bool, starts[None, :], 0), 1)
    last = jnp.sum(jnp.where(group_hot_bool, ends[None, :], 0), 1)
    meta = jnp.concatenate(
        [first[None], last[None], group_clip[None], jnp.zeros((5, group), jnp.int32)], 0
    )
    ranges = jnp.concatenate(
        [
            jnp.stack(
                [
                    jnp.min(first) // KEY_BLOCK,
                    (jnp.max(last) + KEY_BLOCK - 1) // KEY_BLOCK,
                    jnp.min(group_clip),
                    jnp.max(group_clip) + 1,
                    seq,
                    sub,
                ]
            ).astype(jnp.int32),
            cap_lengths,
        ]
    )
    gate_tanh = jnp.tanh(cross_gate.astype(F32))
    gates = lax.dynamic_slice_in_dim(gate_tanh, sub * heads, heads, 0)

    cond_float = conditioning.astype(F32)
    cond_act = jax.nn.silu(cond_float).astype(BF)
    cond_rows = ada_weight.shape[0]
    cond_slice = lax.dynamic_slice_in_dim(cond_act, device * cond_rows, cond_rows, 1)
    mod_part = dot(cond_slice, ada_weight)
    mod_part = mod_part + lax.dynamic_update_slice_in_dim(
        jnp.zeros((1, 4 * width), F32), ada_bias.astype(F32)[None], device * ada_bias.shape[0], 1
    )
    mod_part = mod_part.reshape(clips, 4, width)
    gain_rows = attn_gain.shape[0]

    def spread(gains):
        stacked = jnp.stack(gains).astype(F32)
        return lax.dynamic_update_slice_in_dim(
            jnp.zeros((len(gains), width), F32), stacked, device * gain_rows, 1
        )

    order = Schedule()
    out_full = gather_rows(out_weight, BOTH)
    early_flow = Flow(
        total_cube(
            jnp.concatenate([mod_part[:, 0], spread([attn_gain, query_gain, key_gain])], 0),
            ("seq", "sub"),
        )
    )
    late_flow = Flow(
        total_cube(
            jnp.concatenate(
                [
                    mod_part[:, 1],
                    mod_part[:, 2],
                    mod_part[:, 3],
                    spread([text_key_gain, attn_out_gain, ffn_gain, ffn_out_gain]),
                ],
                0,
            ),
            ("seq", "sub"),
        )
    )
    w_rows = query_weight.shape[0]
    qkv_blocks = [
        jnp.concatenate(parts, 1)
        for parts in zip(*[blocks_for(w, 1) for w in (query_weight, key_weight, value_weight)])
    ]
    flow = Flow(swap_direct(qkv_blocks))
    order.step(flow, early_flow)
    packed = jnp.concatenate(
        [video, jnp.pad(positions.astype(BF), ((0, 0), (0, 128 - positions.shape[1])))], 1
    )
    packed = swap_copies(order.tie(packed)[0]).reshape(num_sub * rows, -1)
    flow = Flow(gather_seq(jnp.concatenate(in_order(flow.result, sub), 0)))
    while not (flow.done and early_flow.done):
        order.step(flow, early_flow)
    qkv_weight = flow.result
    early = early_flow.result
    scale_rows = early[:clips]
    attn_gain_f = early[clips : clips + 1]
    query_gain_f = lax.dynamic_slice_in_dim(early[clips + 1 : clips + 2], sub * cols, cols, 1)
    key_gain_f = lax.dynamic_slice_in_dim(early[clips + 2 : clips + 3], sub * cols, cols, 1)
    packed = jnp.concatenate(blocks_for(packed, 0), 0)
    video_group = packed[:, :width].astype(F32)
    group_pos = packed[:, width : width + 3].astype(F32)
    cap_shard = captions.shape[0]
    cap_total = cap_shard * num_sub
    t_rows = text_key_weight.shape[0]
    t_block = num_sub * t_rows
    cap_block = lax.dynamic_slice_in_dim(captions, seq * t_block, t_block, 1)
    cap_block = lax.optimization_barrier((cap_block, packed))[0]
    cap_block = swap_copies(cap_block).reshape(cap_total, t_block)
    text_weight = jnp.stack(
        [
            jnp.concatenate(
                [w[:, i * cols : (i + 1) * cols] for w in (text_key_weight, text_value_weight)], 1
            )
            for i in range(num_sub)
        ]
    )
    text_weight = lax.optimization_barrier((text_weight, cap_block))[0]
    text_weight = swap_blocks(text_weight, "sub").reshape(t_block, 2 * cols)

    video_inv = inv_rms(video_group)
    video_hat = video_group * video_inv
    attn_scale1 = 1.0 + pick_rows(group_hot, scale_rows)
    normed = (video_hat * (attn_gain_f * attn_scale1)).astype(BF)
    qkv_pre = dot(normed, qkv_weight)
    query_pre = qkv_pre[:, :cols]
    key_pre = qkv_pre[:, cols : 2 * cols]
    flow = Flow(
        total_rows(
            jnp.stack([jnp.sum(query_pre * query_pre, 1), jnp.sum(key_pre * key_pre, 1)])
        )
    )
    order.step(flow)
    inverse = lax.rsqrt(flow.result / width + epsilon)
    query_inv = inverse[0].reshape(group, 1)
    key_inv = inverse[1].reshape(group, 1)
    query_hat = query_pre * query_inv
    key_hat = key_pre * key_inv
    cosine, sine = rope_tables(group_pos, head_dim, heads)
    queries = (rotate(query_hat * query_gain_f, cosine, sine).astype(BF) * score_scale).astype(BF)
    keys = rotate(key_hat * key_gain_f, cosine, sine).astype(BF)
    values = qkv_pre[:, 2 * cols :].astype(BF)
    lanes = 2 * head_dim if heads % 2 == 0 else head_dim
    parts = [slice(i * lanes, (i + 1) * lanes) for i in range(cols // lanes)]
    kv = gather_rows(order.tie(jnp.concatenate([keys, values], 1))[0], "seq")

    units = gate_weight.shape[1] // num_seq
    gate_up = jnp.stack(
        [
            jnp.concatenate(
                [w[:, i * units : (i + 1) * units] for w in (gate_weight, up_weight)], 1
            )
            for i in range(num_seq)
        ]
    )
    (gate_up,) = order.tie(gate_up)
    gate_up = swap_blocks(gate_up, "seq").reshape(num_seq * w_rows, 2 * units)
    gate_up = gather_rows(lax.optimization_barrier((gate_up, kv))[0], "sub")
    gate_up = (
        gate_up.reshape(num_sub, num_seq, w_rows, 2 * units)
        .transpose(1, 0, 2, 3)
        .reshape(width, 2 * units)
    )
    down_block = lax.optimization_barrier((down_weight, text_weight))[0]
    down_block = gather_rows(down_block, "sub")

    slots = cap_total // num_seq
    text_parts = {}

    def text_chain():
        part = dot(cap_block, text_weight).astype(BF)
        pre = yield from scatter_seq(part)
        key_pre = pre[:, :cols]
        square = yield from total(jnp.sum(key_pre * key_pre, 1)[None], ("sub",))
        inv = lax.rsqrt(square / width + epsilon).reshape(slots, 1)
        text_parts["inv"], text_parts["hat"] = inv, key_pre * inv
        gain = lax.dynamic_slice_in_dim(
            late_flow.result[3 * clips : 3 * clips + 1], sub * cols, cols, 1
        )
        text_parts["gain"] = gain
        gathered = yield from gather_seq(
            jnp.concatenate([(key_pre * inv * gain).astype(BF), pre[:, cols:].astype(BF)], 1)
        )
        return gathered

    for _ in range(len(axis_bits("seq")) + len(axis_bits("sub")) - 3):
        order.step(late_flow)
    text_flow = Flow(text_chain())
    for _ in range(3):
        order.step(late_flow, text_flow)
    self_out, lse = order.step(
        text_flow,
        work=lambda *a: self_forward(ranges, *a, meta, head_dim, lanes, rows),
        args=(queries, kv),
    )
    while not (text_flow.done and late_flow.done):
        order.step(text_flow, late_flow)
    tkv = text_flow.result
    text_inv, text_hat, text_key_gain_f = (text_parts[k] for k in ("inv", "hat", "gain"))
    late = late_flow.result
    attn_gate = pick_rows(own_hot, late[:clips])
    ffn_scale = pick_rows(own_hot, late[clips : 2 * clips])
    ffn_gate = pick_rows(own_hot, late[2 * clips : 3 * clips])
    attn_out_f = late[3 * clips + 1 : 3 * clips + 2]
    ffn_gain_f = late[3 * clips + 2 : 3 * clips + 3]
    ffn_out_f = late[3 * clips + 3 : 3 * clips + 4]

    mixed_heads, cross_out, cross_lse = cross_forward(
        ranges, gates, queries, tkv, meta, self_out, head_dim, lanes
    )
    flow = Flow(swap_direct([mixed_heads[i * rows : (i + 1) * rows] for i in range(num_sub)]))
    order.step(flow)
    mixed = jnp.concatenate(in_order(flow.result, sub), 1)

    def run(flow):
        while not flow.done:
            order.step(flow)
        return flow.result

    video_own = video.astype(F32)
    projected = dot(mixed, out_full)
    proj_inv = inv_rms(projected)
    proj_hat = projected * proj_inv
    attn_tanh = jnp.tanh(attn_gate)
    hidden_state = video_own + attn_tanh * proj_hat * attn_out_f
    hidden_inv = inv_rms(hidden_state)
    hidden_hat = hidden_state * hidden_inv
    ffn_mult = ffn_gain_f * (1.0 + ffn_scale)
    ffn_in = jnp.concatenate(run(Flow(gather_even_odd((hidden_hat * ffn_mult).astype(BF)))), 0)
    half = ffn_in.shape[0] // 2
    gate_up_pre = dot(ffn_in, gate_up)
    gate_pre = gate_up_pre[:, :units]
    up_pre = gate_up_pre[:, units:]
    gate_sig = jax.nn.sigmoid(gate_pre)
    gate_act = gate_pre * gate_sig
    activated = (gate_act * up_pre).astype(BF)
    down_part = dot(activated, down_block).astype(BF)
    down_out = run(Flow(scatter_even_odd(down_part[:half], down_part[half:])))
    down_inv = inv_rms(down_out)
    down_hat = down_out * down_inv
    ffn_tanh = jnp.tanh(ffn_gate)
    block_out = (hidden_state + ffn_tanh * down_hat * ffn_out_f).astype(BF)

    grad_out = cotangent.astype(F32)
    ffn_gate_grad = grad_out * down_hat * ffn_out_f * (1.0 - ffn_tanh * ffn_tanh)
    ffn_out_gain_part = jnp.sum(grad_out * ffn_tanh * down_hat, 0)
    down_grad = norm_back(down_hat, down_inv, grad_out * ffn_tanh * ffn_out_f).astype(BF)
    down_grad = jnp.concatenate(run(Flow(gather_even_odd(down_grad))), 0)
    act_grad = dot_nt(down_grad, down_block)
    gate_grad = (act_grad * up_pre * gate_sig * (1.0 + gate_pre * (1.0 - gate_sig))).astype(BF)
    up_grad = (act_grad * gate_act).astype(BF)
    gate_up_grad = jnp.concatenate([gate_grad, up_grad], 1)
    ffn_in_part = dot_nt(gate_up_grad, gate_up).astype(BF)
    ffn_in_grad = run(Flow(scatter_even_odd(ffn_in_part[:half], ffn_in_part[half:])))
    down_weight_term = dot_tn(activated, down_grad).astype(BF)
    down_weight_grad = scatter_rows(down_weight_term, "sub").astype(F32)
    gate_up_term = dot_tn(ffn_in, gate_up_grad).astype(BF)
    gate_up_term = (
        gate_up_term.reshape(num_seq, num_sub, w_rows, 2 * units)
        .transpose(1, 0, 2, 3)
        .reshape(width, 2 * units)
    )
    gate_up_term = scatter_rows(gate_up_term, "sub").reshape(num_seq, w_rows, 2 * units)

    ffn_gain_part = jnp.sum(ffn_in_grad * hidden_hat * (1.0 + ffn_scale), 0)
    ffn_scale_grad = ffn_in_grad * hidden_hat * ffn_gain_f
    hidden_grad = grad_out + norm_back(hidden_hat, hidden_inv, ffn_in_grad * ffn_mult)
    attn_gate_grad = hidden_grad * proj_hat * attn_out_f * (1.0 - attn_tanh * attn_tanh)
    attn_out_gain_part = jnp.sum(hidden_grad * attn_tanh * proj_hat, 0)
    proj_grad = norm_back(proj_hat, proj_inv, hidden_grad * attn_tanh * attn_out_f).astype(BF)
    mixed_grad = dot_nt(proj_grad, out_full).astype(BF)
    out_weight_term = dot_tn(mixed, proj_grad).astype(BF)
    flow = Flow(swap_direct(blocks_for(mixed_grad, 1)))
    order.step(flow)
    dout = jnp.concatenate(flow.result, 0)
    cross_gate_part = jnp.sum(
        (dout.astype(F32) * cross_out).reshape(group, heads, head_dim), (0, 2)
    ) * (1.0 - gates * gates)

    def clip_sums(values):
        return dot_tn(own_hot.astype(BF), values.astype(BF))

    def at_columns(part):
        return lax.dynamic_update_slice_in_dim(
            jnp.zeros((1, width), F32), part.reshape(1, -1), sub * cols, 1
        )

    gate_row = lax.dynamic_update_slice_in_dim(
        jnp.zeros((1, width), F32), cross_gate_part.reshape(1, -1), sub * heads, 1
    )
    late_flow = Flow(
        total_cube(
            jnp.concatenate(
                [
                    clip_sums(attn_gate_grad),
                    clip_sums(ffn_scale_grad),
                    clip_sums(ffn_gate_grad),
                    attn_out_gain_part[None],
                    ffn_gain_part[None],
                    ffn_out_gain_part[None],
                    gate_row,
                ],
                0,
            ),
            ("seq", "sub"),
        )
    )
    query_start, dtkv = cross_backward(
        ranges, gates, queries, tkv, meta, dout, cross_lse, head_dim, lanes
    )
    text_flow = Flow(scatter_seq(dtkv))
    def text_back_chain():
        reduced = yield from scatter_seq(dtkv)
        low = reduced[:, :cols].astype(BF).astype(F32)
        hat_grad = low * text_key_gain_f
        inner = yield from total(jnp.sum(text_hat * hat_grad, 1)[None], ("sub",))
        text_parts["gain"] = jnp.sum(low * text_hat, 0)
        pre_grad = text_inv * (hat_grad - text_hat * (inner / width).reshape(slots, 1))
        gathered = yield from gather_seq(
            jnp.concatenate([pre_grad.astype(BF), reduced[:, cols:].astype(BF)], 1)
        )
        return gathered

    text_flow = Flow(text_back_chain())
    query_rot_grad, dkv = order.step(
        text_flow,
        late_flow,
        work=lambda *a: self_backward(ranges, a[0], a[1], meta, *a[2:], head_dim, lanes, rows),
        args=(queries, kv, dout, self_out, lse, query_start),
    )
    dkv = scatter_rows(dkv, "seq")
    out_weight_term = lax.optimization_barrier((out_weight_term, dkv))[0]
    out_weight_grad = scatter_rows(scatter_rows(out_weight_term, "seq"), "sub").astype(F32)
    while not (text_flow.done and late_flow.done):
        order.step(text_flow, late_flow)
    text_key_gain_part = text_parts["gain"]
    text_grad = text_flow.result
    query_rot_grad = query_rot_grad.astype(BF).astype(F32)
    key_rot_grad = dkv[:, :cols].astype(F32)
    value_grad = dkv[:, cols:]
    query_norm_grad = rotate(query_rot_grad, cosine, -sine)
    query_gain_part = jnp.sum(query_norm_grad * query_hat, 0)
    query_hat_grad = query_norm_grad * query_gain_f
    key_norm_grad = rotate(key_rot_grad, cosine, -sine)
    key_gain_part = jnp.sum(key_norm_grad * key_hat, 0)
    key_hat_grad = key_norm_grad * key_gain_f
    flow = Flow(
        total_rows(
            jnp.stack(
                [jnp.sum(query_hat * query_hat_grad, 1), jnp.sum(key_hat * key_hat_grad, 1)]
            )
        )
    )
    order.step(flow)
    inner = flow.result / width
    caption_part = dot_nt(text_grad, text_weight).astype(BF).reshape(num_sub, cap_shard, t_block)
    text_term = dot_tn(cap_block, text_grad).astype(BF).reshape(num_sub, t_rows, 2 * cols)
    query_pre_grad = query_inv * (query_hat_grad - query_hat * inner[0].reshape(group, 1))
    key_pre_grad = key_inv * (key_hat_grad - key_hat * inner[1].reshape(group, 1))
    qkv_grad = jnp.concatenate([query_pre_grad.astype(BF), key_pre_grad.astype(BF), value_grad], 1)
    qkv_term = dot_tn(normed, qkv_grad).astype(BF)
    normed_part = dot_nt(qkv_grad, qkv_weight)

    hat_grad = normed_part * video_hat
    attn_gain_part = jnp.sum(hat_grad * attn_scale1, 0)
    scale_part = dot_tn(group_hot.astype(BF), (hat_grad * attn_gain_f).astype(BF))
    early_flow = Flow(
        total(
            jnp.concatenate(
                [
                    scale_part,
                    attn_gain_part[None],
                    at_columns(query_gain_part),
                    at_columns(key_gain_part),
                    at_columns(text_key_gain_part),
                ],
                0,
            ),
            ("seq", "sub"),
        )
    )
    qkv_flow = Flow(scatter_seq(qkv_term))
    caption_block = jnp.sum(
        swap_blocks(order.tie(caption_part)[0], "sub").astype(F32), 0
    ).astype(BF)
    normed_low = jnp.concatenate(blocks_for(normed_part.astype(BF), 0), 0)
    normed_grad = scatter_rows(order.tie(normed_low)[0], "sub").astype(F32)
    text_term = lax.optimization_barrier((text_term, normed_grad))[0]
    text_term = swap_blocks(text_term, "sub")
    caption_flow = Flow(gather_seq(caption_block, 1, F32))
    order.step(early_flow, qkv_flow)
    order.step(early_flow, qkv_flow)
    order.step(early_flow)
    late_sum = late_flow.result
    early_sum = early_flow.result
    mod_low = jnp.concatenate(
        [
            early_sum[:clips],
            late_sum[:clips],
            late_sum[clips : 2 * clips],
            late_sum[2 * clips : 3 * clips],
        ],
        1,
    ).astype(BF)
    cond_part = lax.dynamic_update_slice_in_dim(
        jnp.zeros(conditioning.shape, F32), dot_nt(mod_low, ada_weight), device * cond_rows, 1
    )
    cond_flow = Flow(total(cond_part, ("seq", "sub")))
    qkv_term = order.tie(qkv_flow.result.astype(BF).reshape(num_sub, w_rows, 3 * cols))[0]
    qkv_term = swap_blocks(qkv_term, "sub")
    order.step(caption_flow)
    order.step(cond_flow, caption_flow)
    order.step(cond_flow)
    order.step(cond_flow)
    caption_grad = caption_flow.result
    query_weight_grad, key_weight_grad, value_weight_grad = (
        jnp.concatenate([block[:, j * cols : (j + 1) * cols] for block in qkv_term], 1).astype(F32)
        for j in range(3)
    )
    text_key_weight_grad, text_value_weight_grad = (
        jnp.concatenate([block[:, j * cols : (j + 1) * cols] for block in text_term], 1).astype(F32)
        for j in range(2)
    )
    gate_up_term = swap_blocks(gate_up_term, "seq")
    gate_weight_grad, up_weight_grad = (
        jnp.concatenate(
            [gate_up_term[i, :, j * units : (j + 1) * units] for i in range(num_seq)], 1
        ).astype(F32)
        for j in range(2)
    )

    own_hat, own_inv, own_scale1 = video_hat[:rows], video_inv[:rows], attn_scale1[:rows]
    video_grad = hidden_grad + norm_back(own_hat, own_inv, normed_grad * (attn_gain_f * own_scale1))

    def own_gain(row):
        return lax.dynamic_slice_in_dim(row, device * gain_rows, gain_rows, 0)

    bias_rows = ada_bias.shape[0]
    ada_bias_grad = jnp.sum(
        lax.dynamic_slice_in_dim(mod_low.astype(F32), device * bias_rows, bias_rows, 1), 0
    )
    ada_weight_grad = dot_tn(cond_slice, mod_low)
    cond_sig = jax.nn.sigmoid(cond_float)
    cond_grad = cond_flow.result * cond_sig * (1.0 + cond_float * (1.0 - cond_sig))
    return (
        block_out,
        video_grad,
        caption_grad,
        cond_grad,
        ada_weight_grad,
        ada_bias_grad,
        query_weight_grad,
        key_weight_grad,
        value_weight_grad,
        out_weight_grad,
        text_key_weight_grad,
        text_value_weight_grad,
        gate_weight_grad,
        up_weight_grad,
        down_weight_grad,
        own_gain(early_sum[clips]),
        own_gain(early_sum[clips + 1]),
        own_gain(early_sum[clips + 2]),
        own_gain(early_sum[clips + 3]),
        own_gain(late_sum[3 * clips]),
        own_gain(late_sum[3 * clips + 1]),
        own_gain(late_sum[3 * clips + 2]),
        late_sum[3 * clips + 3, :heads_total],
    )


def solution(mesh):
    matrix = P(BOTH, None)
    vector = P(BOTH)
    return jax.shard_map(
        body,
        mesh=mesh,
        in_specs=(matrix, P(), P("sub", None), P(), P(), matrix, matrix, vector)
        + (matrix,) * 9
        + (vector,) * 7
        + (P(), matrix),
        out_specs=(matrix, matrix, P("sub", None), P(), matrix, vector)
        + (matrix,) * 9
        + (vector,) * 7
        + (P(),),
        check_vma=False,
    )
```

time: 949 us -> 791 us (0.83); the launches traced: 945 us -> 800 us
  waiting for transfers between devices: 500 us -> 303 us
  starting transfers between devices: 108 us -> 200 us
  local copies, waits for them, and re-layouts: 116 us -> 71.4 us
  other arithmetic: 61.2 us -> 82.2 us
  matrix products: 73.2 us -> 59 us
  blocking collectives: 13.3 us -> 0 us
  Pallas kernels: 52.3 us -> 62.7 us
    all_gather x8 -> x4, waiting for transfers between devices: 175 us -> 31.4 us  [gather_rows(): return lax.all_gather(values, axis, axis=0, tiled=True)]
    ppermute x75 -> x94, starting transfers between devices: 70.8 us -> 166 us  [send(): return lax.ppermute(values, axis, [(i, i ^ mask) for i in range(count)])]
    reduce_scatter x7 -> x6, waiting for transfers between devices: 81.1 us -> 14.4 us  [scatter_rows(): return lax.psum_scatter(values, axis, scatter_dimension=0, tiled=True)]
    reshape x14 -> x0, local copies, waits for them, and re-layouts: 23.1 us -> none  [the longest x1 12.5 us: body(): text_grad.reshape(num_seq, num_sub, slots, 2 * cols).transpose(0, 2, 1, 3)]
    all_to_all x1 -> x0, blocking collectives: 13.3 us -> none  [swap_blocks(): return lax.all_to_all(values, axis, split_axis=0, concat_axis=0, tiled=True)]
    dot_general x1 -> x0, local copies, waits for them, and re-layouts: 10.8 us -> none  [dot_tn(): lax.dot_general(left, right, (((0,), (0,)), ((), ())), preferred_element_...]
    pallas_call x2 -> x8, Pallas kernels: 52.3 us -> 62.7 us  [the longest x4 48.4 us: kernel_call(): pl.pallas_call(kernel, out_shape=tuple((jax.ShapeDtypeStruct(shape, dtype...]
    ppermute x75 -> x94, waiting for transfers between devices: 169 us -> 177 us  [send(): return lax.ppermute(values, axis, [(i, i ^ mask) for i in range(count)])]
  transfers between devices with their start and end apart: 98 -> 112, of which waited for: 66 -> 61; matrix products, arithmetic and copies ran while one was open for 22% -> 19% of each run, Pallas kernels for 3% -> 8%
where the time goes in v2:
time: 791 us; the launch traced here: 800 us
  waiting for transfers between devices  303 us (38%)
  starting transfers between devices  200 us (25%)
  other arithmetic  82.2 us (10%)
  local copies, waits for them, and re-layouts  71.4 us (9%)
  Pallas kernels  62.7 us (8%)
  matrix products  59 us (7%)
  between operations  21.7 us (3%)
    ppermute x94, waiting for transfers between devices, send(): return lax.ppermute(values, axis, [(i, i ^ mask) for i in range(count)])  177 us
    ppermute x94, starting transfers between devices, send(): return lax.ppermute(values, axis, [(i, i ^ mask) for i in range(count)])  166 us
    all_to_all x8, waiting for transfers between devices, swap_blocks(): return lax.all_to_all(values, axis, split_axis=0, concat_axis=0, tiled=True)  79.8 us
    pallas_call x4, Pallas kernels, kernel_call(): pl.pallas_call(kernel, out_shape=tuple((jax.ShapeDtypeStruct(shape, dtype...  48.4 us
    all_to_all x8, starting transfers between devices, swap_blocks(): return lax.all_to_all(values, axis, split_axis=0, concat_axis=0, tiled=True)  33.3 us
    all_gather x4, waiting for transfers between devices, gather_rows(): return lax.all_gather(values, axis, axis=0, tiled=True)  31.4 us
    unnamed x377, local copies, waits for them, and re-layouts  25.5 us
    dot_general x10, matrix products, dot_tn(): lax.dot_general(left, right, (((0,), (0,)), ((), ())), preferred_element_...  22.4 us
  transfers between devices with their start and end apart: 112, of which 61 were waited for; matrix products, arithmetic and copies ran while one was open for 19% of the time, Pallas kernels for 8%

profile of v2, /device:TPU:0, one launch (start us, length us, event | category | flops | bytes accessed | tf_op | source)
XLA Modules:
  0.0 800.4 jit_solution(9994601222435580815)
XLA Ops:
  22.8 7.9 collective-permute-done.1
  38.7 4.6 all-to-all-start
  49.5 5.1 collective-permute-done.6
  70.6 5.2 collective-permute-start.11
  76.3 4.0 shard_map.443
  80.4 4.2 collective-permute-done.11
  112.9 3.9 all-to-all-start.1
  119.4 27.0 %all-to-all-done.1 = bf16[4,320,512]{2,1,0:T(8,128)(2,1)S(1)} async-done(((bf16[4,320,512]{2,1,0:T(8,128)(2,1)}), bf16[4,320,512]{2,1,0:T(8,128)(2,1)S(1)}, u32[]{:S(2)}, u32[]{:S(2)}) %all-to-all-start.1) | async-done | bytes 1310752 | tf_op jit(solution)/shard_map/all_to_all | solution.py:212
  146.4 4.5 all-to-all-start.2
  159.4 11.2 %all-to-all-done.2 = bf16[4,128,768]{2,1,0:T(8,128)(2,1)} async-done(((bf16[4,128,768]{2,1,0:T(8,128)(2,1)}), bf16[4,128,768]{2,1,0:T(8,128)(2,1)}, u32[]{:S(2)}, u32[]{:S(2)}) %all-to-all-start.2) | async-done | bytes 786464 | tf_op jit(solution)/shard_map/all_to_all | solution.py:212
  192.9 4.4 all-to-all-start.3
  212.7 7.7 collective-permute-done.23
  225.0 15.0 %shard_map.444 = (f32[512,384]{1,0:T(8,128)}, f32[8,512]{1,0:T(8,128)}) custom-call(s32[11]{0:T(128)} %concatenate.231.ranges, bf16[512,384]{1,0:T(8,128)(2,1)} %fusion.27.q_ref, bf16[4096,768]{1,0:T(8,128)(2,1)} %all-gather.5.cloned.1.call-done.kv_ref, s32[8,512]{1,0:T(8,128)} %add_add_fusion.5.meta_ref), custom_call_target="tpu_custom_call" | custom-call | flops 12884901888 | bytes 6692864 | tf_op jit(solution)/shard_map/pallas_call | solution.py:556
  246.8 5.5 shard_map.446
  270.5 29.1 %collective-permute-start.34 = (bf16[128,1536]{1,0:T(8,128)(2,1)S(1)}, bf16[128,1536]{1,0:T(8,128)(2,1)S(1)}, u32[]{:S(2)}, u32[]{:S(2)}) collective-permute-start(bf16[128,1536]{1,0:T(8,128)(2,1)S(1)} %get-tuple-element.191), channel_id=1, source_target_pairs={{0,8},{4,12},{8,0},{12,4},{16,24},{20,28},{24,16},{28,20},{1,9},{5... | collective-permute-start | bytes 1179656 | tf_op jit(solution)/shard_map/ppermute | solution.py:34
  301.2 6.7 collective-permute-done.34
  307.9 5.6 collective-permute-done.35
  324.1 3.6 fusion.143
  330.4 31.3 %all-gather.11.cloned.1.call-done = bf16[512,1536]{1,0:T(8,128)(2,1)} async-done(((bf16[128,1536]{1,0:T(8,128)(2,1)}), bf16[512,1536]{1,0:T(8,128)(2,1)}) %all-gather.11.cloned.1.call-update) | async-done | bytes 1572880 | tf_op jit(solution)/shard_map/all_gather | solution.py:220
  372.7 8.5 %collective-permute-done.39 = bf16[128,1536]{1,0:T(8,128)(2,1)S(1)} collective-permute-done((bf16[128,1536]{1,0:T(8,128)(2,1)S(1)}, bf16[128,1536]{1,0:T(8,128)(2,1)S(1)}, u32[]{:S(2)}, u32[]{:S(2)}) %collective-permute-start.39) | collective-permute-done | bytes 393248 | tf_op jit(solution)/shard_map/ppermute | solution.py:34
  381.2 8.8 %collective-permute-done.40 = bf16[128,1536]{1,0:T(8,128)(2,1)S(1)} collective-permute-done((bf16[128,1536]{1,0:T(8,128)(2,1)S(1)}, bf16[128,1536]{1,0:T(8,128)(2,1)S(1)}, u32[]{:S(2)}, u32[]{:S(2)}) %collective-permute-start.40) | collective-permute-done | bytes 393248 | tf_op jit(solution)/shard_map/ppermute | solution.py:34
  396.0 8.6 %collective-permute-done.42 = bf16[128,1536]{1,0:T(8,128)(2,1)S(1)} collective-permute-done((bf16[128,1536]{1,0:T(8,128)(2,1)S(1)}, bf16[128,1536]{1,0:T(8,128)(2,1)S(1)}, u32[]{:S(2)}, u32[]{:S(2)}) %collective-permute-start.42) | collective-permute-done | bytes 393248 | tf_op jit(solution)/shard_map/ppermute | solution.py:34
  404.5 7.6 collective-permute-done.43
  418.3 4.2 convolution_convert_fusion.4
  437.3 4.7 convolution_convert_fusion.3
  446.0 7.9 collective-permute-done.48
  464.2 4.9 collective-permute-done.51
  470.7 6.7 shard_map.447
  479.2 21.1 %shard_map.448 = (f32[512,384]{1,0:T(8,128)}, bf16[4096,768]{1,0:T(8,128)(2,1)}) custom-call(s32[11]{0:T(128)} %concatenate.231.ranges, bf16[512,384]{1,0:T(8,128)(2,1)} %fusion.27.q_ref, bf16[4096,768]{1,0:T(8,128)(2,1)} %all-gather.5.cloned.1.call-done.kv_ref, s32[8,512]{1,0:T(8,128)} %add_add_fusion.5.meta_ref, ...), custom_call_target="tpu_custom_call" | custom-call | flops 25769803776 | bytes 7880704 | tf_op jit(solution)/shard_map/pallas_call | solution.py:556
  504.4 28.7 %collective-permute-start.58 = (f32[19,1536]{1,0:T(8,128)S(1)}, f32[19,1536]{1,0:T(8,128)}, u32[]{:S(2)}, u32[]{:S(2)}) collective-permute-start(f32[19,1536]{1,0:T(8,128)S(1)} %add.654), channel_id=1, source_target_pairs={{0,8},{4,12},{8,0},{12,4},{16,24},{20,28},{24,16},{28,20},{1,9},{5... | collective-permute-start | bytes 350216 | tf_op jit(solution)/shard_map/ppermute | solution.py:34
  536.6 3.7 convolution_convert_fusion
  556.9 4.9 collective-permute-done.62
  567.7 8.8 %collective-permute-done.63 = bf16[160,768]{1,0:T(8,128)(2,1)S(1)} collective-permute-done((bf16[160,768]{1,0:T(8,128)(2,1)S(1)}, bf16[160,768]{1,0:T(8,128)(2,1)S(1)}, u32[]{:S(2)}, u32[]{:S(2)}) %collective-permute-start.63) | collective-permute-done | bytes 245792 | tf_op jit(solution)/shard_map/ppermute | solution.py:34
  576.5 6.0 collective-permute-done.64
  596.2 3.8 convolution_convert_fusion.9
  600.0 4.6 all-to-all-start.6
  611.1 13.5 %all-to-all-done.6 = bf16[4,128,768]{2,1,0:T(8,128)(2,1)} async-done(((bf16[4,128,768]{2,1,0:T(8,128)(2,1)}), bf16[4,128,768]{2,1,0:T(8,128)(2,1)}, u32[]{:S(2)}, u32[]{:S(2)}) %all-to-all-start.6) | async-done | bytes 786464 | tf_op jit(solution)/shard_map/all_to_all | solution.py:212
  626.0 3.6 all-to-all-start.7
  631.8 10.3 %all-to-all-done.7 = bf16[8,48,1024]{2,1,0:T(8,128)(2,1)S(1)} async-done(((bf16[8,48,1024]{2,1,0:T(8,128)(2,1)}), bf16[8,48,1024]{2,1,0:T(8,128)(2,1)S(1)}, u32[]{:S(2)}, u32[]{:S(2)}) %all-to-all-start.7) | async-done | bytes 786464 | tf_op jit(solution)/shard_map/all_to_all | solution.py:212
  647.7 3.5 multiply_reduce_fusion.1
  660.5 7.8 multiply_reduce_fusion
  682.7 4.3 all-to-all-start.4
  700.0 17.8 %all-to-all-done.4 = bf16[4,320,512]{2,1,0:T(8,128)(2,1)} async-done(((bf16[4,320,512]{2,1,0:T(8,128)(2,1)}), bf16[4,320,512]{2,1,0:T(8,128)(2,1)}, u32[]{:S(2)}, u32[]{:S(2)}) %all-to-all-start.4) | async-done | bytes 1310752 | tf_op jit(solution)/shard_map/all_to_all | solution.py:212
  741.4 4.1 collective-permute-done.83
  745.5 4.5 collective-permute-done.84
  761.2 5.9 reduce-scatter.9.cloned.1.call-done
  778.0 4.4 shard_map.450
  783.1 8.5 %reduce-scatter.13.cloned.1.call-done = bf16[48,1536]{1,0:T(8,128)(2,1)} async-done(((bf16[192,1536]{1,0:T(8,128)(2,1)}), bf16[48,1536]{1,0:T(8,128)(2,1)}) %reduce-scatter.13.cloned.1.call-update) | async-done | bytes 147472 | tf_op jit(solution)/shard_map/reduce_scatter | solution.py:224
  (847 shorter events, 360.6 us)
Async XLA Ops:
  33.5 14.2 %collective-permute-start.5 = (bf16[192,1152]{1,0:T(8,128)(2,1)S(1)}, bf16[192,1152]{1,0:T(8,128)(2,1)}, u32[]{:S(2)}, u32[]{:S(2)}) collective-permute-start(bf16[192,1152]{1,0:T(8,128)(2,1)S(1)} %pad_maximum_fusion.18), channel_id=1, source_target_pairs={{0,8},{4,12},{8,0},{12,4},{16,24},{20,28},{24,16},{28,20},{1,9},{5... | collective-permute-start | bytes 1327112 | tf_op jit(solution)/shard_map/ppermute | solution.py:34
  35.8 18.8 %collective-permute-start.6 = (bf16[192,1152]{1,0:T(8,128)(2,1)S(1)}, bf16[192,1152]{1,0:T(8,128)(2,1)}, u32[]{:S(2)}, u32[]{:S(2)}) collective-permute-start(bf16[192,1152]{1,0:T(8,128)(2,1)S(1)} %pad_maximum_fusion.18), channel_id=1, source_target_pairs={{0,16},{4,20},{8,24},{12,28},{16,0},{20,4},{24,8},{28,12},{1,17},{... | collective-permute-start | bytes 1327112 | tf_op jit(solution)/shard_map/ppermute | solution.py:34
  38.7 46.1 %all-to-all-start = ((bf16[4,128,1664]{2,1,0:T(8,128)(2,1)}), bf16[4,128,1664]{2,1,0:T(8,128)(2,1)}, u32[]{:S(2)}, u32[]{:S(2)}) async-start(bf16[4,128,1664]{2,1,0:T(8,128)(2,1)} %broadcast_in_dim.86), calls=%async_computation | async-start | bytes 3407872 | tf_op jit(solution)/shard_map/all_to_all | solution.py:212
  43.3 177.6 %all-gather.5.cloned.1.call-start = ((), (), s32[]{:S(2)}) async-start(), calls=%async_computation.14 | async-start | bytes 7077888 | tf_op jit(solution)/shard_map/all_gather | solution.py:220
  43.3 13.1 %collective-permute-start.7 = (bf16[192,1152]{1,0:T(8,128)(2,1)S(1)}, bf16[192,1152]{1,0:T(8,128)(2,1)S(1)}, u32[]{:S(2)}, u32[]{:S(2)}) collective-permute-start(bf16[192,1152]{1,0:T(8,128)(2,1)S(1)} %pad_maximum_fusion.18), channel_id=1, source_target_pairs={{0,24},{4,28},{8,16},{12,20},{16,8},{20,12},{24,0},{28,4},{1,25},{... | collective-permute-start | bytes 1327112 | tf_op jit(solution)/shard_map/ppermute | solution.py:34
  70.6 13.9 %collective-permute-start.11 = (f32[8,1536]{1,0:T(8,128)S(1)}, f32[8,1536]{1,0:T(8,128)S(1)}, u32[]{:S(2)}, u32[]{:S(2)}) collective-permute-start(f32[8,1536]{1,0:T(8,128)S(1)} %add.577), channel_id=1, source_target_pairs={{0,2},{1,3},{2,0},{3,1},{4,6},{5,7},{6,4},{7,5},{8,10},{9,11},{10,... | collective-permute-start | bytes 147464 | tf_op jit(solution)/shard_map/ppermute | solution.py:34
  110.6 154.7 %all-gather.7.cloned.1.call-start = ((), (), s32[]{:S(2)}) async-start(), calls=%async_computation.15 | async-start | bytes 4866048 | tf_op jit(solution)/shard_map/all_gather | solution.py:220
  112.9 33.5 %all-to-all-start.1 = ((bf16[4,320,512]{2,1,0:T(8,128)(2,1)}), bf16[4,320,512]{2,1,0:T(8,128)(2,1)S(1)}, u32[]{:S(2)}, u32[]{:S(2)}) async-start(bf16[4,320,512]{2,1,0:T(8,128)(2,1)} %broadcast_in_dim.87), calls=%async_computation.1 | async-start | bytes 2621440 | tf_op jit(solution)/shard_map/all_to_all | solution.py:212
  146.4 24.3 %all-to-all-start.2 = ((bf16[4,128,768]{2,1,0:T(8,128)(2,1)}), bf16[4,128,768]{2,1,0:T(8,128)(2,1)}, u32[]{:S(2)}, u32[]{:S(2)}) async-start(bf16[4,128,768]{2,1,0:T(8,128)(2,1)} %pad_maximum_fusion.14), calls=%async_computation.2 | async-start | bytes 1572864 | tf_op jit(solution)/shard_map/all_to_all | solution.py:212
  189.3 13.4 %collective-permute-start.21 = (bf16[160,768]{1,0:T(8,128)(2,1)}, bf16[160,768]{1,0:T(8,128)(2,1)}, u32[]{:S(2)}, u32[]{:S(2)}) collective-permute-start(bf16[160,768]{1,0:T(8,128)(2,1)} %get-tuple-element.170), channel_id=1, source_target_pairs={{0,16},{4,20},{8,24},{12,28},{16,0},{20,4},{24,8},{28,12},{1,17},{... | collective-permute-start | bytes 737288 | tf_op jit(solution)/shard_map/ppermute | solution.py:34
  192.9 47.4 %all-to-all-start.3 = ((bf16[8,48,1024]{2,1,0:T(8,128)(2,1)}), bf16[8,48,1024]{2,1,0:T(8,128)(2,1)}, u32[]{:S(2)}, u32[]{:S(2)}) async-start(bf16[8,48,1024]{2,1,0:T(8,128)(2,1)} %copy-done.50), calls=%async_computation.3 | async-start | bytes 1572864 | tf_op jit(solution)/shard_map/all_to_all | solution.py:212
  197.2 124.0 %all-gather.9.cloned.1.call-start = ((), (), s32[]{:S(2)}) async-start(), calls=%async_computation.16 | async-start | bytes 3932160 | tf_op jit(solution)/shard_map/all_gather | solution.py:220
  220.9 19.1 %collective-permute-start.27 = (bf16[160,768]{1,0:T(8,128)(2,1)S(1)}, bf16[160,768]{1,0:T(8,128)(2,1)S(1)}, u32[]{:S(2)}, u32[]{:S(2)}) collective-permute-start(bf16[160,768]{1,0:T(8,128)(2,1)S(1)} %pad_maximum_fusion.21), channel_id=1, source_target_pairs={{0,8},{4,12},{8,0},{12,4},{16,24},{20,28},{24,16},{28,20},{1,9},{5... | collective-permute-start | bytes 737288 | tf_op jit(solution)/shard_map/ppermute | solution.py:34
  223.3 16.8 %collective-permute-start.28 = (bf16[160,768]{1,0:T(8,128)(2,1)S(1)}, bf16[160,768]{1,0:T(8,128)(2,1)S(1)}, u32[]{:S(2)}, u32[]{:S(2)}) collective-permute-start(bf16[160,768]{1,0:T(8,128)(2,1)S(1)} %pad_maximum_fusion.21), channel_id=1, source_target_pairs={{0,16},{4,20},{8,24},{12,28},{16,0},{20,4},{24,8},{28,12},{1,17},{... | collective-permute-start | bytes 737288 | tf_op jit(solution)/shard_map/ppermute | solution.py:34
  225.0 15.1 %collective-permute-start.29 = (bf16[160,768]{1,0:T(8,128)(2,1)S(1)}, bf16[160,768]{1,0:T(8,128)(2,1)S(1)}, u32[]{:S(2)}, u32[]{:S(2)}) collective-permute-start(bf16[160,768]{1,0:T(8,128)(2,1)S(1)} %pad_maximum_fusion.21), channel_id=1, source_target_pairs={{0,24},{4,28},{8,16},{12,20},{16,8},{20,12},{24,0},{28,4},{1,25},{... | collective-permute-start | bytes 737288 | tf_op jit(solution)/shard_map/ppermute | solution.py:34
  240.3 121.4 %all-gather.11.cloned.1.call-start = ((), (), s32[]{:S(2)}) async-start(), calls=%async_computation.17 | async-start | bytes 1966080 | tf_op jit(solution)/shard_map/all_gather | solution.py:220
  270.5 37.4 %collective-permute-start.34 = (bf16[128,1536]{1,0:T(8,128)(2,1)S(1)}, bf16[128,1536]{1,0:T(8,128)(2,1)S(1)}, u32[]{:S(2)}, u32[]{:S(2)}) collective-permute-start(bf16[128,1536]{1,0:T(8,128)(2,1)S(1)} %get-tuple-element.191), channel_id=1, source_target_pairs={{0,8},{4,12},{8,0},{12,4},{16,24},{20,28},{24,16},{28,20},{1,9},{5... | collective-permute-start | bytes 1179656 | tf_op jit(solution)/shard_map/ppermute | solution.py:34
  299.7 13.9 %collective-permute-start.35 = (bf16[128,1536]{1,0:T(8,128)(2,1)S(1)}, bf16[128,1536]{1,0:T(8,128)(2,1)S(1)}, u32[]{:S(2)}, u32[]{:S(2)}) collective-permute-start(bf16[128,1536]{1,0:T(8,128)(2,1)S(1)} %get-tuple-element.191), channel_id=1, source_target_pairs={{0,16},{4,20},{8,24},{12,28},{16,0},{20,4},{24,8},{28,12},{1,17},{... | collective-permute-start | bytes 1179656 | tf_op jit(solution)/shard_map/ppermute | solution.py:34
  299.7 13.9 %collective-permute-start.36 = (bf16[128,1536]{1,0:T(8,128)(2,1)S(1)}, bf16[128,1536]{1,0:T(8,128)(2,1)S(1)}, u32[]{:S(2)}, u32[]{:S(2)}) collective-permute-start(bf16[128,1536]{1,0:T(8,128)(2,1)S(1)} %get-tuple-element.191), channel_id=1, source_target_pairs={{0,24},{4,28},{8,16},{12,20},{16,8},{20,12},{24,0},{28,4},{1,25},{... | collective-permute-start | bytes 1179656 | tf_op jit(solution)/shard_map/ppermute | solution.py:34
  314.8 271.1 %reduce-scatter.17.cloned.1.call-start = ((), (), s32[]{:S(2)}) async-start(), calls=%async_computation.23 | async-start | bytes 1966080 | tf_op jit(solution)/shard_map/reduce_scatter | solution.py:224
  370.7 19.3 %collective-permute-start.40 = (bf16[128,1536]{1,0:T(8,128)(2,1)S(1)}, bf16[128,1536]{1,0:T(8,128)(2,1)S(1)}, u32[]{:S(2)}, u32[]{:S(2)}) collective-permute-start(bf16[128,1536]{1,0:T(8,128)(2,1)S(1)} %get-tuple-element.198), channel_id=1, source_target_pairs={{0,16},{4,20},{8,24},{12,28},{16,0},{20,4},{24,8},{28,12},{1,17},{... | collective-permute-start | bytes 1179656 | tf_op jit(solution)/shard_map/ppermute | solution.py:34
  372.1 17.8 %collective-permute-start.41 = (bf16[128,1536]{1,0:T(8,128)(2,1)S(1)}, bf16[128,1536]{1,0:T(8,128)(2,1)S(1)}, u32[]{:S(2)}, u32[]{:S(2)}) collective-permute-start(bf16[128,1536]{1,0:T(8,128)(2,1)S(1)} %get-tuple-element.199), channel_id=1, source_target_pairs={{0,24},{4,28},{8,16},{12,20},{16,8},{20,12},{24,0},{28,4},{1,25},{... | collective-permute-start | bytes 1179656 | tf_op jit(solution)/shard_map/ppermute | solution.py:34
  393.7 18.5 %collective-permute-start.43 = (bf16[128,1536]{1,0:T(8,128)(2,1)S(1)}, bf16[128,1536]{1,0:T(8,128)(2,1)S(1)}, u32[]{:S(2)}, u32[]{:S(2)}) collective-permute-start(bf16[128,1536]{1,0:T(8,128)(2,1)S(1)} %get-tuple-element.202), channel_id=1, source_target_pairs={{0,16},{4,20},{8,24},{12,28},{16,0},{20,4},{24,8},{28,12},{1,17},{... | collective-permute-start | bytes 1179656 | tf_op jit(solution)/shard_map/ppermute | solution.py:34
  394.5 17.6 %collective-permute-start.44 = (bf16[128,1536]{1,0:T(8,128)(2,1)S(1)}, bf16[128,1536]{1,0:T(8,128)(2,1)S(1)}, u32[]{:S(2)}, u32[]{:S(2)}) collective-permute-start(bf16[128,1536]{1,0:T(8,128)(2,1)S(1)} %get-tuple-element.202), channel_id=1, source_target_pairs={{0,24},{4,28},{8,16},{12,20},{16,8},{20,12},{24,0},{28,4},{1,25},{... | collective-permute-start | bytes 1179656 | tf_op jit(solution)/shard_map/ppermute | solution.py:34
  428.8 197.1 %reduce-scatter.15.cloned.1.call-start = ((), (), s32[]{:S(2)}) async-start(), calls=%async_computation.22 | async-start | bytes 3932160 | tf_op jit(solution)/shard_map/reduce_scatter | solution.py:224
  434.4 19.6 %collective-permute-start.48 = (bf16[128,1536]{1,0:T(8,128)(2,1)}, bf16[128,1536]{1,0:T(8,128)(2,1)}, u32[]{:S(2)}, u32[]{:S(2)}) collective-permute-start(bf16[128,1536]{1,0:T(8,128)(2,1)} %get-tuple-element.206), channel_id=1, source_target_pairs={{0,16},{4,20},{8,24},{12,28},{16,0},{20,4},{24,8},{28,12},{1,17},{... | collective-permute-start | bytes 1179656 | tf_op jit(solution)/shard_map/ppermute | solution.py:34
  435.5 18.5 %collective-permute-start.49 = (bf16[128,1536]{1,0:T(8,128)(2,1)}, bf16[128,1536]{1,0:T(8,128)(2,1)}, u32[]{:S(2)}, u32[]{:S(2)}) collective-permute-start(bf16[128,1536]{1,0:T(8,128)(2,1)} %get-tuple-element.207), channel_id=1, source_target_pairs={{0,24},{4,28},{8,16},{12,20},{16,8},{20,12},{24,0},{28,4},{1,25},{... | collective-permute-start | bytes 1179656 | tf_op jit(solution)/shard_map/ppermute | solution.py:34
  444.1 199.3 %reduce-scatter.7.cloned.1.call-start = ((), (), s32[]{:S(2)}) async-start(), calls=%async_computation.18 | async-start | bytes 7077888 | tf_op jit(solution)/shard_map/reduce_scatter | solution.py:224
  504.4 35.9 %collective-permute-start.58 = (f32[19,1536]{1,0:T(8,128)S(1)}, f32[19,1536]{1,0:T(8,128)}, u32[]{:S(2)}, u32[]{:S(2)}) collective-permute-start(f32[19,1536]{1,0:T(8,128)S(1)} %add.654), channel_id=1, source_target_pairs={{0,8},{4,12},{8,0},{12,4},{16,24},{20,28},{24,16},{28,20},{1,9},{5... | collective-permute-start | bytes 350216 | tf_op jit(solution)/shard_map/ppermute | solution.py:34
  533.2 13.2 %collective-permute-start.56 = (bf16[160,768]{1,0:T(8,128)(2,1)}, bf16[160,768]{1,0:T(8,128)(2,1)S(1)}, u32[]{:S(2)}, u32[]{:S(2)}) collective-permute-start(bf16[160,768]{1,0:T(8,128)(2,1)} %get-tuple-element.226), channel_id=1, source_target_pairs={{0,16},{4,20},{8,24},{12,28},{16,0},{20,4},{24,8},{28,12},{1,17},{... | collective-permute-start | bytes 737288 | tf_op jit(solution)/shard_map/ppermute | solution.py:34
  533.2 14.0 %collective-permute-start.57 = (bf16[160,768]{1,0:T(8,128)(2,1)}, bf16[160,768]{1,0:T(8,128)(2,1)S(1)}, u32[]{:S(2)}, u32[]{:S(2)}) collective-permute-start(bf16[160,768]{1,0:T(8,128)(2,1)} %get-tuple-element.227), channel_id=1, source_target_pairs={{0,24},{4,28},{8,16},{12,20},{16,8},{20,12},{24,0},{28,4},{1,25},{... | collective-permute-start | bytes 737288 | tf_op jit(solution)/shard_map/ppermute | solution.py:34
  562.7 13.8 %collective-permute-start.63 = (bf16[160,768]{1,0:T(8,128)(2,1)S(1)}, bf16[160,768]{1,0:T(8,128)(2,1)S(1)}, u32[]{:S(2)}, u32[]{:S(2)}) collective-permute-start(bf16[160,768]{1,0:T(8,128)(2,1)S(1)} %pad_maximum_fusion.22), channel_id=1, source_target_pairs={{0,8},{4,12},{8,0},{12,4},{16,24},{20,28},{24,16},{28,20},{1,9},{5... | collective-permute-start | bytes 737288 | tf_op jit(solution)/shard_map/ppermute | solution.py:34
  564.4 18.1 %collective-permute-start.64 = (bf16[160,768]{1,0:T(8,128)(2,1)S(1)}, bf16[160,768]{1,0:T(8,128)(2,1)S(1)}, u32[]{:S(2)}, u32[]{:S(2)}) collective-permute-start(bf16[160,768]{1,0:T(8,128)(2,1)S(1)} %pad_maximum_fusion.22), channel_id=1, source_target_pairs={{0,16},{4,20},{8,24},{12,28},{16,0},{20,4},{24,8},{28,12},{1,17},{... | collective-permute-start | bytes 737288 | tf_op jit(solution)/shard_map/ppermute | solution.py:34
  566.3 16.1 %collective-permute-start.65 = (bf16[160,768]{1,0:T(8,128)(2,1)S(1)}, bf16[160,768]{1,0:T(8,128)(2,1)S(1)}, u32[]{:S(2)}, u32[]{:S(2)}) collective-permute-start(bf16[160,768]{1,0:T(8,128)(2,1)S(1)} %pad_maximum_fusion.22), channel_id=1, source_target_pairs={{0,24},{4,28},{8,16},{12,20},{16,8},{20,12},{24,0},{28,4},{1,25},{... | collective-permute-start | bytes 737288 | tf_op jit(solution)/shard_map/ppermute | solution.py:34
  600.0 24.6 %all-to-all-start.6 = ((bf16[4,128,768]{2,1,0:T(8,128)(2,1)}), bf16[4,128,768]{2,1,0:T(8,128)(2,1)}, u32[]{:S(2)}, u32[]{:S(2)}) async-start(bf16[4,128,768]{2,1,0:T(8,128)(2,1)} %bitcast.319), calls=%async_computation.10 | async-start | bytes 1572864 | tf_op jit(solution)/shard_map/all_to_all | solution.py:212
  626.0 16.1 %all-to-all-start.7 = ((bf16[8,48,1024]{2,1,0:T(8,128)(2,1)}), bf16[8,48,1024]{2,1,0:T(8,128)(2,1)S(1)}, u32[]{:S(2)}, u32[]{:S(2)}) async-start(bf16[8,48,1024]{2,1,0:T(8,128)(2,1)} %bitcast.325), calls=%async_computation.12 | async-start | bytes 1572864 | tf_op jit(solution)/shard_map/all_to_all | solution.py:212
  629.5 131.6 %reduce-scatter.11.cloned.1.call-start = ((), (), s32[]{:S(2)}) async-start(), calls=%async_computation.20 | async-start | bytes 5308416 | tf_op jit(solution)/shard_map/reduce_scatter | solution.py:224
  676.5 14.2 %collective-permute-start.75 = (bf16[768,1152]{1,0:T(8,128)(2,1)}, bf16[768,1152]{1,0:T(8,128)(2,1)}, u32[]{:S(2)}, u32[]{:S(2)}) collective-permute-start(bf16[768,1152]{1,0:T(8,128)(2,1)} %pad_maximum_fusion.1), channel_id=1, source_target_pairs={{0,4},{4,0},{8,12},{12,8},{16,20},{20,16},{24,28},{28,24},{1,5},{5... | collective-permute-start | bytes 5308424 | tf_op jit(solution)/shard_map/ppermute | solution.py:34
  682.7 35.1 %all-to-all-start.4 = ((bf16[4,320,512]{2,1,0:T(8,128)(2,1)}), bf16[4,320,512]{2,1,0:T(8,128)(2,1)}, u32[]{:S(2)}, u32[]{:S(2)}) async-start(bf16[4,320,512]{2,1,0:T(8,128)(2,1)} %bitcast.323), calls=%async_computation.6 | async-start | bytes 2621440 | tf_op jit(solution)/shard_map/all_to_all | solution.py:212
  687.1 80.0 %reduce-scatter.9.cloned.1.call-start = ((), (), s32[]{:S(2)}) async-start(), calls=%async_computation.19 | async-start | bytes 1966080 | tf_op jit(solution)/shard_map/reduce_scatter | solution.py:224
  693.8 25.7 %collective-permute-start.77 = (bf16[192,1152]{1,0:T(8,128)(2,1)}, bf16[192,1152]{1,0:T(8,128)(2,1)S(1)}, u32[]{:S(2)}, u32[]{:S(2)}) collective-permute-start(bf16[192,1152]{1,0:T(8,128)(2,1)} %get-tuple-element.249), channel_id=1, source_target_pairs={{0,8},{4,12},{8,0},{12,4},{16,24},{20,28},{24,16},{28,20},{1,9},{5... | collective-permute-start | bytes 1327112 | tf_op jit(solution)/shard_map/ppermute | solution.py:34
  693.9 25.6 %collective-permute-start.78 = (bf16[192,1152]{1,0:T(8,128)(2,1)}, bf16[192,1152]{1,0:T(8,128)(2,1)S(1)}, u32[]{:S(2)}, u32[]{:S(2)}) collective-permute-start(bf16[192,1152]{1,0:T(8,128)(2,1)} %get-tuple-element.250), channel_id=1, source_target_pairs={{0,16},{4,20},{8,24},{12,28},{16,0},{20,4},{24,8},{28,12},{1,17},{... | collective-permute-start | bytes 1327112 | tf_op jit(solution)/shard_map/ppermute | solution.py:34
  695.8 26.0 %collective-permute-start.79 = (bf16[192,1152]{1,0:T(8,128)(2,1)}, bf16[192,1152]{1,0:T(8,128)(2,1)}, u32[]{:S(2)}, u32[]{:S(2)}) collective-permute-start(bf16[192,1152]{1,0:T(8,128)(2,1)} %get-tuple-element.251), channel_id=1, source_target_pairs={{0,24},{4,28},{8,16},{12,20},{16,8},{20,12},{24,0},{28,4},{1,25},{... | collective-permute-start | bytes 1327112 | tf_op jit(solution)/shard_map/ppermute | solution.py:34
  731.5 27.3 %all-to-all-start.5 = ((bf16[4,48,1152]{2,1,0:T(8,128)(2,1)}), bf16[4,48,1152]{2,1,0:T(8,128)(2,1)S(1)}, u32[]{:S(2)}, u32[]{:S(2)}) async-start(bf16[4,48,1152]{2,1,0:T(8,128)(2,1)} %bitcast.102), calls=%async_computation.7 | async-start | bytes 884736 | tf_op jit(solution)/shard_map/all_to_all | solution.py:212
  735.0 56.5 %reduce-scatter.13.cloned.1.call-start = ((), (), s32[]{:S(2)}) async-start(), calls=%async_computation.21 | async-start | bytes 737280 | tf_op jit(solution)/shard_map/reduce_scatter | solution.py:224
  736.4 13.6 %collective-permute-start.84 = (bf16[320,512]{1,0:T(8,128)(2,1)S(1)}, bf16[320,512]{1,0:T(8,128)(2,1)S(1)}, u32[]{:S(2)}, u32[]{:S(2)}) collective-permute-start(bf16[320,512]{1,0:T(8,128)(2,1)S(1)} %reduce_sum.276), channel_id=1, source_target_pairs={{0,16},{4,20},{8,24},{12,28},{16,0},{20,4},{24,8},{28,12},{1,17},{... | collective-permute-start | bytes 983048 | tf_op jit(solution)/shard_map/ppermute | solution.py:34
  737.0 13.7 %collective-permute-start.85 = (bf16[320,512]{1,0:T(8,128)(2,1)S(1)}, bf16[320,512]{1,0:T(8,128)(2,1)S(1)}, u32[]{:S(2)}, u32[]{:S(2)}) collective-permute-start(bf16[320,512]{1,0:T(8,128)(2,1)S(1)} %reduce_sum.276), channel_id=1, source_target_pairs={{0,24},{4,28},{8,16},{12,20},{16,8},{20,12},{24,0},{28,4},{1,25},{... | collective-permute-start | bytes 983048 | tf_op jit(solution)/shard_map/ppermute | solution.py:34
  755.5 13.2 %collective-permute-start.86 = (bf16[1280,512]{1,0:T(8,128)(2,1)S(1)}, bf16[1280,512]{1,0:T(8,128)(2,1)}, u32[]{:S(2)}, u32[]{:S(2)}) collective-permute-start(bf16[1280,512]{1,0:T(8,128)(2,1)S(1)} %pad_maximum_fusion.8.even_ref), channel_id=1, source_target_pairs={{0,4},{4,0},{8,12},{12,8},{16,20},{20,16},{24,28},{28,24},{1,5},{5... | collective-permute-start | bytes 3932168 | tf_op jit(solution)/shard_map/ppermute | solution.py:34
  (244 other events, 2264.6 us)
Sparse Core Ops, SparseCore 0:
  110.7 44.7 all-gather.4
  158.3 69.1 all-gather.6
  240.4 75.8 all-gather.8
  317.8 43.8 all-gather.10
  429.0 32.9 reduce-scatter.16
  464.1 59.8 reduce-scatter.14
  527.4 75.3 reduce-scatter.6
  655.8 64.5 reduce-scatter.10
  722.7 44.2 reduce-scatter.8
  769.2 22.2 reduce-scatter.12

commit v3 on v2

--- a/solution.py
+++ b/solution.py
@@ -738,7 +738,7 @@
     packed = jnp.concatenate(
         [video, jnp.pad(positions.astype(BF), ((0, 0), (0, 128 - positions.shape[1])))], 1
     )
-    packed = swap_copies(order.tie(packed)[0]).reshape(num_sub * rows, -1)
+    packed = gather_rows(order.tie(packed)[0], "sub")
     flow = Flow(gather_seq(jnp.concatenate(in_order(flow.result, sub), 0)))
     while not (flow.done and early_flow.done):
         order.step(flow, early_flow)

time: 791 us -> 780 us (0.986)
  starting transfers between devices: 200 us -> 176 us
  waiting for transfers between devices: 303 us -> 313 us
    ppermute x94, starting transfers between devices: 166 us -> 146 us  [send(): return lax.ppermute(values, axis, [(i, i ^ mask) for i in range(count)])]
    ppermute x94, waiting for transfers between devices: 177 us -> 186 us  [send(): return lax.ppermute(values, axis, [(i, i ^ mask) for i in range(count)])]
    all_to_all x8 -> x7, starting transfers between devices: 33.3 us -> 29.4 us  [swap_blocks(): return lax.all_to_all(values, axis, split_axis=0, concat_axis=0, tiled=True)]
    all_gather x4 -> x5, waiting for transfers between devices: 31.4 us -> 33.4 us  [gather_rows(): return lax.all_gather(values, axis, axis=0, tiled=True)]
    all_to_all x8 -> x7, waiting for transfers between devices: 79.8 us -> 79.5 us  [swap_blocks(): return lax.all_to_all(values, axis, split_axis=0, concat_axis=0, tiled=True)]
  transfers between devices with their start and end apart: 112 -> 112, of which waited for: 61 -> 60; matrix products, arithmetic and copies ran while one was open for 19% -> 19% of each run, Pallas kernels for 8% -> 8%
where the time goes in v3:
time: 780 us; the launch traced here: 784 us
  waiting for transfers between devices  313 us (40%)
  starting transfers between devices  176 us (23%)
  other arithmetic  83.3 us (11%)
  local copies, waits for them, and re-layouts  70 us (9%)
  Pallas kernels  59.6 us (8%)
  matrix products  59.4 us (8%)
  between operations  21.4 us (3%)
    ppermute x94, waiting for transfers between devices, send(): return lax.ppermute(values, axis, [(i, i ^ mask) for i in range(count)])  186 us
    ppermute x94, starting transfers between devices, send(): return lax.ppermute(values, axis, [(i, i ^ mask) for i in range(count)])  146 us
    all_to_all x7, waiting for transfers between devices, swap_blocks(): return lax.all_to_all(values, axis, split_axis=0, concat_axis=0, tiled=True)  79.5 us
    pallas_call x4, Pallas kernels, kernel_call(): pl.pallas_call(kernel, out_shape=tuple((jax.ShapeDtypeStruct(shape, dtype...  45.3 us
    all_gather x5, waiting for transfers between devices, gather_rows(): return lax.all_gather(values, axis, axis=0, tiled=True)  33.4 us
    all_to_all x7, starting transfers between devices, swap_blocks(): return lax.all_to_all(values, axis, split_axis=0, concat_axis=0, tiled=True)  29.4 us
    unnamed x377, local copies, waits for them, and re-layouts  25.4 us
    dot_general x10, matrix products, dot_tn(): lax.dot_general(left, right, (((0,), (0,)), ((), ())), preferred_element_...  22.8 us
  transfers between devices with their start and end apart: 112, of which 60 were waited for; matrix products, arithmetic and copies ran while one was open for 19% of the time, Pallas kernels for 8%

profile of v3, /device:TPU:0, one launch (start us, length us, event | category | flops | bytes accessed | tf_op | source)
XLA Modules:
  0.0 783.6 jit_solution(18385197207866608728)
XLA Ops:
  22.8 7.9 %collective-permute-done.1 = bf16[48,1152]{1,0:T(8,128)(2,1)S(1)} collective-permute-done((bf16[48,1152]{1,0:T(8,128)(2,1)S(1)}, bf16[48,1152]{1,0:T(8,128)(2,1)S(1)}, u32[]{:S(2)}, u32[]{:S(2)}) %collective-permute-start.1) | collective-permute-done | bytes 110624 | tf_op jit(solution)/shard_map/ppermute | solution.py:34
  39.8 8.1 %collective-permute-done.4 = f32[8,1536]{1,0:T(8,128)} collective-permute-done((f32[8,1536]{1,0:T(8,128)S(1)}, f32[8,1536]{1,0:T(8,128)}, u32[]{:S(2)}, u32[]{:S(2)}) %collective-permute-start.4) | collective-permute-done | bytes 49184 | tf_op jit(solution)/shard_map/ppermute | solution.py:34
  50.5 4.2 collective-permute-done.6
  67.1 5.8 collective-permute-done.10
  74.3 4.0 shard_map.443
  107.9 3.8 all-to-all-start
  114.4 27.0 %all-to-all-done = bf16[4,320,512]{2,1,0:T(8,128)(2,1)S(1)} async-done(((bf16[4,320,512]{2,1,0:T(8,128)(2,1)}), bf16[4,320,512]{2,1,0:T(8,128)(2,1)S(1)}, u32[]{:S(2)}, u32[]{:S(2)}) %all-to-all-start) | async-done | bytes 1310752 | tf_op jit(solution)/shard_map/all_to_all | solution.py:212
  141.4 4.5 all-to-all-start.1
  154.6 11.1 %all-to-all-done.1 = bf16[4,128,768]{2,1,0:T(8,128)(2,1)} async-done(((bf16[4,128,768]{2,1,0:T(8,128)(2,1)}), bf16[4,128,768]{2,1,0:T(8,128)(2,1)}, u32[]{:S(2)}, u32[]{:S(2)}) %all-to-all-start.1) | async-done | bytes 786464 | tf_op jit(solution)/shard_map/all_to_all | solution.py:212
  188.7 4.3 all-to-all-start.2
  208.9 8.5 %collective-permute-done.23 = f32[19,1536]{1,0:T(8,128)S(1)} collective-permute-done((f32[19,1536]{1,0:T(8,128)S(1)}, f32[19,1536]{1,0:T(8,128)S(1)}, u32[]{:S(2)}, u32[]{:S(2)}) %collective-permute-start.23) | collective-permute-done | bytes 116768 | tf_op jit(solution)/shard_map/ppermute | solution.py:34
  219.6 4.6 collective-permute-start.28
  224.2 11.3 %shard_map.444 = (f32[512,384]{1,0:T(8,128)}, f32[8,512]{1,0:T(8,128)}) custom-call(s32[11]{0:T(128)} %concatenate.231.ranges, bf16[512,384]{1,0:T(8,128)(2,1)} %fusion.27.q_ref, bf16[4096,768]{1,0:T(8,128)(2,1)} %all-gather.8.cloned.1.call-done.kv_ref, s32[8,512]{1,0:T(8,128)} %add_add_fusion.5.meta_ref), custom_call_target="tpu_custom_call" | custom-call | flops 12884901888 | bytes 6692864 | tf_op jit(solution)/shard_map/pallas_call | solution.py:556
  242.2 7.9 %shard_map.446 = (bf16[512,384]{1,0:T(8,128)(2,1)}, f32[512,384]{1,0:T(8,128)}, f32[8,512]{1,0:T(8,128)}) custom-call(s32[11]{0:T(128)} %concatenate.231.ranges, f32[6]{0:T(128)} %dynamic_slice.170.gates, bf16[512,384]{1,0:T(8,128)(2,1)} %fusion.27.q_ref, bf16[1280,768]{1,0:T(8,128)(2,1)} %shard_map.445.tkv_ref, s32[8,512]{1,0:T(8,128)} %add_add_fusion.5.meta_ref, ...), custom_call_target="tpu_custom_call" | custom-call | flops 805306368 | bytes 2760704 | tf_op jit(solution)/shard_map/pallas_call | solution.py:556
  258.7 6.3 collective-permute-done.32
  271.2 20.7 %collective-permute-start.34 = (bf16[128,1536]{1,0:T(8,128)(2,1)S(1)}, bf16[128,1536]{1,0:T(8,128)(2,1)S(1)}, u32[]{:S(2)}, u32[]{:S(2)}) collective-permute-start(bf16[128,1536]{1,0:T(8,128)(2,1)S(1)} %get-tuple-element.191), channel_id=1, source_target_pairs={{0,8},{4,12},{8,0},{12,4},{16,24},{20,28},{24,16},{28,20},{1,9},{5... | collective-permute-start | bytes 1179656 | tf_op jit(solution)/shard_map/ppermute | solution.py:34
  293.5 8.3 %collective-permute-done.34 = bf16[128,1536]{1,0:T(8,128)(2,1)S(1)} collective-permute-done((bf16[128,1536]{1,0:T(8,128)(2,1)S(1)}, bf16[128,1536]{1,0:T(8,128)(2,1)S(1)}, u32[]{:S(2)}, u32[]{:S(2)}) %collective-permute-start.34) | collective-permute-done | bytes 393248 | tf_op jit(solution)/shard_map/ppermute | solution.py:34
  301.8 6.0 collective-permute-done.35
  318.5 3.6 fusion.143
  324.7 33.3 %all-gather.14.cloned.1.call-done = bf16[512,1536]{1,0:T(8,128)(2,1)} async-done(((bf16[128,1536]{1,0:T(8,128)(2,1)}), bf16[512,1536]{1,0:T(8,128)(2,1)}) %all-gather.14.cloned.1.call-update) | async-done | bytes 1572880 | tf_op jit(solution)/shard_map/all_gather | solution.py:220
  369.0 8.5 %collective-permute-done.39 = bf16[128,1536]{1,0:T(8,128)(2,1)S(1)} collective-permute-done((bf16[128,1536]{1,0:T(8,128)(2,1)S(1)}, bf16[128,1536]{1,0:T(8,128)(2,1)S(1)}, u32[]{:S(2)}, u32[]{:S(2)}) %collective-permute-start.39) | collective-permute-done | bytes 393248 | tf_op jit(solution)/shard_map/ppermute | solution.py:34
  377.5 8.8 %collective-permute-done.40 = bf16[128,1536]{1,0:T(8,128)(2,1)S(1)} collective-permute-done((bf16[128,1536]{1,0:T(8,128)(2,1)S(1)}, bf16[128,1536]{1,0:T(8,128)(2,1)S(1)}, u32[]{:S(2)}, u32[]{:S(2)}) %collective-permute-start.40) | collective-permute-done | bytes 393248 | tf_op jit(solution)/shard_map/ppermute | solution.py:34
  392.3 8.6 %collective-permute-done.42 = bf16[128,1536]{1,0:T(8,128)(2,1)S(1)} collective-permute-done((bf16[128,1536]{1,0:T(8,128)(2,1)S(1)}, bf16[128,1536]{1,0:T(8,128)(2,1)S(1)}, u32[]{:S(2)}, u32[]{:S(2)}) %collective-permute-start.42) | collective-permute-done | bytes 393248 | tf_op jit(solution)/shard_map/ppermute | solution.py:34
  400.8 7.6 collective-permute-done.43
  414.6 4.2 convolution_convert_fusion.4
  433.6 4.7 convolution_convert_fusion.3
  442.4 7.9 %collective-permute-done.48 = bf16[128,1536]{1,0:T(8,128)(2,1)} collective-permute-done((bf16[128,1536]{1,0:T(8,128)(2,1)}, bf16[128,1536]{1,0:T(8,128)(2,1)}, u32[]{:S(2)}, u32[]{:S(2)}) %collective-permute-start.48) | collective-permute-done | bytes 393248 | tf_op jit(solution)/shard_map/ppermute | solution.py:34
  460.6 4.9 collective-permute-done.51
  467.0 9.7 %shard_map.447 = (f32[384,512]{1,0:T(8,128)}, bf16[1280,768]{1,0:T(8,128)(2,1)}) custom-call(s32[11]{0:T(128)} %concatenate.231.ranges, f32[6]{0:T(128)} %dynamic_slice.170.gates, bf16[512,384]{1,0:T(8,128)(2,1)} %fusion.27.q_ref, bf16[1280,768]{1,0:T(8,128)(2,1)} %shard_map.445.tkv_ref, s32[8,512]{1,0:T(8,128)} %add_add_fusion.5.meta_ref, ...), custom_call_target="tpu_custom_call" | custom-call | flops 1610612736 | bytes 2768896 | tf_op jit(solution)/shard_map/pallas_call | solution.py:556
  478.6 16.4 %shard_map.448 = (f32[512,384]{1,0:T(8,128)}, bf16[4096,768]{1,0:T(8,128)(2,1)}) custom-call(s32[11]{0:T(128)} %concatenate.231.ranges, bf16[512,384]{1,0:T(8,128)(2,1)} %fusion.27.q_ref, bf16[4096,768]{1,0:T(8,128)(2,1)} %all-gather.8.cloned.1.call-done.kv_ref, s32[8,512]{1,0:T(8,128)} %add_add_fusion.5.meta_ref, ...), custom_call_target="tpu_custom_call" | custom-call | flops 25769803776 | bytes 7880704 | tf_op jit(solution)/shard_map/pallas_call | solution.py:556
  500.5 18.4 %collective-permute-start.58 = (f32[19,1536]{1,0:T(8,128)S(1)}, f32[19,1536]{1,0:T(8,128)}, u32[]{:S(2)}, u32[]{:S(2)}) collective-permute-start(f32[19,1536]{1,0:T(8,128)S(1)} %add.654), channel_id=1, source_target_pairs={{0,8},{4,12},{8,0},{12,4},{16,24},{20,28},{24,16},{28,20},{1,9},{5... | collective-permute-start | bytes 350216 | tf_op jit(solution)/shard_map/ppermute | solution.py:34
  522.3 3.6 convolution_convert_fusion
  528.7 5.4 collective-permute-done.57
  550.4 7.7 collective-permute-done.63
  560.7 4.9 collective-permute-done.65
  579.0 4.2 convolution_convert_fusion.9
  583.2 4.2 all-to-all-start.5
  593.9 13.3 %all-to-all-done.5 = bf16[4,128,768]{2,1,0:T(8,128)(2,1)} async-done(((bf16[4,128,768]{2,1,0:T(8,128)(2,1)}), bf16[4,128,768]{2,1,0:T(8,128)(2,1)}, u32[]{:S(2)}, u32[]{:S(2)}) %all-to-all-start.5) | async-done | bytes 786464 | tf_op jit(solution)/shard_map/all_to_all | solution.py:212
  608.5 4.7 all-to-all-start.6
  615.4 10.4 %all-to-all-done.6 = bf16[8,48,1024]{2,1,0:T(8,128)(2,1)S(1)} async-done(((bf16[8,48,1024]{2,1,0:T(8,128)(2,1)}), bf16[8,48,1024]{2,1,0:T(8,128)(2,1)S(1)}, u32[]{:S(2)}, u32[]{:S(2)}) %all-to-all-start.6) | async-done | bytes 786464 | tf_op jit(solution)/shard_map/all_to_all | solution.py:212
  644.2 7.8 multiply_reduce_fusion
  666.5 4.3 all-to-all-start.3
  683.8 17.8 %all-to-all-done.3 = bf16[4,320,512]{2,1,0:T(8,128)(2,1)} async-done(((bf16[4,320,512]{2,1,0:T(8,128)(2,1)}), bf16[4,320,512]{2,1,0:T(8,128)(2,1)}, u32[]{:S(2)}, u32[]{:S(2)}) %all-to-all-start.3) | async-done | bytes 1310752 | tf_op jit(solution)/shard_map/all_to_all | solution.py:212
  725.1 4.2 collective-permute-done.83
  729.3 4.6 collective-permute-done.84
  745.0 5.5 reduce-scatter.9.cloned.1.call-done
  761.4 4.4 shard_map.450
  766.5 8.5 %reduce-scatter.13.cloned.1.call-done = bf16[48,1536]{1,0:T(8,128)(2,1)} async-done(((bf16[192,1536]{1,0:T(8,128)(2,1)}), bf16[48,1536]{1,0:T(8,128)(2,1)}) %reduce-scatter.13.cloned.1.call-update) | async-done | bytes 147472 | tf_op jit(solution)/shard_map/reduce_scatter | solution.py:224
  (847 shorter events, 355.9 us)
Async XLA Ops:
  7.2 72.7 %all-gather.6.cloned.1.call-start = ((), (), s32[]{:S(2)}) async-start(), calls=%async_computation.13 | async-start | bytes 2129920 | tf_op jit(solution)/shard_map/all_gather | solution.py:220
  33.6 15.1 %collective-permute-start.5 = (bf16[192,1152]{1,0:T(8,128)(2,1)S(1)}, bf16[192,1152]{1,0:T(8,128)(2,1)}, u32[]{:S(2)}, u32[]{:S(2)}) collective-permute-start(bf16[192,1152]{1,0:T(8,128)(2,1)S(1)} %pad_maximum_fusion.18), channel_id=1, source_target_pairs={{0,8},{4,12},{8,0},{12,4},{16,24},{20,28},{24,16},{28,20},{1,9},{5... | collective-permute-start | bytes 1327112 | tf_op jit(solution)/shard_map/ppermute | solution.py:34
  35.3 12.6 %collective-permute-start.4 = (f32[8,1536]{1,0:T(8,128)S(1)}, f32[8,1536]{1,0:T(8,128)}, u32[]{:S(2)}, u32[]{:S(2)}) collective-permute-start(f32[8,1536]{1,0:T(8,128)S(1)} %fusion.171), channel_id=1, source_target_pairs={{0,8},{4,12},{8,0},{12,4},{16,24},{20,28},{24,16},{28,20},{1,9},{5... | collective-permute-start | bytes 147464 | tf_op jit(solution)/shard_map/ppermute | solution.py:34
  35.9 18.8 %collective-permute-start.6 = (bf16[192,1152]{1,0:T(8,128)(2,1)S(1)}, bf16[192,1152]{1,0:T(8,128)(2,1)}, u32[]{:S(2)}, u32[]{:S(2)}) collective-permute-start(bf16[192,1152]{1,0:T(8,128)(2,1)S(1)} %pad_maximum_fusion.18), channel_id=1, source_target_pairs={{0,16},{4,20},{8,24},{12,28},{16,0},{20,4},{24,8},{28,12},{1,17},{... | collective-permute-start | bytes 1327112 | tf_op jit(solution)/shard_map/ppermute | solution.py:34
  38.2 179.6 %all-gather.8.cloned.1.call-start = ((), (), s32[]{:S(2)}) async-start(), calls=%async_computation.14 | async-start | bytes 7077888 | tf_op jit(solution)/shard_map/all_gather | solution.py:220
  38.3 18.2 %collective-permute-start.7 = (bf16[192,1152]{1,0:T(8,128)(2,1)S(1)}, bf16[192,1152]{1,0:T(8,128)(2,1)S(1)}, u32[]{:S(2)}, u32[]{:S(2)}) collective-permute-start(bf16[192,1152]{1,0:T(8,128)(2,1)S(1)} %pad_maximum_fusion.18), channel_id=1, source_target_pairs={{0,24},{4,28},{8,16},{12,20},{16,8},{20,12},{24,0},{28,4},{1,25},{... | collective-permute-start | bytes 1327112 | tf_op jit(solution)/shard_map/ppermute | solution.py:34
  105.7 160.3 %all-gather.10.cloned.1.call-start = ((), (), s32[]{:S(2)}) async-start(), calls=%async_computation.15 | async-start | bytes 4866048 | tf_op jit(solution)/shard_map/all_gather | solution.py:220
  107.9 33.5 %all-to-all-start = ((bf16[4,320,512]{2,1,0:T(8,128)(2,1)}), bf16[4,320,512]{2,1,0:T(8,128)(2,1)S(1)}, u32[]{:S(2)}, u32[]{:S(2)}) async-start(bf16[4,320,512]{2,1,0:T(8,128)(2,1)} %broadcast_in_dim.80), calls=%async_computation | async-start | bytes 2621440 | tf_op jit(solution)/shard_map/all_to_all | solution.py:212
  141.4 24.2 %all-to-all-start.1 = ((bf16[4,128,768]{2,1,0:T(8,128)(2,1)}), bf16[4,128,768]{2,1,0:T(8,128)(2,1)}, u32[]{:S(2)}, u32[]{:S(2)}) async-start(bf16[4,128,768]{2,1,0:T(8,128)(2,1)} %pad_maximum_fusion.14), calls=%async_computation.1 | async-start | bytes 1572864 | tf_op jit(solution)/shard_map/all_to_all | solution.py:212
  183.6 13.2 %collective-permute-start.20 = (bf16[160,768]{1,0:T(8,128)(2,1)}, bf16[160,768]{1,0:T(8,128)(2,1)}, u32[]{:S(2)}, u32[]{:S(2)}) collective-permute-start(bf16[160,768]{1,0:T(8,128)(2,1)} %get-tuple-element.169), channel_id=1, source_target_pairs={{0,8},{4,12},{8,0},{12,4},{16,24},{20,28},{24,16},{28,20},{1,9},{5... | collective-permute-start | bytes 737288 | tf_op jit(solution)/shard_map/ppermute | solution.py:34
  185.0 14.1 %collective-permute-start.21 = (bf16[160,768]{1,0:T(8,128)(2,1)}, bf16[160,768]{1,0:T(8,128)(2,1)}, u32[]{:S(2)}, u32[]{:S(2)}) collective-permute-start(bf16[160,768]{1,0:T(8,128)(2,1)} %get-tuple-element.170), channel_id=1, source_target_pairs={{0,16},{4,20},{8,24},{12,28},{16,0},{20,4},{24,8},{28,12},{1,17},{... | collective-permute-start | bytes 737288 | tf_op jit(solution)/shard_map/ppermute | solution.py:34
  185.8 13.3 %collective-permute-start.22 = (bf16[160,768]{1,0:T(8,128)(2,1)}, bf16[160,768]{1,0:T(8,128)(2,1)}, u32[]{:S(2)}, u32[]{:S(2)}) collective-permute-start(bf16[160,768]{1,0:T(8,128)(2,1)} %get-tuple-element.171), channel_id=1, source_target_pairs={{0,24},{4,28},{8,16},{12,20},{16,8},{20,12},{24,0},{28,4},{1,25},{... | collective-permute-start | bytes 737288 | tf_op jit(solution)/shard_map/ppermute | solution.py:34
  188.7 47.0 %all-to-all-start.2 = ((bf16[8,48,1024]{2,1,0:T(8,128)(2,1)}), bf16[8,48,1024]{2,1,0:T(8,128)(2,1)}, u32[]{:S(2)}, u32[]{:S(2)}) async-start(bf16[8,48,1024]{2,1,0:T(8,128)(2,1)} %copy-done.50), calls=%async_computation.2 | async-start | bytes 1572864 | tf_op jit(solution)/shard_map/all_to_all | solution.py:212
  193.0 122.6 %all-gather.12.cloned.1.call-start = ((), (), s32[]{:S(2)}) async-start(), calls=%async_computation.16 | async-start | bytes 3932160 | tf_op jit(solution)/shard_map/all_gather | solution.py:220
  217.9 17.6 %collective-permute-start.27 = (bf16[160,768]{1,0:T(8,128)(2,1)S(1)}, bf16[160,768]{1,0:T(8,128)(2,1)S(1)}, u32[]{:S(2)}, u32[]{:S(2)}) collective-permute-start(bf16[160,768]{1,0:T(8,128)(2,1)S(1)} %pad_maximum_fusion.21), channel_id=1, source_target_pairs={{0,8},{4,12},{8,0},{12,4},{16,24},{20,28},{24,16},{28,20},{1,9},{5... | collective-permute-start | bytes 737288 | tf_op jit(solution)/shard_map/ppermute | solution.py:34
  219.6 15.9 %collective-permute-start.28 = (bf16[160,768]{1,0:T(8,128)(2,1)S(1)}, bf16[160,768]{1,0:T(8,128)(2,1)S(1)}, u32[]{:S(2)}, u32[]{:S(2)}) collective-permute-start(bf16[160,768]{1,0:T(8,128)(2,1)S(1)} %pad_maximum_fusion.21), channel_id=1, source_target_pairs={{0,16},{4,20},{8,24},{12,28},{16,0},{20,4},{24,8},{28,12},{1,17},{... | collective-permute-start | bytes 737288 | tf_op jit(solution)/shard_map/ppermute | solution.py:34
  235.7 122.3 %all-gather.14.cloned.1.call-start = ((), (), s32[]{:S(2)}) async-start(), calls=%async_computation.17 | async-start | bytes 1966080 | tf_op jit(solution)/shard_map/all_gather | solution.py:220
  271.2 30.6 %collective-permute-start.34 = (bf16[128,1536]{1,0:T(8,128)(2,1)S(1)}, bf16[128,1536]{1,0:T(8,128)(2,1)S(1)}, u32[]{:S(2)}, u32[]{:S(2)}) collective-permute-start(bf16[128,1536]{1,0:T(8,128)(2,1)S(1)} %get-tuple-element.191), channel_id=1, source_target_pairs={{0,8},{4,12},{8,0},{12,4},{16,24},{20,28},{24,16},{28,20},{1,9},{5... | collective-permute-start | bytes 1179656 | tf_op jit(solution)/shard_map/ppermute | solution.py:34
  291.9 15.9 %collective-permute-start.35 = (bf16[128,1536]{1,0:T(8,128)(2,1)S(1)}, bf16[128,1536]{1,0:T(8,128)(2,1)S(1)}, u32[]{:S(2)}, u32[]{:S(2)}) collective-permute-start(bf16[128,1536]{1,0:T(8,128)(2,1)S(1)} %get-tuple-element.191), channel_id=1, source_target_pairs={{0,16},{4,20},{8,24},{12,28},{16,0},{20,4},{24,8},{28,12},{1,17},{... | collective-permute-start | bytes 1179656 | tf_op jit(solution)/shard_map/ppermute | solution.py:34
  293.5 14.3 %collective-permute-start.36 = (bf16[128,1536]{1,0:T(8,128)(2,1)S(1)}, bf16[128,1536]{1,0:T(8,128)(2,1)S(1)}, u32[]{:S(2)}, u32[]{:S(2)}) collective-permute-start(bf16[128,1536]{1,0:T(8,128)(2,1)S(1)} %get-tuple-element.191), channel_id=1, source_target_pairs={{0,24},{4,28},{8,16},{12,20},{16,8},{20,12},{24,0},{28,4},{1,25},{... | collective-permute-start | bytes 1179656 | tf_op jit(solution)/shard_map/ppermute | solution.py:34
  309.1 260.1 %reduce-scatter.17.cloned.1.call-start = ((), (), s32[]{:S(2)}) async-start(), calls=%async_computation.23 | async-start | bytes 1966080 | tf_op jit(solution)/shard_map/reduce_scatter | solution.py:224
  367.0 19.3 %collective-permute-start.40 = (bf16[128,1536]{1,0:T(8,128)(2,1)S(1)}, bf16[128,1536]{1,0:T(8,128)(2,1)S(1)}, u32[]{:S(2)}, u32[]{:S(2)}) collective-permute-start(bf16[128,1536]{1,0:T(8,128)(2,1)S(1)} %get-tuple-element.198), channel_id=1, source_target_pairs={{0,16},{4,20},{8,24},{12,28},{16,0},{20,4},{24,8},{28,12},{1,17},{... | collective-permute-start | bytes 1179656 | tf_op jit(solution)/shard_map/ppermute | solution.py:34
  368.4 17.8 %collective-permute-start.41 = (bf16[128,1536]{1,0:T(8,128)(2,1)S(1)}, bf16[128,1536]{1,0:T(8,128)(2,1)S(1)}, u32[]{:S(2)}, u32[]{:S(2)}) collective-permute-start(bf16[128,1536]{1,0:T(8,128)(2,1)S(1)} %get-tuple-element.199), channel_id=1, source_target_pairs={{0,24},{4,28},{8,16},{12,20},{16,8},{20,12},{24,0},{28,4},{1,25},{... | collective-permute-start | bytes 1179656 | tf_op jit(solution)/shard_map/ppermute | solution.py:34
  390.0 18.5 %collective-permute-start.43 = (bf16[128,1536]{1,0:T(8,128)(2,1)S(1)}, bf16[128,1536]{1,0:T(8,128)(2,1)S(1)}, u32[]{:S(2)}, u32[]{:S(2)}) collective-permute-start(bf16[128,1536]{1,0:T(8,128)(2,1)S(1)} %get-tuple-element.202), channel_id=1, source_target_pairs={{0,16},{4,20},{8,24},{12,28},{16,0},{20,4},{24,8},{28,12},{1,17},{... | collective-permute-start | bytes 1179656 | tf_op jit(solution)/shard_map/ppermute | solution.py:34
  390.8 17.6 %collective-permute-start.44 = (bf16[128,1536]{1,0:T(8,128)(2,1)S(1)}, bf16[128,1536]{1,0:T(8,128)(2,1)S(1)}, u32[]{:S(2)}, u32[]{:S(2)}) collective-permute-start(bf16[128,1536]{1,0:T(8,128)(2,1)S(1)} %get-tuple-element.202), channel_id=1, source_target_pairs={{0,24},{4,28},{8,16},{12,20},{16,8},{20,12},{24,0},{28,4},{1,25},{... | collective-permute-start | bytes 1179656 | tf_op jit(solution)/shard_map/ppermute | solution.py:34
  425.2 183.3 %reduce-scatter.15.cloned.1.call-start = ((), (), s32[]{:S(2)}) async-start(), calls=%async_computation.22 | async-start | bytes 3932160 | tf_op jit(solution)/shard_map/reduce_scatter | solution.py:224
  430.7 19.6 %collective-permute-start.48 = (bf16[128,1536]{1,0:T(8,128)(2,1)}, bf16[128,1536]{1,0:T(8,128)(2,1)}, u32[]{:S(2)}, u32[]{:S(2)}) collective-permute-start(bf16[128,1536]{1,0:T(8,128)(2,1)} %get-tuple-element.206), channel_id=1, source_target_pairs={{0,16},{4,20},{8,24},{12,28},{16,0},{20,4},{24,8},{28,12},{1,17},{... | collective-permute-start | bytes 1179656 | tf_op jit(solution)/shard_map/ppermute | solution.py:34
  431.8 18.5 %collective-permute-start.49 = (bf16[128,1536]{1,0:T(8,128)(2,1)}, bf16[128,1536]{1,0:T(8,128)(2,1)}, u32[]{:S(2)}, u32[]{:S(2)}) collective-permute-start(bf16[128,1536]{1,0:T(8,128)(2,1)} %get-tuple-element.207), channel_id=1, source_target_pairs={{0,24},{4,28},{8,16},{12,20},{16,8},{20,12},{24,0},{28,4},{1,25},{... | collective-permute-start | bytes 1179656 | tf_op jit(solution)/shard_map/ppermute | solution.py:34
  440.4 186.7 %reduce-scatter.7.cloned.1.call-start = ((), (), s32[]{:S(2)}) async-start(), calls=%async_computation.18 | async-start | bytes 7077888 | tf_op jit(solution)/shard_map/reduce_scatter | solution.py:224
  500.5 25.5 %collective-permute-start.58 = (f32[19,1536]{1,0:T(8,128)S(1)}, f32[19,1536]{1,0:T(8,128)}, u32[]{:S(2)}, u32[]{:S(2)}) collective-permute-start(f32[19,1536]{1,0:T(8,128)S(1)} %add.654), channel_id=1, source_target_pairs={{0,8},{4,12},{8,0},{12,4},{16,24},{20,28},{24,16},{28,20},{1,9},{5... | collective-permute-start | bytes 350216 | tf_op jit(solution)/shard_map/ppermute | solution.py:34
  520.1 14.0 %collective-permute-start.57 = (bf16[160,768]{1,0:T(8,128)(2,1)}, bf16[160,768]{1,0:T(8,128)(2,1)S(1)}, u32[]{:S(2)}, u32[]{:S(2)}) collective-permute-start(bf16[160,768]{1,0:T(8,128)(2,1)} %get-tuple-element.227), channel_id=1, source_target_pairs={{0,24},{4,28},{8,16},{12,20},{16,8},{20,12},{24,0},{28,4},{1,25},{... | collective-permute-start | bytes 737288 | tf_op jit(solution)/shard_map/ppermute | solution.py:34
  545.5 12.6 %collective-permute-start.63 = (bf16[160,768]{1,0:T(8,128)(2,1)S(1)}, bf16[160,768]{1,0:T(8,128)(2,1)S(1)}, u32[]{:S(2)}, u32[]{:S(2)}) collective-permute-start(bf16[160,768]{1,0:T(8,128)(2,1)S(1)} %pad_maximum_fusion.22), channel_id=1, source_target_pairs={{0,8},{4,12},{8,0},{12,4},{16,24},{20,28},{24,16},{28,20},{1,9},{5... | collective-permute-start | bytes 737288 | tf_op jit(solution)/shard_map/ppermute | solution.py:34
  547.2 13.5 %collective-permute-start.64 = (bf16[160,768]{1,0:T(8,128)(2,1)S(1)}, bf16[160,768]{1,0:T(8,128)(2,1)S(1)}, u32[]{:S(2)}, u32[]{:S(2)}) collective-permute-start(bf16[160,768]{1,0:T(8,128)(2,1)S(1)} %pad_maximum_fusion.22), channel_id=1, source_target_pairs={{0,16},{4,20},{8,24},{12,28},{16,0},{20,4},{24,8},{28,12},{1,17},{... | collective-permute-start | bytes 737288 | tf_op jit(solution)/shard_map/ppermute | solution.py:34
  548.1 17.5 %collective-permute-start.65 = (bf16[160,768]{1,0:T(8,128)(2,1)S(1)}, bf16[160,768]{1,0:T(8,128)(2,1)S(1)}, u32[]{:S(2)}, u32[]{:S(2)}) collective-permute-start(bf16[160,768]{1,0:T(8,128)(2,1)S(1)} %pad_maximum_fusion.22), channel_id=1, source_target_pairs={{0,24},{4,28},{8,16},{12,20},{16,8},{20,12},{24,0},{28,4},{1,25},{... | collective-permute-start | bytes 737288 | tf_op jit(solution)/shard_map/ppermute | solution.py:34
  583.2 23.9 %all-to-all-start.5 = ((bf16[4,128,768]{2,1,0:T(8,128)(2,1)}), bf16[4,128,768]{2,1,0:T(8,128)(2,1)}, u32[]{:S(2)}, u32[]{:S(2)}) async-start(bf16[4,128,768]{2,1,0:T(8,128)(2,1)} %bitcast.320), calls=%async_computation.9 | async-start | bytes 1572864 | tf_op jit(solution)/shard_map/all_to_all | solution.py:212
  608.5 17.3 %all-to-all-start.6 = ((bf16[8,48,1024]{2,1,0:T(8,128)(2,1)}), bf16[8,48,1024]{2,1,0:T(8,128)(2,1)S(1)}, u32[]{:S(2)}, u32[]{:S(2)}) async-start(bf16[8,48,1024]{2,1,0:T(8,128)(2,1)} %bitcast.327), calls=%async_computation.11 | async-start | bytes 1572864 | tf_op jit(solution)/shard_map/all_to_all | solution.py:212
  613.2 131.8 %reduce-scatter.11.cloned.1.call-start = ((), (), s32[]{:S(2)}) async-start(), calls=%async_computation.20 | async-start | bytes 5308416 | tf_op jit(solution)/shard_map/reduce_scatter | solution.py:224
  660.1 14.3 %collective-permute-start.75 = (bf16[768,1152]{1,0:T(8,128)(2,1)}, bf16[768,1152]{1,0:T(8,128)(2,1)}, u32[]{:S(2)}, u32[]{:S(2)}) collective-permute-start(bf16[768,1152]{1,0:T(8,128)(2,1)} %pad_maximum_fusion.1), channel_id=1, source_target_pairs={{0,4},{4,0},{8,12},{12,8},{16,20},{20,16},{24,28},{28,24},{1,5},{5... | collective-permute-start | bytes 5308424 | tf_op jit(solution)/shard_map/ppermute | solution.py:34
  666.5 35.1 %all-to-all-start.3 = ((bf16[4,320,512]{2,1,0:T(8,128)(2,1)}), bf16[4,320,512]{2,1,0:T(8,128)(2,1)}, u32[]{:S(2)}, u32[]{:S(2)}) async-start(bf16[4,320,512]{2,1,0:T(8,128)(2,1)} %bitcast.325), calls=%async_computation.5 | async-start | bytes 2621440 | tf_op jit(solution)/shard_map/all_to_all | solution.py:212
  670.8 79.7 %reduce-scatter.9.cloned.1.call-start = ((), (), s32[]{:S(2)}) async-start(), calls=%async_computation.19 | async-start | bytes 1966080 | tf_op jit(solution)/shard_map/reduce_scatter | solution.py:224
  677.5 25.7 %collective-permute-start.77 = (bf16[192,1152]{1,0:T(8,128)(2,1)}, bf16[192,1152]{1,0:T(8,128)(2,1)S(1)}, u32[]{:S(2)}, u32[]{:S(2)}) collective-permute-start(bf16[192,1152]{1,0:T(8,128)(2,1)} %get-tuple-element.249), channel_id=1, source_target_pairs={{0,8},{4,12},{8,0},{12,4},{16,24},{20,28},{24,16},{28,20},{1,9},{5... | collective-permute-start | bytes 1327112 | tf_op jit(solution)/shard_map/ppermute | solution.py:34
  677.6 25.6 %collective-permute-start.78 = (bf16[192,1152]{1,0:T(8,128)(2,1)}, bf16[192,1152]{1,0:T(8,128)(2,1)S(1)}, u32[]{:S(2)}, u32[]{:S(2)}) collective-permute-start(bf16[192,1152]{1,0:T(8,128)(2,1)} %get-tuple-element.250), channel_id=1, source_target_pairs={{0,16},{4,20},{8,24},{12,28},{16,0},{20,4},{24,8},{28,12},{1,17},{... | collective-permute-start | bytes 1327112 | tf_op jit(solution)/shard_map/ppermute | solution.py:34
  679.5 26.0 %collective-permute-start.79 = (bf16[192,1152]{1,0:T(8,128)(2,1)}, bf16[192,1152]{1,0:T(8,128)(2,1)}, u32[]{:S(2)}, u32[]{:S(2)}) collective-permute-start(bf16[192,1152]{1,0:T(8,128)(2,1)} %get-tuple-element.251), channel_id=1, source_target_pairs={{0,24},{4,28},{8,16},{12,20},{16,8},{20,12},{24,0},{28,4},{1,25},{... | collective-permute-start | bytes 1327112 | tf_op jit(solution)/shard_map/ppermute | solution.py:34
  715.2 27.4 %all-to-all-start.4 = ((bf16[4,48,1152]{2,1,0:T(8,128)(2,1)}), bf16[4,48,1152]{2,1,0:T(8,128)(2,1)S(1)}, u32[]{:S(2)}, u32[]{:S(2)}) async-start(bf16[4,48,1152]{2,1,0:T(8,128)(2,1)} %bitcast.103), calls=%async_computation.6 | async-start | bytes 884736 | tf_op jit(solution)/shard_map/all_to_all | solution.py:212
  718.7 56.3 %reduce-scatter.13.cloned.1.call-start = ((), (), s32[]{:S(2)}) async-start(), calls=%async_computation.21 | async-start | bytes 737280 | tf_op jit(solution)/shard_map/reduce_scatter | solution.py:224
  720.1 13.7 %collective-permute-start.84 = (bf16[320,512]{1,0:T(8,128)(2,1)S(1)}, bf16[320,512]{1,0:T(8,128)(2,1)S(1)}, u32[]{:S(2)}, u32[]{:S(2)}) collective-permute-start(bf16[320,512]{1,0:T(8,128)(2,1)S(1)} %reduce_sum.276), channel_id=1, source_target_pairs={{0,16},{4,20},{8,24},{12,28},{16,0},{20,4},{24,8},{28,12},{1,17},{... | collective-permute-start | bytes 983048 | tf_op jit(solution)/shard_map/ppermute | solution.py:34
  720.7 13.7 %collective-permute-start.85 = (bf16[320,512]{1,0:T(8,128)(2,1)S(1)}, bf16[320,512]{1,0:T(8,128)(2,1)S(1)}, u32[]{:S(2)}, u32[]{:S(2)}) collective-permute-start(bf16[320,512]{1,0:T(8,128)(2,1)S(1)} %reduce_sum.276), channel_id=1, source_target_pairs={{0,24},{4,28},{8,16},{12,20},{16,8},{20,12},{24,0},{28,4},{1,25},{... | collective-permute-start | bytes 983048 | tf_op jit(solution)/shard_map/ppermute | solution.py:34
  739.3 12.9 %collective-permute-start.86 = (bf16[1280,512]{1,0:T(8,128)(2,1)S(1)}, bf16[1280,512]{1,0:T(8,128)(2,1)}, u32[]{:S(2)}, u32[]{:S(2)}) collective-permute-start(bf16[1280,512]{1,0:T(8,128)(2,1)S(1)} %pad_maximum_fusion.8.even_ref), channel_id=1, source_target_pairs={{0,4},{4,0},{8,12},{12,8},{16,20},{20,16},{24,28},{28,24},{1,5},{5... | collective-permute-start | bytes 3932168 | tf_op jit(solution)/shard_map/ppermute | solution.py:34
  (244 other events, 2209.0 us)
Sparse Core Ops, SparseCore 0:
  38.3 39.2 all-gather.5
  105.8 45.6 all-gather.7
  154.3 69.3 all-gather.9
  235.9 77.5 all-gather.11
  314.9 43.0 all-gather.13
  425.3 32.9 reduce-scatter.16
  460.6 59.8 reduce-scatter.14
  523.9 67.7 reduce-scatter.6
  639.5 64.5 reduce-scatter.10
  706.2 44.2 reduce-scatter.8
  752.8 22.1 reduce-scatter.12

commit v4 on v3

--- a/solution.py
+++ b/solution.py
@@ -981,7 +981,8 @@
     )
     dkv = scatter_rows(dkv, "seq")
     out_weight_term = lax.optimization_barrier((out_weight_term, dkv))[0]
-    out_weight_grad = scatter_rows(scatter_rows(out_weight_term, "seq"), "sub").astype(F32)
+    out_weight_term = scatter_rows(out_weight_term, "seq").reshape(num_sub, w_rows, width)
+    out_weight_grad = jnp.sum(swap_blocks(out_weight_term, "sub").astype(F32), 0)
     while not (text_flow.done and late_flow.done):
         order.step(text_flow, late_flow)
     text_key_gain_part = text_parts["gain"]

time: 780 us -> 784 us (level)
  waiting for transfers between devices: 313 us -> 323 us
    ppermute x94, waiting for transfers between devices: 186 us -> 212 us  [send(): return lax.ppermute(values, axis, [(i, i ^ mask) for i in range(count)])]
    reduce_scatter x6 -> x5, waiting for transfers between devices: 14 us -> 0.04 us  [scatter_rows(): return lax.psum_scatter(values, axis, scatter_dimension=0, tiled=True)]
    all_to_all x7 -> x8, starting transfers between devices: 29.4 us -> 42.4 us  [swap_blocks(): return lax.all_to_all(values, axis, split_axis=0, concat_axis=0, tiled=True)]
    ppermute x94, starting transfers between devices: 146 us -> 138 us  [send(): return lax.ppermute(values, axis, [(i, i ^ mask) for i in range(count)])]
    unnamed x377 -> x401, local copies, waits for them, and re-layouts: 25.4 us -> 29.3 us
    all_to_all x7 -> x8, waiting for transfers between devices: 79.5 us -> 80 us  [swap_blocks(): return lax.all_to_all(values, axis, split_axis=0, concat_axis=0, tiled=True)]
  transfers between devices with their start and end apart: 112 -> 112, of which waited for: 60 -> 58; matrix products, arithmetic and copies ran while one was open for 19% -> 20% of each run, Pallas kernels for 8% -> 7%
where the time goes in v4:
time: 784 us; the launch traced here: 792 us
  waiting for transfers between devices  323 us (41%)
  starting transfers between devices  181 us (23%)
  other arithmetic  79.2 us (10%)
  local copies, waits for them, and re-layouts  73.1 us (9%)
  matrix products  59 us (8%)
  Pallas kernels  55.2 us (7%)
  between operations  21.6 us (3%)
    ppermute x94, waiting for transfers between devices, send(): return lax.ppermute(values, axis, [(i, i ^ mask) for i in range(count)])  212 us
    ppermute x94, starting transfers between devices, send(): return lax.ppermute(values, axis, [(i, i ^ mask) for i in range(count)])  138 us
    all_to_all x8, waiting for transfers between devices, swap_blocks(): return lax.all_to_all(values, axis, split_axis=0, concat_axis=0, tiled=True)  80 us
    all_to_all x8, starting transfers between devices, swap_blocks(): return lax.all_to_all(values, axis, split_axis=0, concat_axis=0, tiled=True)  42.4 us
    pallas_call x4, Pallas kernels, kernel_call(): pl.pallas_call(kernel, out_shape=tuple((jax.ShapeDtypeStruct(shape, dtype...  40.7 us
    all_gather x5, waiting for transfers between devices, gather_rows(): return lax.all_gather(values, axis, axis=0, tiled=True)  29.7 us
    unnamed x401, local copies, waits for them, and re-layouts  29.3 us
    dot_general x10, matrix products, dot_tn(): lax.dot_general(left, right, (((0,), (0,)), ((), ())), preferred_element_...  24.9 us
  transfers between devices with their start and end apart: 112, of which 58 were waited for; matrix products, arithmetic and copies ran while one was open for 20% of the time, Pallas kernels for 7%

profile of v4, /device:TPU:0, one launch (start us, length us, event | category | flops | bytes accessed | tf_op | source)
XLA Modules:
  0.0 792.3 jit_solution(5603895455676622953)
XLA Ops:
  22.8 7.9 collective-permute-done.1
  39.8 8.1 %collective-permute-done.4 = f32[8,1536]{1,0:T(8,128)} collective-permute-done((f32[8,1536]{1,0:T(8,128)S(1)}, f32[8,1536]{1,0:T(8,128)}, u32[]{:S(2)}, u32[]{:S(2)}) %collective-permute-start.4) | collective-permute-done | bytes 49184 | tf_op jit(solution)/shard_map/ppermute | solution.py:34
  50.5 4.2 collective-permute-done.6
  67.2 5.8 collective-permute-done.10
  74.3 4.0 shard_map.443
  107.9 3.8 all-to-all-start
  114.4 27.0 %all-to-all-done = bf16[4,320,512]{2,1,0:T(8,128)(2,1)S(1)} async-done(((bf16[4,320,512]{2,1,0:T(8,128)(2,1)}), bf16[4,320,512]{2,1,0:T(8,128)(2,1)S(1)}, u32[]{:S(2)}, u32[]{:S(2)}) %all-to-all-start) | async-done | bytes 1310752 | tf_op jit(solution)/shard_map/all_to_all | solution.py:212
  141.4 14.2 %all-to-all-start.1 = ((bf16[4,128,768]{2,1,0:T(8,128)(2,1)}), bf16[4,128,768]{2,1,0:T(8,128)(2,1)}, u32[]{:S(2)}, u32[]{:S(2)}) async-start(bf16[4,128,768]{2,1,0:T(8,128)(2,1)} %pad_maximum_fusion.14), calls=%async_computation.1 | async-start | bytes 1572864 | tf_op jit(solution)/shard_map/all_to_all | solution.py:212
  164.1 13.9 %all-to-all-done.1 = bf16[4,128,768]{2,1,0:T(8,128)(2,1)} async-done(((bf16[4,128,768]{2,1,0:T(8,128)(2,1)}), bf16[4,128,768]{2,1,0:T(8,128)(2,1)}, u32[]{:S(2)}, u32[]{:S(2)}) %all-to-all-start.1) | async-done | bytes 786464 | tf_op jit(solution)/shard_map/all_to_all | solution.py:212
  202.1 4.4 all-to-all-start.2
  206.6 6.0 collective-permute-done.19
  225.5 9.4 %collective-permute-done.23 = f32[19,1536]{1,0:T(8,128)S(1)} collective-permute-done((f32[19,1536]{1,0:T(8,128)S(1)}, f32[19,1536]{1,0:T(8,128)S(1)}, u32[]{:S(2)}, u32[]{:S(2)}) %collective-permute-start.23) | collective-permute-done | bytes 116768 | tf_op jit(solution)/shard_map/ppermute | solution.py:34
  239.9 11.3 %shard_map.444 = (f32[512,384]{1,0:T(8,128)}, f32[8,512]{1,0:T(8,128)}) custom-call(s32[11]{0:T(128)} %concatenate.231.ranges, bf16[512,384]{1,0:T(8,128)(2,1)} %fusion.27.q_ref, bf16[4096,768]{1,0:T(8,128)(2,1)} %all-gather.8.cloned.1.call-done.kv_ref, s32[8,512]{1,0:T(8,128)} %add_add_fusion.5.meta_ref), custom_call_target="tpu_custom_call" | custom-call | flops 12884901888 | bytes 6692864 | tf_op jit(solution)/shard_map/pallas_call | solution.py:556
  251.4 9.7 %collective-permute-start.30 = (bf16[640,768]{1,0:T(8,128)(2,1)S(1)}, bf16[640,768]{1,0:T(8,128)(2,1)S(1)}, u32[]{:S(2)}, u32[]{:S(2)}) collective-permute-start(bf16[640,768]{1,0:T(8,128)(2,1)S(1)} %pad_maximum_fusion.11.even_ref), channel_id=1, source_target_pairs={{0,4},{4,0},{8,12},{12,8},{16,20},{20,16},{24,28},{28,24},{1,5},{5... | collective-permute-start | bytes 2949128 | tf_op jit(solution)/shard_map/ppermute | solution.py:34
  267.2 5.8 shard_map.446
  274.2 4.3 collective-permute-start.33
  283.1 7.5 collective-permute-done.32
  297.0 7.1 collective-permute-start.34
  305.5 8.6 %collective-permute-done.34 = bf16[128,1536]{1,0:T(8,128)(2,1)S(1)} collective-permute-done((bf16[128,1536]{1,0:T(8,128)(2,1)S(1)}, bf16[128,1536]{1,0:T(8,128)(2,1)S(1)}, u32[]{:S(2)}, u32[]{:S(2)}) %collective-permute-start.34) | collective-permute-done | bytes 393248 | tf_op jit(solution)/shard_map/ppermute | solution.py:34
  314.1 7.5 collective-permute-done.35
  341.3 28.6 %all-gather.14.cloned.1.call-done = bf16[512,1536]{1,0:T(8,128)(2,1)} async-done(((bf16[128,1536]{1,0:T(8,128)(2,1)}), bf16[512,1536]{1,0:T(8,128)(2,1)}) %all-gather.14.cloned.1.call-update) | async-done | bytes 1572880 | tf_op jit(solution)/shard_map/all_gather | solution.py:220
  381.0 8.5 %collective-permute-done.39 = bf16[128,1536]{1,0:T(8,128)(2,1)S(1)} collective-permute-done((bf16[128,1536]{1,0:T(8,128)(2,1)S(1)}, bf16[128,1536]{1,0:T(8,128)(2,1)S(1)}, u32[]{:S(2)}, u32[]{:S(2)}) %collective-permute-start.39) | collective-permute-done | bytes 393248 | tf_op jit(solution)/shard_map/ppermute | solution.py:34
  389.5 8.8 %collective-permute-done.40 = bf16[128,1536]{1,0:T(8,128)(2,1)S(1)} collective-permute-done((bf16[128,1536]{1,0:T(8,128)(2,1)S(1)}, bf16[128,1536]{1,0:T(8,128)(2,1)S(1)}, u32[]{:S(2)}, u32[]{:S(2)}) %collective-permute-start.40) | collective-permute-done | bytes 393248 | tf_op jit(solution)/shard_map/ppermute | solution.py:34
  404.4 8.6 %collective-permute-done.42 = bf16[128,1536]{1,0:T(8,128)(2,1)S(1)} collective-permute-done((bf16[128,1536]{1,0:T(8,128)(2,1)S(1)}, bf16[128,1536]{1,0:T(8,128)(2,1)S(1)}, u32[]{:S(2)}, u32[]{:S(2)}) %collective-permute-start.42) | collective-permute-done | bytes 393248 | tf_op jit(solution)/shard_map/ppermute | solution.py:34
  412.9 7.6 collective-permute-done.43
  426.7 3.9 convolution_convert_fusion.4
  445.4 4.7 convolution_convert_fusion.3
  454.2 8.0 %collective-permute-done.48 = bf16[128,1536]{1,0:T(8,128)(2,1)} collective-permute-done((bf16[128,1536]{1,0:T(8,128)(2,1)}, bf16[128,1536]{1,0:T(8,128)(2,1)}, u32[]{:S(2)}, u32[]{:S(2)}) %collective-permute-start.48) | collective-permute-done | bytes 393248 | tf_op jit(solution)/shard_map/ppermute | solution.py:34
  472.5 4.9 collective-permute-done.51
  478.9 6.8 shard_map.447
  487.5 16.8 %shard_map.448 = (f32[512,384]{1,0:T(8,128)}, bf16[4096,768]{1,0:T(8,128)(2,1)}) custom-call(s32[11]{0:T(128)} %concatenate.231.ranges, bf16[512,384]{1,0:T(8,128)(2,1)} %fusion.27.q_ref, bf16[4096,768]{1,0:T(8,128)(2,1)} %all-gather.8.cloned.1.call-done.kv_ref, s32[8,512]{1,0:T(8,128)} %add_add_fusion.5.meta_ref, ...), custom_call_target="tpu_custom_call" | custom-call | flops 25769803776 | bytes 7880704 | tf_op jit(solution)/shard_map/pallas_call | solution.py:556
  504.3 18.8 %collective-permute-start.53 = (bf16[640,768]{1,0:T(8,128)(2,1)S(1)}, bf16[640,768]{1,0:T(8,128)(2,1)S(1)}, u32[]{:S(2)}, u32[]{:S(2)}) collective-permute-start(bf16[640,768]{1,0:T(8,128)(2,1)S(1)} %pad_maximum_fusion.12), channel_id=1, source_target_pairs={{0,4},{4,0},{8,12},{12,8},{16,20},{20,16},{24,28},{28,24},{1,5},{5... | collective-permute-start | bytes 2949128 | tf_op jit(solution)/shard_map/ppermute | solution.py:34
  534.2 4.6 collective-permute-done.55
  539.5 5.2 collective-permute-done.57
  563.3 8.2 %collective-permute-done.63 = bf16[160,768]{1,0:T(8,128)(2,1)S(1)} collective-permute-done((bf16[160,768]{1,0:T(8,128)(2,1)S(1)}, bf16[160,768]{1,0:T(8,128)(2,1)S(1)}, u32[]{:S(2)}, u32[]{:S(2)}) %collective-permute-start.63) | collective-permute-done | bytes 245792 | tf_op jit(solution)/shard_map/ppermute | solution.py:34
  572.6 6.2 collective-permute-done.65
  603.6 14.3 %all-to-all-done.6 = bf16[4,128,768]{2,1,0:T(8,128)(2,1)S(1)} async-done(((bf16[4,128,768]{2,1,0:T(8,128)(2,1)}), bf16[4,128,768]{2,1,0:T(8,128)(2,1)S(1)}, u32[]{:S(2)}, u32[]{:S(2)}) %all-to-all-start.6) | async-done | bytes 786464 | tf_op jit(solution)/shard_map/all_to_all | solution.py:212
  620.0 4.1 all-to-all-start.7
  639.1 5.5 multiply_reduce_fusion
  646.7 6.5 convolution_convert_fusion.1
  666.2 4.3 all-to-all-start.3
  684.2 24.8 %all-to-all-done.3 = bf16[4,320,512]{2,1,0:T(8,128)(2,1)} async-done(((bf16[4,320,512]{2,1,0:T(8,128)(2,1)}), bf16[4,320,512]{2,1,0:T(8,128)(2,1)}, u32[]{:S(2)}, u32[]{:S(2)}) %all-to-all-start.3) | async-done | bytes 1310752 | tf_op jit(solution)/shard_map/all_to_all | solution.py:212
  717.4 4.2 collective-permute-done.81
  730.9 8.5 %collective-permute-done.83 = bf16[320,512]{1,0:T(8,128)(2,1)S(1)} collective-permute-done((bf16[320,512]{1,0:T(8,128)(2,1)S(1)}, bf16[320,512]{1,0:T(8,128)(2,1)S(1)}, u32[]{:S(2)}, u32[]{:S(2)}) %collective-permute-start.83) | collective-permute-done | bytes 327712 | tf_op jit(solution)/shard_map/ppermute | solution.py:34
  739.4 8.3 %collective-permute-done.85 = bf16[320,512]{1,0:T(8,128)(2,1)} collective-permute-done((bf16[320,512]{1,0:T(8,128)(2,1)S(1)}, bf16[320,512]{1,0:T(8,128)(2,1)}, u32[]{:S(2)}, u32[]{:S(2)}) %collective-permute-start.85) | collective-permute-done | bytes 327712 | tf_op jit(solution)/shard_map/ppermute | solution.py:34
  760.1 4.7 all-to-all-start.5
  771.9 4.6 shard_map.450
  776.4 7.4 collective-permute-done.92
  (870 shorter events, 352.8 us)
Async XLA Ops:
  7.2 72.7 %all-gather.6.cloned.1.call-start = ((), (), s32[]{:S(2)}) async-start(), calls=%async_computation.13 | async-start | bytes 2129920 | tf_op jit(solution)/shard_map/all_gather | solution.py:220
  33.6 15.1 %collective-permute-start.5 = (bf16[192,1152]{1,0:T(8,128)(2,1)S(1)}, bf16[192,1152]{1,0:T(8,128)(2,1)}, u32[]{:S(2)}, u32[]{:S(2)}) collective-permute-start(bf16[192,1152]{1,0:T(8,128)(2,1)S(1)} %pad_maximum_fusion.18), channel_id=1, source_target_pairs={{0,8},{4,12},{8,0},{12,4},{16,24},{20,28},{24,16},{28,20},{1,9},{5... | collective-permute-start | bytes 1327112 | tf_op jit(solution)/shard_map/ppermute | solution.py:34
  35.9 18.8 %collective-permute-start.6 = (bf16[192,1152]{1,0:T(8,128)(2,1)S(1)}, bf16[192,1152]{1,0:T(8,128)(2,1)}, u32[]{:S(2)}, u32[]{:S(2)}) collective-permute-start(bf16[192,1152]{1,0:T(8,128)(2,1)S(1)} %pad_maximum_fusion.18), channel_id=1, source_target_pairs={{0,16},{4,20},{8,24},{12,28},{16,0},{20,4},{24,8},{28,12},{1,17},{... | collective-permute-start | bytes 1327112 | tf_op jit(solution)/shard_map/ppermute | solution.py:34
  38.2 197.7 %all-gather.8.cloned.1.call-start = ((), (), s32[]{:S(2)}) async-start(), calls=%async_computation.14 | async-start | bytes 7077888 | tf_op jit(solution)/shard_map/all_gather | solution.py:220
  38.3 18.2 %collective-permute-start.7 = (bf16[192,1152]{1,0:T(8,128)(2,1)S(1)}, bf16[192,1152]{1,0:T(8,128)(2,1)S(1)}, u32[]{:S(2)}, u32[]{:S(2)}) collective-permute-start(bf16[192,1152]{1,0:T(8,128)(2,1)S(1)} %pad_maximum_fusion.18), channel_id=1, source_target_pairs={{0,24},{4,28},{8,16},{12,20},{16,8},{20,12},{24,0},{28,4},{1,25},{... | collective-permute-start | bytes 1327112 | tf_op jit(solution)/shard_map/ppermute | solution.py:34
  105.7 185.9 %all-gather.10.cloned.1.call-start = ((), (), s32[]{:S(2)}) async-start(), calls=%async_computation.15 | async-start | bytes 4866048 | tf_op jit(solution)/shard_map/all_gather | solution.py:220
  107.9 33.5 %all-to-all-start = ((bf16[4,320,512]{2,1,0:T(8,128)(2,1)}), bf16[4,320,512]{2,1,0:T(8,128)(2,1)S(1)}, u32[]{:S(2)}, u32[]{:S(2)}) async-start(bf16[4,320,512]{2,1,0:T(8,128)(2,1)} %broadcast_in_dim.80), calls=%async_computation | async-start | bytes 2621440 | tf_op jit(solution)/shard_map/all_to_all | solution.py:212
  141.4 36.6 %all-to-all-start.1 = ((bf16[4,128,768]{2,1,0:T(8,128)(2,1)}), bf16[4,128,768]{2,1,0:T(8,128)(2,1)}, u32[]{:S(2)}, u32[]{:S(2)}) async-start(bf16[4,128,768]{2,1,0:T(8,128)(2,1)} %pad_maximum_fusion.14), calls=%async_computation.1 | async-start | bytes 1572864 | tf_op jit(solution)/shard_map/all_to_all | solution.py:212
  197.0 16.5 %collective-permute-start.20 = (bf16[160,768]{1,0:T(8,128)(2,1)}, bf16[160,768]{1,0:T(8,128)(2,1)}, u32[]{:S(2)}, u32[]{:S(2)}) collective-permute-start(bf16[160,768]{1,0:T(8,128)(2,1)} %get-tuple-element.169), channel_id=1, source_target_pairs={{0,8},{4,12},{8,0},{12,4},{16,24},{20,28},{24,16},{28,20},{1,9},{5... | collective-permute-start | bytes 737288 | tf_op jit(solution)/shard_map/ppermute | solution.py:34
  198.5 16.8 %collective-permute-start.21 = (bf16[160,768]{1,0:T(8,128)(2,1)}, bf16[160,768]{1,0:T(8,128)(2,1)}, u32[]{:S(2)}, u32[]{:S(2)}) collective-permute-start(bf16[160,768]{1,0:T(8,128)(2,1)} %get-tuple-element.170), channel_id=1, source_target_pairs={{0,16},{4,20},{8,24},{12,28},{16,0},{20,4},{24,8},{28,12},{1,17},{... | collective-permute-start | bytes 737288 | tf_op jit(solution)/shard_map/ppermute | solution.py:34
  199.1 17.9 %collective-permute-start.22 = (bf16[160,768]{1,0:T(8,128)(2,1)}, bf16[160,768]{1,0:T(8,128)(2,1)}, u32[]{:S(2)}, u32[]{:S(2)}) collective-permute-start(bf16[160,768]{1,0:T(8,128)(2,1)} %get-tuple-element.171), channel_id=1, source_target_pairs={{0,24},{4,28},{8,16},{12,20},{16,8},{20,12},{24,0},{28,4},{1,25},{... | collective-permute-start | bytes 737288 | tf_op jit(solution)/shard_map/ppermute | solution.py:34
  202.1 58.9 %all-to-all-start.2 = ((bf16[8,48,1024]{2,1,0:T(8,128)(2,1)}), bf16[8,48,1024]{2,1,0:T(8,128)(2,1)}, u32[]{:S(2)}, u32[]{:S(2)}) async-start(bf16[8,48,1024]{2,1,0:T(8,128)(2,1)} %copy-done.49), calls=%async_computation.2 | async-start | bytes 1572864 | tf_op jit(solution)/shard_map/all_to_all | solution.py:212
  206.5 125.8 %all-gather.12.cloned.1.call-start = ((), (), s32[]{:S(2)}) async-start(), calls=%async_computation.16 | async-start | bytes 3932160 | tf_op jit(solution)/shard_map/all_gather | solution.py:220
  235.9 15.3 %collective-permute-start.27 = (bf16[160,768]{1,0:T(8,128)(2,1)S(1)}, bf16[160,768]{1,0:T(8,128)(2,1)S(1)}, u32[]{:S(2)}, u32[]{:S(2)}) collective-permute-start(bf16[160,768]{1,0:T(8,128)(2,1)S(1)} %pad_maximum_fusion.21), channel_id=1, source_target_pairs={{0,8},{4,12},{8,0},{12,4},{16,24},{20,28},{24,16},{28,20},{1,9},{5... | collective-permute-start | bytes 737288 | tf_op jit(solution)/shard_map/ppermute | solution.py:34
  261.1 108.9 %all-gather.14.cloned.1.call-start = ((), (), s32[]{:S(2)}) async-start(), calls=%async_computation.17 | async-start | bytes 1966080 | tf_op jit(solution)/shard_map/all_gather | solution.py:220
  274.1 16.5 %collective-permute-start.32 = (bf16[128,384]{1,0:T(8,128)(2,1)S(1)}, bf16[128,384]{1,0:T(8,128)(2,1)S(1)}, u32[]{:S(2)}, u32[]{:S(2)}) collective-permute-start(bf16[128,384]{1,0:T(8,128)(2,1)S(1)} %get-tuple-element.187), channel_id=1, source_target_pairs={{0,2},{1,3},{2,0},{3,1},{4,6},{5,7},{6,4},{7,5},{8,10},{9,11},{10,... | collective-permute-start | bytes 294920 | tf_op jit(solution)/shard_map/ppermute | solution.py:34
  274.2 16.4 %collective-permute-start.33 = (bf16[128,384]{1,0:T(8,128)(2,1)S(1)}, bf16[128,384]{1,0:T(8,128)(2,1)S(1)}, u32[]{:S(2)}, u32[]{:S(2)}) collective-permute-start(bf16[128,384]{1,0:T(8,128)(2,1)S(1)} %get-tuple-element.188), channel_id=1, source_target_pairs={{0,1},{1,0},{2,3},{3,2},{4,5},{5,4},{6,7},{7,6},{8,9},{9,8},{10,11... | collective-permute-start | bytes 294920 | tf_op jit(solution)/shard_map/ppermute | solution.py:34
  297.0 17.1 %collective-permute-start.34 = (bf16[128,1536]{1,0:T(8,128)(2,1)S(1)}, bf16[128,1536]{1,0:T(8,128)(2,1)S(1)}, u32[]{:S(2)}, u32[]{:S(2)}) collective-permute-start(bf16[128,1536]{1,0:T(8,128)(2,1)S(1)} %get-tuple-element.191), channel_id=1, source_target_pairs={{0,8},{4,12},{8,0},{12,4},{16,24},{20,28},{24,16},{28,20},{1,9},{5... | collective-permute-start | bytes 1179656 | tf_op jit(solution)/shard_map/ppermute | solution.py:34
  304.1 17.5 %collective-permute-start.35 = (bf16[128,1536]{1,0:T(8,128)(2,1)S(1)}, bf16[128,1536]{1,0:T(8,128)(2,1)S(1)}, u32[]{:S(2)}, u32[]{:S(2)}) collective-permute-start(bf16[128,1536]{1,0:T(8,128)(2,1)S(1)} %get-tuple-element.191), channel_id=1, source_target_pairs={{0,16},{4,20},{8,24},{12,28},{16,0},{20,4},{24,8},{28,12},{1,17},{... | collective-permute-start | bytes 1179656 | tf_op jit(solution)/shard_map/ppermute | solution.py:34
  304.1 19.4 %collective-permute-start.36 = (bf16[128,1536]{1,0:T(8,128)(2,1)S(1)}, bf16[128,1536]{1,0:T(8,128)(2,1)S(1)}, u32[]{:S(2)}, u32[]{:S(2)}) collective-permute-start(bf16[128,1536]{1,0:T(8,128)(2,1)S(1)} %get-tuple-element.191), channel_id=1, source_target_pairs={{0,24},{4,28},{8,16},{12,20},{16,8},{20,12},{24,0},{28,4},{1,25},{... | collective-permute-start | bytes 1179656 | tf_op jit(solution)/shard_map/ppermute | solution.py:34
  324.8 256.6 %reduce-scatter.14.cloned.1.call-start = ((), (), s32[]{:S(2)}) async-start(), calls=%async_computation.22 | async-start | bytes 1966080 | tf_op jit(solution)/shard_map/reduce_scatter | solution.py:224
  379.0 19.3 %collective-permute-start.40 = (bf16[128,1536]{1,0:T(8,128)(2,1)S(1)}, bf16[128,1536]{1,0:T(8,128)(2,1)S(1)}, u32[]{:S(2)}, u32[]{:S(2)}) collective-permute-start(bf16[128,1536]{1,0:T(8,128)(2,1)S(1)} %get-tuple-element.198), channel_id=1, source_target_pairs={{0,16},{4,20},{8,24},{12,28},{16,0},{20,4},{24,8},{28,12},{1,17},{... | collective-permute-start | bytes 1179656 | tf_op jit(solution)/shard_map/ppermute | solution.py:34
  380.5 17.8 %collective-permute-start.41 = (bf16[128,1536]{1,0:T(8,128)(2,1)S(1)}, bf16[128,1536]{1,0:T(8,128)(2,1)S(1)}, u32[]{:S(2)}, u32[]{:S(2)}) collective-permute-start(bf16[128,1536]{1,0:T(8,128)(2,1)S(1)} %get-tuple-element.199), channel_id=1, source_target_pairs={{0,24},{4,28},{8,16},{12,20},{16,8},{20,12},{24,0},{28,4},{1,25},{... | collective-permute-start | bytes 1179656 | tf_op jit(solution)/shard_map/ppermute | solution.py:34
  402.1 18.5 %collective-permute-start.43 = (bf16[128,1536]{1,0:T(8,128)(2,1)S(1)}, bf16[128,1536]{1,0:T(8,128)(2,1)S(1)}, u32[]{:S(2)}, u32[]{:S(2)}) collective-permute-start(bf16[128,1536]{1,0:T(8,128)(2,1)S(1)} %get-tuple-element.202), channel_id=1, source_target_pairs={{0,16},{4,20},{8,24},{12,28},{16,0},{20,4},{24,8},{28,12},{1,17},{... | collective-permute-start | bytes 1179656 | tf_op jit(solution)/shard_map/ppermute | solution.py:34
  402.9 17.6 %collective-permute-start.44 = (bf16[128,1536]{1,0:T(8,128)(2,1)S(1)}, bf16[128,1536]{1,0:T(8,128)(2,1)S(1)}, u32[]{:S(2)}, u32[]{:S(2)}) collective-permute-start(bf16[128,1536]{1,0:T(8,128)(2,1)S(1)} %get-tuple-element.202), channel_id=1, source_target_pairs={{0,24},{4,28},{8,16},{12,20},{16,8},{20,12},{24,0},{28,4},{1,25},{... | collective-permute-start | bytes 1179656 | tf_op jit(solution)/shard_map/ppermute | solution.py:34
  437.0 183.0 %reduce-scatter.12.cloned.1.call-start = ((), (), s32[]{:S(2)}) async-start(), calls=%async_computation.21 | async-start | bytes 3932160 | tf_op jit(solution)/shard_map/reduce_scatter | solution.py:224
  442.5 19.6 %collective-permute-start.48 = (bf16[128,1536]{1,0:T(8,128)(2,1)}, bf16[128,1536]{1,0:T(8,128)(2,1)}, u32[]{:S(2)}, u32[]{:S(2)}) collective-permute-start(bf16[128,1536]{1,0:T(8,128)(2,1)} %get-tuple-element.206), channel_id=1, source_target_pairs={{0,16},{4,20},{8,24},{12,28},{16,0},{20,4},{24,8},{28,12},{1,17},{... | collective-permute-start | bytes 1179656 | tf_op jit(solution)/shard_map/ppermute | solution.py:34
  443.7 18.5 %collective-permute-start.49 = (bf16[128,1536]{1,0:T(8,128)(2,1)}, bf16[128,1536]{1,0:T(8,128)(2,1)}, u32[]{:S(2)}, u32[]{:S(2)}) collective-permute-start(bf16[128,1536]{1,0:T(8,128)(2,1)} %get-tuple-element.207), channel_id=1, source_target_pairs={{0,24},{4,28},{8,16},{12,20},{16,8},{20,12},{24,0},{28,4},{1,25},{... | collective-permute-start | bytes 1179656 | tf_op jit(solution)/shard_map/ppermute | solution.py:34
  452.4 171.8 %reduce-scatter.6.cloned.1.call-start = ((), (), s32[]{:S(2)}) async-start(), calls=%async_computation.18 | async-start | bytes 7077888 | tf_op jit(solution)/shard_map/reduce_scatter | solution.py:224
  504.3 21.3 %collective-permute-start.53 = (bf16[640,768]{1,0:T(8,128)(2,1)S(1)}, bf16[640,768]{1,0:T(8,128)(2,1)S(1)}, u32[]{:S(2)}, u32[]{:S(2)}) collective-permute-start(bf16[640,768]{1,0:T(8,128)(2,1)S(1)} %pad_maximum_fusion.12), channel_id=1, source_target_pairs={{0,4},{4,0},{8,12},{12,8},{16,20},{20,16},{24,28},{28,24},{1,5},{5... | collective-permute-start | bytes 2949128 | tf_op jit(solution)/shard_map/ppermute | solution.py:34
  530.5 14.2 %collective-permute-start.57 = (bf16[160,768]{1,0:T(8,128)(2,1)}, bf16[160,768]{1,0:T(8,128)(2,1)}, u32[]{:S(2)}, u32[]{:S(2)}) collective-permute-start(bf16[160,768]{1,0:T(8,128)(2,1)} %get-tuple-element.227), channel_id=1, source_target_pairs={{0,24},{4,28},{8,16},{12,20},{16,8},{20,12},{24,0},{28,4},{1,25},{... | collective-permute-start | bytes 737288 | tf_op jit(solution)/shard_map/ppermute | solution.py:34
  558.7 14.0 %collective-permute-start.64 = (bf16[160,768]{1,0:T(8,128)(2,1)S(1)}, bf16[160,768]{1,0:T(8,128)(2,1)S(1)}, u32[]{:S(2)}, u32[]{:S(2)}) collective-permute-start(bf16[160,768]{1,0:T(8,128)(2,1)S(1)} %pad_maximum_fusion.22), channel_id=1, source_target_pairs={{0,16},{4,20},{8,24},{12,28},{16,0},{20,4},{24,8},{28,12},{1,17},{... | collective-permute-start | bytes 737288 | tf_op jit(solution)/shard_map/ppermute | solution.py:34
  559.3 19.5 %collective-permute-start.65 = (bf16[160,768]{1,0:T(8,128)(2,1)S(1)}, bf16[160,768]{1,0:T(8,128)(2,1)S(1)}, u32[]{:S(2)}, u32[]{:S(2)}) collective-permute-start(bf16[160,768]{1,0:T(8,128)(2,1)S(1)} %pad_maximum_fusion.22), channel_id=1, source_target_pairs={{0,24},{4,28},{8,16},{12,20},{16,8},{20,12},{24,0},{28,4},{1,25},{... | collective-permute-start | bytes 737288 | tf_op jit(solution)/shard_map/ppermute | solution.py:34
  594.4 23.6 %all-to-all-start.6 = ((bf16[4,128,768]{2,1,0:T(8,128)(2,1)}), bf16[4,128,768]{2,1,0:T(8,128)(2,1)S(1)}, u32[]{:S(2)}, u32[]{:S(2)}) async-start(bf16[4,128,768]{2,1,0:T(8,128)(2,1)} %bitcast.321), calls=%async_computation.9 | async-start | bytes 1572864 | tf_op jit(solution)/shard_map/all_to_all | solution.py:212
  620.0 38.6 %all-to-all-start.7 = ((bf16[8,48,1024]{2,1,0:T(8,128)(2,1)}), bf16[8,48,1024]{2,1,0:T(8,128)(2,1)S(1)}, u32[]{:S(2)}, u32[]{:S(2)}) async-start(bf16[8,48,1024]{2,1,0:T(8,128)(2,1)} %bitcast.328), calls=%async_computation.11 | async-start | bytes 1572864 | tf_op jit(solution)/shard_map/all_to_all | solution.py:212
  624.1 134.2 %reduce-scatter.8.cloned.1.call-start = ((), (), s32[]{:S(2)}) async-start(), calls=%async_computation.19 | async-start | bytes 1966080 | tf_op jit(solution)/shard_map/reduce_scatter | solution.py:224
  646.0 114.1 %reduce-scatter.10.cloned.1.call-start = ((), (), s32[]{:S(2)}) async-start(), calls=%async_computation.20 | async-start | bytes 5308416 | tf_op jit(solution)/shard_map/reduce_scatter | solution.py:224
  658.6 13.3 %collective-permute-start.75 = (bf16[768,1152]{1,0:T(8,128)(2,1)}, bf16[768,1152]{1,0:T(8,128)(2,1)S(1)}, u32[]{:S(2)}, u32[]{:S(2)}) collective-permute-start(bf16[768,1152]{1,0:T(8,128)(2,1)} %pad_maximum_fusion.1), channel_id=1, source_target_pairs={{0,4},{4,0},{8,12},{12,8},{16,20},{20,16},{24,28},{28,24},{1,5},{5... | collective-permute-start | bytes 5308424 | tf_op jit(solution)/shard_map/ppermute | solution.py:34
  666.2 42.8 %all-to-all-start.3 = ((bf16[4,320,512]{2,1,0:T(8,128)(2,1)}), bf16[4,320,512]{2,1,0:T(8,128)(2,1)}, u32[]{:S(2)}, u32[]{:S(2)}) async-start(bf16[4,320,512]{2,1,0:T(8,128)(2,1)} %bitcast.326), calls=%async_computation.5 | async-start | bytes 2621440 | tf_op jit(solution)/shard_map/all_to_all | solution.py:212
  676.5 34.1 %collective-permute-start.77 = (bf16[192,1152]{1,0:T(8,128)(2,1)}, bf16[192,1152]{1,0:T(8,128)(2,1)}, u32[]{:S(2)}, u32[]{:S(2)}) collective-permute-start(bf16[192,1152]{1,0:T(8,128)(2,1)} %get-tuple-element.249), channel_id=1, source_target_pairs={{0,8},{4,12},{8,0},{12,4},{16,24},{20,28},{24,16},{28,20},{1,9},{5... | collective-permute-start | bytes 1327112 | tf_op jit(solution)/shard_map/ppermute | solution.py:34
  677.9 32.8 %collective-permute-start.78 = (bf16[192,1152]{1,0:T(8,128)(2,1)}, bf16[192,1152]{1,0:T(8,128)(2,1)}, u32[]{:S(2)}, u32[]{:S(2)}) collective-permute-start(bf16[192,1152]{1,0:T(8,128)(2,1)} %get-tuple-element.250), channel_id=1, source_target_pairs={{0,16},{4,20},{8,24},{12,28},{16,0},{20,4},{24,8},{28,12},{1,17},{... | collective-permute-start | bytes 1327112 | tf_op jit(solution)/shard_map/ppermute | solution.py:34
  679.3 31.3 %collective-permute-start.79 = (bf16[192,1152]{1,0:T(8,128)(2,1)}, bf16[192,1152]{1,0:T(8,128)(2,1)}, u32[]{:S(2)}, u32[]{:S(2)}) collective-permute-start(bf16[192,1152]{1,0:T(8,128)(2,1)} %get-tuple-element.251), channel_id=1, source_target_pairs={{0,24},{4,28},{8,16},{12,20},{16,8},{20,12},{24,0},{28,4},{1,25},{... | collective-permute-start | bytes 1327112 | tf_op jit(solution)/shard_map/ppermute | solution.py:34
  721.6 34.3 %all-to-all-start.4 = ((bf16[4,48,1152]{2,1,0:T(8,128)(2,1)}), bf16[4,48,1152]{2,1,0:T(8,128)(2,1)S(1)}, u32[]{:S(2)}, u32[]{:S(2)}) async-start(bf16[4,48,1152]{2,1,0:T(8,128)(2,1)} %bitcast.103), calls=%async_computation.6 | async-start | bytes 884736 | tf_op jit(solution)/shard_map/all_to_all | solution.py:212
  725.1 14.3 %collective-permute-start.83 = (bf16[320,512]{1,0:T(8,128)(2,1)S(1)}, bf16[320,512]{1,0:T(8,128)(2,1)S(1)}, u32[]{:S(2)}, u32[]{:S(2)}) collective-permute-start(bf16[320,512]{1,0:T(8,128)(2,1)S(1)} %reduce_sum.285), channel_id=1, source_target_pairs={{0,8},{4,12},{8,0},{12,4},{16,24},{20,28},{24,16},{28,20},{1,9},{5... | collective-permute-start | bytes 983048 | tf_op jit(solution)/shard_map/ppermute | solution.py:34
  728.1 19.6 %collective-permute-start.85 = (bf16[320,512]{1,0:T(8,128)(2,1)S(1)}, bf16[320,512]{1,0:T(8,128)(2,1)}, u32[]{:S(2)}, u32[]{:S(2)}) collective-permute-start(bf16[320,512]{1,0:T(8,128)(2,1)S(1)} %reduce_sum.285), channel_id=1, source_target_pairs={{0,24},{4,28},{8,16},{12,20},{16,8},{20,12},{24,0},{28,4},{1,25},{... | collective-permute-start | bytes 983048 | tf_op jit(solution)/shard_map/ppermute | solution.py:34
  760.1 24.3 %all-to-all-start.5 = ((bf16[4,48,1536]{2,1,0:T(8,128)(2,1)}), bf16[4,48,1536]{2,1,0:T(8,128)(2,1)S(1)}, u32[]{:S(2)}, u32[]{:S(2)}) async-start(bf16[4,48,1536]{2,1,0:T(8,128)(2,1)} %bitcast.329), calls=%async_computation.8 | async-start | bytes 1179648 | tf_op jit(solution)/shard_map/all_to_all | solution.py:212
  766.9 16.9 %collective-permute-start.92 = (f32[5,1024]{1,0:T(8,128)S(1)}, f32[5,1024]{1,0:T(8,128)S(1)}, u32[]{:S(2)}, u32[]{:S(2)}) collective-permute-start(f32[5,1024]{1,0:T(8,128)S(1)} %add.678), channel_id=1, source_target_pairs={{0,2},{1,3},{2,0},{3,1},{4,6},{5,7},{6,4},{7,5},{8,10},{9,11},{10,... | collective-permute-start | bytes 61448 | tf_op jit(solution)/shard_map/ppermute | solution.py:34
  769.3 14.5 %collective-permute-start.93 = (f32[5,1024]{1,0:T(8,128)S(1)}, f32[5,1024]{1,0:T(8,128)S(1)}, u32[]{:S(2)}, u32[]{:S(2)}) collective-permute-start(f32[5,1024]{1,0:T(8,128)S(1)} %add.678), channel_id=1, source_target_pairs={{0,3},{1,2},{2,1},{3,0},{4,7},{5,6},{6,5},{7,4},{8,11},{9,10},{10,... | collective-permute-start | bytes 61448 | tf_op jit(solution)/shard_map/ppermute | solution.py:34
  (256 other events, 2900.4 us)
Sparse Core Ops, SparseCore 0:
  38.3 39.2 all-gather.5
  105.8 45.6 all-gather.7
  154.3 81.8 all-gather.9
  261.2 70.9 all-gather.11
  333.7 36.2 all-gather.13
  437.1 32.9 reduce-scatter.13
  472.4 59.8 reduce-scatter.11
  535.7 68.4 reduce-scatter.5
  646.1 44.2 reduce-scatter.7
  694.7 60.0 reduce-scatter.9
